TPU v7x, 256 devices: a whole 4x4x8 slice. The times are simulated.
256 devices in a mesh: dp: 32 (over z, y), head: 8 (over x, core).
Axes of the slice: x: 4, y: 4, z: 8, core: 2. Of those that a mesh axis runs over, the one named last changes fastest.
Arguments:
- teacher_feats: bfloat16 [8192, 384], P('dp'), as said below
- student_feats: bfloat16 [8192, 384], P('dp'), as said below
- prototypes: bfloat16 [65536, 384], P(('dp', 'head')), as said below
Outputs:
- proto_grad: float32 [65536, 384], P(('dp', 'head'))
Inputs may be any that keep to these rules, and one draw needn't show every extreme that they name: `teacher_feats`: finite values. `student_feats`: finite values. `prototypes`: finite values.
All inputs are finite; a program needn't handle non-finite values.
Results may differ from a plain program's by a relative error of at most 0.0034.
Values may be sent and summed in bfloat16 or wider, within the bound.
No kernel may reach another device: no remote copies, remote signals or barrier semaphores. Data moves between devices by JAX's collectives and lax.ppermute only.
A program may use at most 128 MiB of HBM per device.

v0:
```python
import math

import jax
import jax.numpy as jnp
from jax import lax
from jax.sharding import PartitionSpec as P

PROTO = 65536
ITERS = 3


temp_teacher = 0.07
temp_student = 0.1


def unit_rows(values):
    wide = values.astype(jnp.float32)
    return (wide * lax.rsqrt(jnp.sum(wide * wide, axis=1, keepdims=True) + 1e-06)).astype(
        jnp.bfloat16
    )


def shards(teacher_feats, student_feats, prototypes):
    teach = unit_rows(teacher_feats)
    stud = unit_rows(student_feats)
    tok_rows = teach.shape[0]
    stacked = jnp.concatenate([teach, stud], axis=0)
    logits = lax.dot_general(
        stacked,
        unit_rows(lax.all_gather(prototypes, "dp", axis=0, tiled=True)),
        (((1,), (1,)), ((), ())),
        preferred_element_type=jnp.float32,
    )
    expo = jnp.exp(logits[:tok_rows] / temp_teacher)
    expz = jnp.exp(logits[tok_rows:] / temp_student)
    local_total = jnp.sum(expz, axis=1)
    student_sum = lax.psum(local_total, "head")
    weights_r = jnp.ones((tok_rows,), jnp.float32)
    weights_c = jnp.ones((expo.shape[1],), jnp.float32)
    for step in range(ITERS):
        col_local = jnp.dot(weights_r, expo, precision=lax.Precision.HIGHEST)
        weights_c = 1.0 / lax.psum(col_local, "dp")
        row_local = jnp.dot(expo, weights_c, precision=lax.Precision.HIGHEST)
        if step + 1 < ITERS:
            row_total = lax.psum(row_local, "head")
        else:
            row_total = lax.psum(row_local, "head")
        weights_r = 1.0 / row_total
    total_tokens = tok_rows * lax.axis_size("dp")
    scale = PROTO / (temp_student * math.sqrt(total_tokens))
    probs = expz / student_sum[:, None]
    targets = expo * weights_c[None, :] * weights_r[:, None]
    grads = (scale * (probs - targets)).astype(jnp.bfloat16)
    return lax.psum_scatter(
        lax.dot_general(grads, stud, (((0,), (0,)), ((), ())), preferred_element_type=jnp.float32),
        "dp",
        scatter_dimension=0,
        tiled=True,
    )


def solution(mesh):
    placed = (P("dp", None), P("dp", None), P(("dp", "head"), None))
    return jax.shard_map(
        shards, mesh=mesh, in_specs=placed, out_specs=P(("dp", "head"), None), check_vma=False
    )
```

profile of v0, /device:TPU:1, one launch (start us, length us, event | category | flops | bytes accessed | tf_op | source)
XLA Modules:
  0.0 860.1 jit_solution(8800835571829284137)
XLA Ops:
  6.5 0.0 all-gather.2.cloned.1.call-start
  6.5 0.7 all-gather.2.cloned.1.call-update
  7.3 0.0 reduce-scatter.2.cloned.1.call-start
  7.3 1.0 fusion.9
  8.3 1.0 fusion.11
  9.4 1.2 fusion.10
  10.6 91.6 %all-gather.2.cloned.1.call-done = bf16[8192,384]{1,0:T(8,128)(2,1)} async-done(((bf16[256,384]{1,0:T(8,128)(2,1)}), bf16[8192,384]{1,0:T(8,128)(2,1)}) %all-gather.2.cloned.1.call-update) | async-done | bytes 6291472 | tf_op jit(solution)/shard_map/all_gather | solution.py:30
  102.1 0.0 copy-start.1
  102.1 4.3 fusion
  106.4 0.3 copy-done.1
  106.7 4.7 fusion.5
  111.4 0.0 copy-start
  111.4 1.2 fusion.4
  112.6 4.8 fusion.16
  117.4 0.0 copy-done
  117.4 111.9 %psum.50 = f32[8192]{0:T(1024)S(1)} all-reduce(f32[8192]{0:T(1024)S(1)} %bitcast.22), channel_id=1, replica_groups=mesh['dp'=32,'head'=8] {'dp'}, use_global_device_ids=true, to_apply=%region_5.0 | all-reduce | flops 8192 | bytes 65536 | tf_op jit(solution)/shard_map/psum | solution.py:42
  229.3 9.3 %fusion.31 = f32[1,256]{1,0:T(1,128)S(1)} fusion(f32[8192,1]{0,1:T(1,128)S(1)} %bitcast.18, f32[512,8192]{1,0:T(8,128)} %copy-done), kind=kOutput, calls=%fused_computation.43 | convolution fusion | flops 27262976 | bytes 8422400 | tf_op jit(solution)/shard_map/dot_general | solution.py:43
  238.6 40.9 %psum.51 = f32[256]{0:T(256)S(1)} all-reduce(f32[256]{0:T(256)S(1)} %bitcast.24), channel_id=1, replica_groups=mesh['dp'=32,'head'=8] {'head'}, use_global_device_ids=true, to_apply=%region_6.0 | all-reduce | flops 256 | bytes 2048 | tf_op jit(solution)/shard_map/psum | solution.py:45
  279.5 8.2 fusion.29
  287.7 109.9 %psum.52 = f32[8192]{0:T(1024)S(1)} all-reduce(f32[8192]{0:T(1024)S(1)} %bitcast.19), channel_id=1, replica_groups=mesh['dp'=32,'head'=8] {'dp'}, use_global_device_ids=true, to_apply=%region_7.0 | all-reduce | flops 8192 | bytes 65536 | tf_op jit(solution)/shard_map/psum | solution.py:42
  397.6 9.3 %fusion.27 = f32[1,256]{1,0:T(1,128)S(1)} fusion(f32[8192,1]{0,1:T(1,128)S(1)} %bitcast.20, f32[512,8192]{1,0:T(8,128)} %copy-done), kind=kOutput, calls=%fused_computation.41 | convolution fusion | flops 27262976 | bytes 8422400 | tf_op jit(solution)/shard_map/dot_general | solution.py:43
  406.9 40.4 %psum.53 = f32[256]{0:T(256)S(1)} all-reduce(f32[256]{0:T(256)S(1)} %bitcast.26), channel_id=1, replica_groups=mesh['dp'=32,'head'=8] {'head'}, use_global_device_ids=true, to_apply=%region_8.0 | all-reduce | flops 256 | bytes 2048 | tf_op jit(solution)/shard_map/psum | solution.py:45
  447.3 8.2 fusion.25
  455.5 109.9 %psum.54 = f32[8192]{0:T(1024)S(1)} all-reduce(f32[8192]{0:T(1024)S(1)} %bitcast.21), channel_id=1, replica_groups=mesh['dp'=32,'head'=8] {'dp'}, use_global_device_ids=true, to_apply=%region_9.0 | all-reduce | flops 8192 | bytes 65536 | tf_op jit(solution)/shard_map/psum | solution.py:42
  565.4 9.3 %fusion.22 = f32[1,256]{1,0:T(1,128)S(1)} fusion(f32[8192,1]{0,1:T(1,128)S(1)} %bitcast.17, f32[512,8192]{1,0:T(8,128)} %copy-done), kind=kOutput, calls=%fused_computation.39 | convolution fusion | flops 27262976 | bytes 8422400 | tf_op jit(solution)/shard_map/dot_general | solution.py:43
  574.6 40.2 %all-reduce = (f32[256]{0:T(256)S(1)}, f32[256]{0:T(256)S(1)}) all-reduce(f32[256]{0:T(256)S(1)} %bitcast.23, f32[256]{0:T(256)S(1)} %fusion.4), channel_id=1, replica_groups=mesh['dp'=32,'head'=8] {'head'}, use_global_device_ids=true, to_apply=%region_10.0 | all-reduce | flops 512 | bytes 4096 | tf_op jit(solution)/shard_map/psum | solution.py:47
  614.8 10.7 %fusion.8 = f32[8192,384]{1,0:T(8,128)} fusion(bf16[256,384]{1,0:T(8,128)(2,1)S(1)} %get-tuple-element.8, f32[512,8192]{1,0:T(8,128)} %copy-done, f32[256]{0:T(256)S(1)} %broadcast_divide_fusion.5, f32[8192]{0:T(1024)S(1)} %broadcast_divide_fusion, f32[256]{0:T(256)S(1)} %get-tuple-element.6), kind=kOutput, calls=%fused_computation.12 | convolution fusion | flops 1627389952 | bytes 29591552 | tf_op jit(solution)/shard_map/dot_general | solution.py:55
  625.5 0.0 reduce-scatter.2.cloned.1.call-update
  625.5 227.7 %reduce-scatter.2.cloned.1.call-done = f32[256,384]{1,0:T(8,128)} async-done(((f32[8192,384]{1,0:T(8,128)}), f32[256,384]{1,0:T(8,128)}) %reduce-scatter.2.cloned.1.call-update) | async-done | bytes 393232 | tf_op jit(solution)/shard_map/reduce_scatter | solution.py:54
  (9 shorter events, 0.1 us)
Async XLA Ops:
  6.5 95.6 %all-gather.2.cloned.1.call-start = ((), (), s32[]{:S(2)}) async-start(), calls=%async_computation.1 | async-start | bytes 6488064 | tf_op jit(solution)/shard_map/all_gather | solution.py:30
  7.3 846.0 %reduce-scatter.2.cloned.1.call-start = ((), (), s32[]{:S(2)}) async-start(), calls=%async_computation.2 | async-start | bytes 12976128 | tf_op jit(solution)/shard_map/reduce_scatter | solution.py:54
  102.1 4.6 copy-start.1
  111.4 6.0 copy-start
Sparse Core Ops, SparseCore 0:
  9.9 92.1 all-gather.1
  625.6 227.5 reduce-scatter.1
where the time goes:
time: 864 us; the launch traced here: 860 us
  blocking collectives  453 us (52%)
  waiting for transfers between devices  320 us (37%)
  matrix products  64.3 us (7%)
  between operations  13.5 us (2%)
  other arithmetic  8.77 us (1%)
    psum x3, blocking collectives, shards(): weights_c = 1.0 / lax.psum(col_local, 'dp')  332 us
    reduce_scatter x1, waiting for transfers between devices, shards(): lax.psum_scatter(lax.dot_general(grads, stud, (((0,), (0,)), ((), ())), p...  228 us
    psum x3, blocking collectives, shards(): row_total = lax.psum(row_local, 'head')  122 us
    all_gather x1, waiting for transfers between devices, shards(): lax.all_gather(prototypes, 'dp', axis=0, tiled=True)  91.6 us
    dot_general x3, matrix products, shards(): row_local = jnp.dot(expo, weights_c, precision=lax.Precision.HIGHEST)  27.8 us
    dot_general x3, matrix products, shards(): col_local = jnp.dot(weights_r, expo, precision=lax.Precision.HIGHEST)  21.2 us
  transfers between devices with their start and end apart: 2, of which 2 were waited for; matrix products, arithmetic and copies ran while one was open for 0% of the time, Pallas kernels for 0%

commit v1 on v0

v1 whole, which is shorter than its diff:
```python
import functools
import math

import jax
import jax.numpy as jnp
from jax import lax
from jax.experimental import pallas as pl
from jax.experimental.pallas import tpu as pltpu
from jax.sharding import Mesh, PartitionSpec as P

K = 384
PROTO = 65536
TOKENS = 8192
ITERS = 3
TEMP_TEACHER = 0.07
TEMP_STUDENT = 0.1
LOG2E = math.log2(math.e)
SCALE = PROTO / (TEMP_STUDENT * math.sqrt(TOKENS))

NZ, NY, NX, NC = 8, 4, 4, 2
TOK_BLOCK = TOKENS // (NZ * NY)
TOK_HALF = TOK_BLOCK // NC
PRO_BLOCK = PROTO // (NZ * NY * NX * NC)
TOK = TOK_HALF * NZ
PRO = PRO_BLOCK * NY * NC
HALF = PRO // 2
LANES = 128
TROWS = TOK // LANES
PROWS = PRO // LANES
TGROUP = NY * NC
PGROUP = NZ * NX

F32 = jnp.float32
BF16 = jnp.bfloat16
VMEM = pl.BlockSpec(memory_space=pltpu.VMEM)
PARAMS = pltpu.CompilerParams(vmem_limit_bytes=24 * 1024 * 1024)
CONTRACT_LAST = (((1,), (1,)), ((), ()))


def pinned(x):
    return pltpu.with_memory_space_constraint(x, pltpu.VMEM)


def unit(values):
    wide = values.astype(F32)
    return (wide * lax.rsqrt(jnp.sum(wide * wide, axis=1, keepdims=True) + 1e-06)).astype(BF16)


def norm_kernel(teach_ref, stud_ref, proto_ref, teach_out, stud_out, proto_out):
    core = lax.axis_index("core")
    teach = unit(teach_ref[pl.ds(pl.multiple_of(core * TOK_HALF, TOK_HALF), TOK_HALF), :])
    for z in range(NZ):
        teach_out[z] = teach
    stud_out[...] = unit(stud_ref[...])
    proto_out[...] = unit(proto_ref[...])


def to_rows(values):
    return jnp.sum(values.T, axis=0, keepdims=True)


def to_cols(row):
    return jnp.broadcast_to(row, (LANES, LANES)).T


def block_row(step, which):
    core = lax.axis_index("core")
    owner = core if which == 0 else 1 - core
    place = lax.rem(lax.axis_index("y") + (NY - step), NY)
    return pl.multiple_of(owner * HALF + place * PRO_BLOCK, PRO_BLOCK)


def teacher_kernel(teach_ref, *refs):
    protos, (expo_ref, sums_ref) = refs[:NY], refs[NY:]
    teach = teach_ref[...].reshape(TOK, K)
    for step in range(NY):
        for which in range(NC):
            base = block_row(step, which)
            logits = lax.dot_general(
                protos[step][which * PRO_BLOCK : (which + 1) * PRO_BLOCK, :],
                teach,
                CONTRACT_LAST,
                preferred_element_type=F32,
            )
            expo_ref[pl.ds(base, PRO_BLOCK), :] = jnp.exp2(logits * (LOG2E / TEMP_TEACHER))
    col_sums(expo_ref, None, sums_ref)


def col_sums(expo_ref, weights, sums_ref):
    def group(i, carry):
        rows = pl.ds(pl.multiple_of(i * LANES, LANES), LANES)
        total = None
        for j in range(TROWS):
            term = expo_ref[rows, j * LANES : (j + 1) * LANES]
            if weights is not None:
                term = term * weights[j : j + 1, :]
            total = term if total is None else total + term
        sums_ref[0, pl.ds(i, 1), :] = to_rows(total)
        return carry

    lax.fori_loop(0, PROWS, group, 0, unroll=2)
    for peer in range(1, TGROUP):
        sums_ref[peer] = sums_ref[0]


def col_kernel(row_sums_ref, expo_ref, sums_ref):
    weights = 1.0 / jnp.sum(row_sums_ref[...], axis=0)
    col_sums(expo_ref, weights, sums_ref)


def row_sums(expo_ref, weights_ref):
    def group(i, totals):
        rows = pl.ds(pl.multiple_of(i * LANES, LANES), LANES)
        wide = to_cols(weights_ref[pl.ds(i, 1), :])
        out = []
        for j in range(TROWS):
            term = expo_ref[rows, j * LANES : (j + 1) * LANES] * wide
            out.append(totals[j] + jnp.sum(term.reshape(LANES // 8, 8, LANES), axis=0))
        return tuple(out)

    zero = jnp.zeros((8, LANES), F32)
    totals = lax.fori_loop(0, PROWS, group, (zero,) * TROWS, unroll=2)
    return jnp.concatenate([jnp.sum(t, axis=0, keepdims=True) for t in totals], axis=0)


def row_kernel(col_sums_ref, expo_ref, sums_ref, weights_ref):
    weights_ref[...] = 1.0 / jnp.sum(col_sums_ref[...], axis=0)
    sums = row_sums(expo_ref, weights_ref)
    for peer in range(PGROUP):
        sums_ref[peer] = sums


def last_row_kernel(col_sums_ref, expo_ref, stud_sums_ref, sums_ref, weights_ref):
    weights_ref[...] = 1.0 / jnp.sum(col_sums_ref[...], axis=0)
    sums = jnp.concatenate([row_sums(expo_ref, weights_ref), stud_sums_ref[...]], axis=0)
    for peer in range(PGROUP):
        sums_ref[peer] = sums


def student_kernel(stud_ref, *refs):
    protos, (expz_ref, stud_out, sums_ref) = refs[:NY], refs[NY:]
    core = lax.axis_index("core")
    half = pl.ds(pl.multiple_of(core * TOK_HALF, TOK_HALF), TOK_HALF)
    for z in range(NZ):
        stud_out[z * TOK_HALF : (z + 1) * TOK_HALF, :] = stud_ref[z, half, :]
    stud = stud_out[...]
    totals = [jnp.zeros((8, LANES), F32)] * TROWS
    for step in range(NY):
        for which in range(NC):
            base = block_row(step, which)
            logits = lax.dot_general(
                protos[step][which * PRO_BLOCK : (which + 1) * PRO_BLOCK, :],
                stud,
                CONTRACT_LAST,
                preferred_element_type=F32,
            )
            expz = jnp.exp2(logits * (LOG2E / TEMP_STUDENT))
            expz_ref[pl.ds(base, PRO_BLOCK), :] = expz
            for j in range(TROWS):
                part = expz[:, j * LANES : (j + 1) * LANES]
                totals[j] = totals[j] + jnp.sum(part.reshape(PRO_BLOCK // 8, 8, LANES), axis=0)
    sums_ref[...] = jnp.concatenate([jnp.sum(t, axis=0, keepdims=True) for t in totals], axis=0)


def grad_kernel(other, col_sums_ref, row_sums_ref, expo_ref, expz_ref, stud_ref, out_ref, weights_ref):
    core = lax.axis_index("core")
    owner = 1 - core if other else core
    weights_ref[...] = 1.0 / jnp.sum(col_sums_ref[...], axis=0)
    totals = jnp.sum(row_sums_ref[...], axis=0)
    target_scale = SCALE / totals[:TROWS]
    prob_scale = SCALE / totals[TROWS:]
    stud = stud_ref[...]
    block = 256
    for i in range(HALF // block):
        base = pl.multiple_of(owner * HALF + i * block, block)
        parts = []
        for k in range(block // LANES):
            wide = to_cols(weights_ref[pl.ds(owner * (HALF // LANES) + i * (block // LANES) + k, 1), :])
            rows = pl.ds(pl.multiple_of(base + k * LANES, LANES), LANES)
            cols = []
            for j in range(TROWS):
                lanes = slice(j * LANES, (j + 1) * LANES)
                target = (expo_ref[rows, lanes] * wide) * target_scale[j : j + 1, :]
                prob = expz_ref[rows, lanes] * prob_scale[j : j + 1, :]
                cols.append((prob - target).astype(BF16))
            parts.append(jnp.concatenate(cols, axis=1))
        grads = jnp.concatenate(parts, axis=0)
        out_ref[i * block : (i + 1) * block, :] = jnp.dot(grads, stud, preferred_element_type=F32)


def call(kernel, out_shape, *args, scratch=()):
    return pl.pallas_call(
        kernel,
        out_shape=out_shape,
        in_specs=[VMEM] * len(args),
        out_specs=jax.tree.map(lambda _: VMEM, out_shape),
        scratch_shapes=scratch,
        compiler_params=PARAMS,
    )(*args)


def shards(teacher_feats, student_feats, prototypes):
    struct = jax.ShapeDtypeStruct
    teach, stud, own = call(
        norm_kernel,
        (
            struct((NZ, TOK_HALF, K), BF16),
            struct((TOK_BLOCK, K), BF16),
            struct((PRO_BLOCK, K), BF16),
        ),
        teacher_feats,
        student_feats,
        prototypes,
    )
    other = lax.ppermute(own, "core", [(0, 1), (1, 0)])
    pair = jnp.concatenate([own, other], axis=0)
    protos = [pair] + [
        lax.ppermute(pair, "y", [(i, (i + step) % NY) for i in range(NY)]) for step in range(1, NY)
    ]
    teach = lax.all_to_all(teach, "z", 0, 0, tiled=True)
    teach, stud = lax.optimization_barrier((teach, stud))
    stud_all = lax.all_gather(stud, "z", axis=0)

    col_shape = struct((TGROUP, PROWS, LANES), F32)
    row_shape = struct((PGROUP, TROWS, LANES), F32)
    weights = pltpu.VMEM((PROWS, LANES), F32)

    expo, cols = call(
        teacher_kernel, (pltpu.VMEM((PRO, TOK), F32), col_shape), teach, *protos
    )
    cols = lax.all_to_all(cols, ("y", "core"), 0, 0, tiled=True)
    for _ in range(ITERS - 1):
        rows = call(row_kernel, row_shape, cols, pinned(expo), scratch=(weights,))
        rows = lax.all_to_all(rows, ("z", "x"), 0, 0, tiled=True)
        cols = call(col_kernel, col_shape, rows, pinned(expo))
        cols = lax.all_to_all(cols, ("y", "core"), 0, 0, tiled=True)
    expz, stud_rows, stud_sums = call(
        student_kernel,
        (pltpu.VMEM((PRO, TOK), F32), struct((TOK, K), BF16), struct((TROWS, LANES), F32)),
        stud_all,
        *protos,
    )
    rows = call(
        last_row_kernel,
        struct((PGROUP, 2 * TROWS, LANES), F32),
        cols,
        pinned(expo),
        stud_sums,
        scratch=(weights,),
    )
    rows = lax.all_to_all(rows, ("z", "x"), 0, 0, tiled=True)

    def grad(for_other):
        return call(
            functools.partial(grad_kernel, for_other),
            struct((HALF, K), F32),
            cols,
            rows,
            pinned(expo),
            pinned(expz),
            stud_rows,
            scratch=(weights,),
        )

    sent = lax.ppermute(grad(True), "core", [(0, 1), (1, 0)])
    total = (grad(False) + sent).reshape(NY, PRO_BLOCK, K)
    parts = lax.all_to_all(total.astype(BF16), "y", 0, 0, tiled=True)
    return jnp.sum(parts.astype(F32), axis=0)


def solution(mesh):
    grid = Mesh(mesh.devices.reshape(NZ, NY, NX, NC), ("z", "y", "x", "core"))
    tokens = P(("z", "y"), None)
    protos = P(("z", "y", "x", "core"), None)
    return jax.shard_map(
        shards, mesh=grid, in_specs=(tokens, tokens, protos), out_specs=protos, check_vma=False
    )
```

time: 864 us -> 182 us (0.21)
  blocking collectives: 453 us -> 104 us
  waiting for transfers between devices: 320 us -> 22.7 us
  matrix products: 64.3 us -> 0 us
  Pallas kernels: 0 us -> 15.9 us
  starting transfers between devices: 0.04 us -> 14.1 us
  local copies, waits for them, and re-layouts: 0.32 us -> 10.9 us
    psum x6 -> x0, blocking collectives: 453 us -> none  [the longest x3 332 us: shards(): weights_c = 1.0 / lax.psum(col_local, 'dp')]
    reduce_scatter x1 -> x0, waiting for transfers between devices: 228 us -> none  [shards(): lax.psum_scatter(lax.dot_general(grads, stud, (((0,), (0,)), ((), ())), p...]
    all_to_all x0 -> x7, blocking collectives: none -> 104 us  [the longest x3 41 us: shards(): rows = lax.all_to_all(rows, ('z', 'x'), 0, 0, tiled=True)]
    all_gather x1, waiting for transfers between devices: 91.6 us -> 0.01 us  [shards(): stud_all = lax.all_gather(stud, 'z', axis=0)]
    dot_general x8 -> x0, matrix products: 64.3 us -> none  [the longest x3 27.8 us: shards(): row_local = jnp.dot(expo, weights_c, precision=lax.Precision.HIGHEST)]
    ppermute x0 -> x5, waiting for transfers between devices: none -> 22.7 us  [the longest x3 19.9 us: shards(): lax.ppermute(pair, 'y', [(i, (i + step) % NY) for i in range(NY)])]
    pallas_call x0 -> x10, Pallas kernels: none -> 15.9 us  [call(): pl.pallas_call(kernel, out_shape=out_shape, in_specs=[VMEM] * len(args),...]
    unnamed x4 -> x17, local copies, waits for them, and re-layouts: 0.32 us -> 10.8 us
  transfers between devices with their start and end apart: 2 -> 7, of which waited for: 2 -> 4; matrix products, arithmetic and copies ran while one was open for 0% -> 0% of each run, Pallas kernels for 0% -> 7%
where the time goes in v1:
time: 182 us
  blocking collectives  104 us (57%)
  waiting for transfers between devices  22.7 us (12%)
  Pallas kernels  15.9 us (9%)
  starting transfers between devices  14.1 us (8%)
  between operations  13.5 us (7%)
  local copies, waits for them, and re-layouts  10.9 us (6%)
    all_to_all x3, blocking collectives, shards(): rows = lax.all_to_all(rows, ('z', 'x'), 0, 0, tiled=True)  41 us
    all_to_all x1, blocking collectives, shards(): teach = lax.all_to_all(teach, 'z', 0, 0, tiled=True)  30.4 us
    ppermute x3, waiting for transfers between devices, shards(): lax.ppermute(pair, 'y', [(i, (i + step) % NY) for i in range(NY)])  19.9 us
    all_to_all x2, blocking collectives, shards(): cols = lax.all_to_all(cols, ('y', 'core'), 0, 0, tiled=True)  17.1 us
    pallas_call x10, Pallas kernels, call(): pl.pallas_call(kernel, out_shape=out_shape, in_specs=[VMEM] * len(args),...  15.9 us
    all_to_all x1, blocking collectives, shards(): parts = lax.all_to_all(total.astype(BF16), 'y', 0, 0, tiled=True)  15.3 us
    unnamed x17, local copies, waits for them, and re-layouts  10.8 us
    all_to_all x1, starting transfers between devices, shards(): cols = lax.all_to_all(cols, ('y', 'core'), 0, 0, tiled=True)  5.48 us
  transfers between devices with their start and end apart: 7, of which 4 were waited for; matrix products, arithmetic and copies ran while one was open for 0% of the time, Pallas kernels for 7%

profile of v1, /device:TPU:1, one launch (start us, length us, event | category | flops | bytes accessed | tf_op | source)
XLA Modules:
  0.0 181.9 jit_solution(3110080410495504463)
XLA Ops:
  6.5 0.0 all-gather.3.cloned.1.call-start
  6.5 0.0 copy-start.5
  6.5 0.9 copy-done.5
  7.5 0.0 copy-start.6
  7.5 0.9 copy-done.6
  8.4 0.0 copy-start.7
  8.4 0.9 copy-done.7
  9.3 0.9 shard_map.37
  10.2 30.4 %all_to_all.40.teach_ref = bf16[8,128,384]{2,1,0:T(8,128)(2,1)S(1)} all-to-all(bf16[8,128,384]{2,1,0:T(8,128)(2,1)S(1)} %get-tuple-element.15), channel_id=1, replica_groups=mesh['z'=8,'y'=4,'x'=4,'core'=2] {'z'}, dimensions={0} | all-to-all | bytes 1572864 | tf_op jit(solution)/shard_map/all_to_all | solution.py:220
  40.6 0.0 all-gather.3.cloned.1.call-update
  40.6 2.5 %collective-permute-start = (bf16[256,384]{1,0:T(8,128)(2,1)S(1)}, bf16[256,384]{1,0:T(8,128)(2,1)S(1)}, u32[]{:S(2)}, u32[]{:S(2)}) collective-permute-start(bf16[256,384]{1,0:T(8,128)(2,1)S(1)} %get-tuple-element.18), channel_id=1, source_target_pairs={{0,1},{1,0},{2,3},{3,2},{4,5},{5,4},{6,7},{7,6},{8,9},{9,8},{10,11... | collective-permute-start | bytes 589832 | tf_op jit(solution)/shard_map/ppermute | solution.py:215
  43.2 1.0 collective-permute-done
  44.3 2.8 %collective-permute-start.3 = (bf16[512,384]{1,0:T(8,128)(2,1)S(1)}, bf16[512,384]{1,0:T(8,128)(2,1)S(1)}, u32[]{:S(2)}, u32[]{:S(2)}) collective-permute-start(bf16[512,384]{1,0:T(8,128)(2,1)S(1)} %constant_dynamic-update-slice_fusion.refs_0_), channel_id=1, source_target_pairs={{0,24},{8,0},{16,8},{24,16},{1,25},{9,1},{17,9},{25,17},{2,26},{10... | collective-permute-start | bytes 1179656 | tf_op jit(solution)/shard_map/ppermute | solution.py:218
  47.1 0.3 collective-permute-start.2
  47.4 0.7 collective-permute-start.1
  48.1 15.4 %collective-permute-done.3.refs_3_ = bf16[512,384]{1,0:T(8,128)(2,1)S(1)} collective-permute-done((bf16[512,384]{1,0:T(8,128)(2,1)S(1)}, bf16[512,384]{1,0:T(8,128)(2,1)S(1)}, u32[]{:S(2)}, u32[]{:S(2)}) %collective-permute-start.3) | collective-permute-done | bytes 393248 | tf_op jit(solution)/shard_map/ppermute | solution.py:218
  63.5 0.0 collective-permute-done.2.refs_2_
  63.5 4.6 %collective-permute-done.1.refs_1_ = bf16[512,384]{1,0:T(8,128)(2,1)S(1)} collective-permute-done((bf16[512,384]{1,0:T(8,128)(2,1)S(1)}, bf16[512,384]{1,0:T(8,128)(2,1)S(1)}, u32[]{:S(2)}, u32[]{:S(2)}) %collective-permute-start.1) | collective-permute-done | bytes 393248 | tf_op jit(solution)/shard_map/ppermute | solution.py:218
  68.1 3.4 %shard_map.38 = (f32[2048,1024]{1,0:T(8,128)S(1)}, f32[8,16,128]{2,1,0:T(8,128)S(1)}) custom-call(bf16[8,128,384]{2,1,0:T(8,128)(2,1)S(1)} %all_to_all.40.teach_ref, bf16[512,384]{1,0:T(8,128)(2,1)S(1)} %constant_dynamic-update-slice_fusion.refs_0_, bf16[512,384]{1,0:T(8,128)(2,1)S(1)} %collective-permute-done.1.refs_1_, ...), custom_call_target="tpu_custom_call" | custom-call | tf_op jit(solution)/shard_map/pallas_call | solution.py:192
  71.4 0.0 copy-start
  71.5 7.7 %all_to_all.41.col_sums_ref = f32[8,16,128]{2,1,0:T(8,128)S(1)} all-to-all(f32[8,16,128]{2,1,0:T(8,128)S(1)} %get-tuple-element.19), channel_id=1, replica_groups=mesh['z'=8,'y'=4,'x'=4,'core'=2] {'y','core'}, dimensions={0} | all-to-all | bytes 131072 | tf_op jit(solution)/shard_map/all_to_all | solution.py:231
  79.2 1.2 shard_map.39
  80.3 13.6 %all_to_all.42.row_sums_ref = f32[32,8,128]{2,1,0:T(8,128)S(1)} all-to-all(f32[32,8,128]{2,1,0:T(8,128)S(1)} %shard_map.39), channel_id=1, replica_groups=mesh['z'=8,'y'=4,'x'=4,'core'=2] {'z','x'}, dimensions={0} | all-to-all | bytes 262144 | tf_op jit(solution)/shard_map/all_to_all | solution.py:234
  93.9 1.2 shard_map.40
  95.2 9.4 %all_to_all.43.col_sums_ref = f32[8,16,128]{2,1,0:T(8,128)S(1)} all-to-all(f32[8,16,128]{2,1,0:T(8,128)S(1)} %shard_map.40), channel_id=1, replica_groups=mesh['z'=8,'y'=4,'x'=4,'core'=2] {'y','core'}, dimensions={0} | all-to-all | bytes 131072 | tf_op jit(solution)/shard_map/all_to_all | solution.py:236
  104.5 1.2 shard_map.41
  105.7 12.4 %all_to_all.44.row_sums_ref = f32[32,8,128]{2,1,0:T(8,128)S(1)} all-to-all(f32[32,8,128]{2,1,0:T(8,128)S(1)} %shard_map.41), channel_id=1, replica_groups=mesh['z'=8,'y'=4,'x'=4,'core'=2] {'z','x'}, dimensions={0} | all-to-all | bytes 262144 | tf_op jit(solution)/shard_map/all_to_all | solution.py:234
  118.1 0.0 copy-done
  118.1 1.8 %shard_map.42 = f32[8,16,128]{2,1,0:T(8,128)} custom-call(f32[32,8,128]{2,1,0:T(8,128)S(1)} %all_to_all.44.row_sums_ref, f32[2048,1024]{1,0:T(8,128)S(1)} %get-tuple-element.20.expo_ref), custom_call_target="tpu_custom_call" | custom-call | tf_op jit(solution)/shard_map/pallas_call | solution.py:192
  119.9 5.5 %all-to-all-start.5 = ((f32[8,16,128]{2,1,0:T(8,128)}), f32[8,16,128]{2,1,0:T(8,128)S(1)}, u32[]{:S(2)}, u32[]{:S(2)}) async-start(f32[8,16,128]{2,1,0:T(8,128)} %shard_map.42), calls=%async_computation.5 | async-start | bytes 131072 | tf_op jit(solution)/shard_map/all_to_all | solution.py:236
  125.4 0.0 all-gather.3.cloned.1.call-done
  125.4 0.0 copy-start.4
  125.4 1.4 copy-done.4
  126.8 2.4 %shard_map.43 = (f32[2048,1024]{1,0:T(8,128)S(1)}, bf16[1024,384]{1,0:T(8,128)(2,1)S(1)}, f32[8,128]{1,0:T(8,128)S(1)}) custom-call(bf16[8,256,384]{2,1,0:T(8,128)(2,1)S(1)} %bitcast.2, bf16[512,384]{1,0:T(8,128)(2,1)S(1)} %constant_dynamic-update-slice_fusion.refs_0_, bf16[512,384]{1,0:T(8,128)(2,1)S(1)} %collective-permute-done.1.refs_1_, ...), custom_call_target="tpu_custom_call" | custom-call | tf_op jit(solution)/shard_map/pallas_call | solution.py:192
  129.2 0.0 copy-start.2
  129.2 3.2 %copy-done.2 = f32[2048,1024]{1,0:T(8,128)} copy-done((f32[2048,1024]{1,0:T(8,128)}, f32[2048,1024]{1,0:T(8,128)S(1)}, u32[]{:S(2)}) %copy-start.2) | copy-done | bytes 8388632
  132.5 0.0 all-to-all-done.5.col_sums_ref
  132.5 0.0 copy-start.1
  132.5 3.4 %copy-done.1 = f32[2048,1024]{1,0:T(8,128)S(1)} copy-done((f32[2048,1024]{1,0:T(8,128)S(1)}, f32[2048,1024]{1,0:T(8,128)}, u32[]{:S(2)}) %copy-start.1) | copy-done | bytes 8388632
  135.9 0.0 copy-start.3
  135.9 1.2 shard_map.44
  137.0 15.1 %all_to_all.45.row_sums_ref = f32[32,16,128]{2,1,0:T(8,128)S(1)} all-to-all(f32[32,16,128]{2,1,0:T(8,128)S(1)} %shard_map.44), channel_id=1, replica_groups=mesh['z'=8,'y'=4,'x'=4,'core'=2] {'z','x'}, dimensions={0} | all-to-all | bytes 524288 | tf_op jit(solution)/shard_map/all_to_all | solution.py:251
  152.1 0.0 copy-done.3
  152.1 1.3 shard_map.46
  153.5 2.2 %collective-permute-start.4 = (f32[1024,384]{1,0:T(8,128)S(1)}, f32[1024,384]{1,0:T(8,128)S(1)}, u32[]{:S(2)}, u32[]{:S(2)}) collective-permute-start(f32[1024,384]{1,0:T(8,128)S(1)} %shard_map.46), channel_id=1, source_target_pairs={{0,1},{1,0},{2,3},{3,2},{4,5},{5,4},{6,7},{7,6},{8,9},{9,8},{10,11... | collective-permute-start | bytes 4718600 | tf_op jit(solution)/shard_map/ppermute | solution.py:265
  155.7 1.3 shard_map.45
  157.0 1.7 collective-permute-done.4
  158.7 0.2 add_convert_fusion
  158.9 15.3 %all_to_all.46 = bf16[4,256,384]{2,1,0:T(8,128)(2,1)S(1)} all-to-all(bf16[4,256,384]{2,1,0:T(8,128)(2,1)S(1)} %bitcast.3), channel_id=1, replica_groups=mesh['z'=8,'y'=4,'x'=4,'core'=2] {'y'}, dimensions={0} | all-to-all | bytes 1572864 | tf_op jit(solution)/shard_map/all_to_all | solution.py:267
  174.2 0.8 convert_reduce_fusion
  (2 shorter events, 0.1 us)
Async XLA Ops:
  6.5 118.9 %all-gather.3.cloned.1.call-start = ((), (), s32[]{:S(2)}) async-start(), calls=%async_computation.8 | async-start | bytes 1769472 | tf_op jit(solution)/shard_map/all_gather | solution.py:222
  6.5 0.9 copy-start.5
  7.5 0.9 copy-start.6
  8.4 0.9 copy-start.7
  40.6 3.6 %collective-permute-start = (bf16[256,384]{1,0:T(8,128)(2,1)S(1)}, bf16[256,384]{1,0:T(8,128)(2,1)S(1)}, u32[]{:S(2)}, u32[]{:S(2)}) collective-permute-start(bf16[256,384]{1,0:T(8,128)(2,1)S(1)} %get-tuple-element.18), channel_id=1, source_target_pairs={{0,1},{1,0},{2,3},{3,2},{4,5},{5,4},{6,7},{7,6},{8,9},{9,8},{10,11... | collective-permute-start | bytes 589832 | tf_op jit(solution)/shard_map/ppermute | solution.py:215
  44.3 19.2 %collective-permute-start.3 = (bf16[512,384]{1,0:T(8,128)(2,1)S(1)}, bf16[512,384]{1,0:T(8,128)(2,1)S(1)}, u32[]{:S(2)}, u32[]{:S(2)}) collective-permute-start(bf16[512,384]{1,0:T(8,128)(2,1)S(1)} %constant_dynamic-update-slice_fusion.refs_0_), channel_id=1, source_target_pairs={{0,24},{8,0},{16,8},{24,16},{1,25},{9,1},{17,9},{25,17},{2,26},{10... | collective-permute-start | bytes 1179656 | tf_op jit(solution)/shard_map/ppermute | solution.py:218
  47.1 16.4 %collective-permute-start.2 = (bf16[512,384]{1,0:T(8,128)(2,1)S(1)}, bf16[512,384]{1,0:T(8,128)(2,1)S(1)}, u32[]{:S(2)}, u32[]{:S(2)}) collective-permute-start(bf16[512,384]{1,0:T(8,128)(2,1)S(1)} %constant_dynamic-update-slice_fusion.refs_0_), channel_id=1, source_target_pairs={{0,16},{8,24},{16,0},{24,8},{1,17},{9,25},{17,1},{25,9},{2,18},{10... | collective-permute-start | bytes 1179656 | tf_op jit(solution)/shard_map/ppermute | solution.py:218
  47.4 20.6 %collective-permute-start.1 = (bf16[512,384]{1,0:T(8,128)(2,1)S(1)}, bf16[512,384]{1,0:T(8,128)(2,1)S(1)}, u32[]{:S(2)}, u32[]{:S(2)}) collective-permute-start(bf16[512,384]{1,0:T(8,128)(2,1)S(1)} %constant_dynamic-update-slice_fusion.refs_0_), channel_id=1, source_target_pairs={{0,8},{8,16},{16,24},{24,0},{1,9},{9,17},{17,25},{25,1},{2,10},{10... | collective-permute-start | bytes 1179656 | tf_op jit(solution)/shard_map/ppermute | solution.py:218
  71.4 46.6 %copy-start = (f32[2048,1024]{1,0:T(8,128)}, f32[2048,1024]{1,0:T(8,128)S(1)}, u32[]{:S(2)}) copy-start(f32[2048,1024]{1,0:T(8,128)S(1)} %get-tuple-element.20.expo_ref) | copy-start | bytes 25165828
  119.9 12.6 %all-to-all-start.5 = ((f32[8,16,128]{2,1,0:T(8,128)}), f32[8,16,128]{2,1,0:T(8,128)S(1)}, u32[]{:S(2)}, u32[]{:S(2)}) async-start(f32[8,16,128]{2,1,0:T(8,128)} %shard_map.42), calls=%async_computation.5 | async-start | bytes 131072 | tf_op jit(solution)/shard_map/all_to_all | solution.py:236
  125.4 1.4 copy-start.4
  129.2 3.2 %copy-start.2 = (f32[2048,1024]{1,0:T(8,128)}, f32[2048,1024]{1,0:T(8,128)S(1)}, u32[]{:S(2)}) copy-start(f32[2048,1024]{1,0:T(8,128)S(1)} %get-tuple-element.23.expz_ref) | copy-start | bytes 25165828
  132.5 3.4 %copy-start.1 = (f32[2048,1024]{1,0:T(8,128)S(1)}, f32[2048,1024]{1,0:T(8,128)}, u32[]{:S(2)}) copy-start(f32[2048,1024]{1,0:T(8,128)} %copy-done) | copy-start | bytes 25165828
  135.9 16.2 %copy-start.3 = (f32[2048,1024]{1,0:T(8,128)S(1)}, f32[2048,1024]{1,0:T(8,128)}, u32[]{:S(2)}) copy-start(f32[2048,1024]{1,0:T(8,128)} %copy-done.2) | copy-start | bytes 25165828
  153.5 5.3 %collective-permute-start.4 = (f32[1024,384]{1,0:T(8,128)S(1)}, f32[1024,384]{1,0:T(8,128)S(1)}, u32[]{:S(2)}, u32[]{:S(2)}) collective-permute-start(f32[1024,384]{1,0:T(8,128)S(1)} %shard_map.46), channel_id=1, source_target_pairs={{0,1},{1,0},{2,3},{3,2},{4,5},{5,4},{6,7},{7,6},{8,9},{9,8},{10,11... | collective-permute-start | bytes 4718600 | tf_op jit(solution)/shard_map/ppermute | solution.py:265
Sparse Core Ops, SparseCore 0:
  40.7 34.2 all-gather.2

commit v2 on v1

v2 whole, which is shorter than its diff:
```python
import functools
import math

import jax
import jax.numpy as jnp
from jax import lax
from jax.experimental import pallas as pl
from jax.experimental.pallas import tpu as pltpu
from jax.sharding import Mesh, PartitionSpec as P

K = 384
PROTO = 65536
TOKENS = 8192
ITERS = 3
TEMP_TEACHER = 0.07
TEMP_STUDENT = 0.1
LOG2E = math.log2(math.e)
SCALE = PROTO / (TEMP_STUDENT * math.sqrt(TOKENS))

NZ, NY, NX, NC = 8, 4, 4, 2
TOK_BLOCK = TOKENS // (NZ * NY)
TOK_HALF = TOK_BLOCK // NC
PRO_BLOCK = PROTO // (NZ * NY * NX * NC)
TOK = TOK_HALF * NZ
PRO = PRO_BLOCK * NY * NC
HALF = PRO // 2
LANES = 128
TROWS = TOK // LANES
PROWS = PRO // LANES
TGROUP = NY * NC
PGROUP = NZ * NX

F32 = jnp.float32
BF16 = jnp.bfloat16
VMEM = pl.BlockSpec(memory_space=pltpu.VMEM)
PARAMS = pltpu.CompilerParams(vmem_limit_bytes=24 * 1024 * 1024)
CONTRACT_LAST = (((1,), (1,)), ((), ()))


def pinned(x):
    return pltpu.with_memory_space_constraint(x, pltpu.VMEM)


def unit(values):
    wide = values.astype(F32)
    return (wide * lax.rsqrt(jnp.sum(wide * wide, axis=1, keepdims=True) + 1e-06)).astype(BF16)


def norm_kernel(teach_hbm, stud_hbm, teach_out, stud_out, teach_buf, stud_buf, sems):
    half = pl.ds(pl.multiple_of(lax.axis_index("core") * TOK_HALF, TOK_HALF), TOK_HALF)
    first = pltpu.make_async_copy(teach_hbm.at[half, :], teach_buf, sems.at[0])
    second = pltpu.make_async_copy(stud_hbm.at[half, :], stud_buf, sems.at[1])
    first.start()
    second.start()
    first.wait()
    teach = unit(teach_buf[...])
    for z in range(NZ):
        teach_out[z] = teach
    second.wait()
    stud_out[...] = unit(stud_buf[...])


def to_rows(values):
    return jnp.sum(values.T, axis=0, keepdims=True)


def to_cols(row):
    return jnp.broadcast_to(row, (LANES, LANES)).T


def block_row(step, which):
    core = lax.axis_index("core")
    owner = core if which == 0 else 1 - core
    place = lax.rem(lax.axis_index("y") + (NY - step), NY)
    return pl.multiple_of(owner * HALF + place * PRO_BLOCK, PRO_BLOCK)


def teacher_kernel(teach_ref, *refs):
    raw, (expo_ref, unit_ref, sums_ref, protos, sems) = refs[:NY], refs[NY:]
    copies = [pltpu.make_async_copy(raw[i], protos.at[i], sems.at[i]) for i in range(NY)]
    for copy in copies:
        copy.start()
    teach = teach_ref[...].reshape(TOK, K)
    for step in range(NY):
        copies[step].wait()
        for which in range(NC):
            base = block_row(step, which)
            proto = unit(protos[step, which * PRO_BLOCK : (which + 1) * PRO_BLOCK, :])
            unit_ref[pl.ds(base, PRO_BLOCK), :] = proto
            logits = lax.dot_general(
                proto,
                teach,
                CONTRACT_LAST,
                preferred_element_type=F32,
            )
            expo_ref[pl.ds(base, PRO_BLOCK), :] = jnp.exp2(logits * (LOG2E / TEMP_TEACHER))
    col_sums(expo_ref, None, sums_ref)


def col_sums(expo_ref, weights, sums_ref):
    def group(i, carry):
        rows = pl.ds(pl.multiple_of(i * LANES, LANES), LANES)
        total = None
        for j in range(TROWS):
            term = expo_ref[rows, j * LANES : (j + 1) * LANES]
            if weights is not None:
                term = term * weights[j : j + 1, :]
            total = term if total is None else total + term
        sums_ref[0, pl.ds(i, 1), :] = to_rows(total)
        return carry

    lax.fori_loop(0, PROWS, group, 0, unroll=2)
    for peer in range(1, TGROUP):
        sums_ref[peer] = sums_ref[0]


def col_kernel(row_sums_ref, expo_ref, sums_ref):
    weights = 1.0 / jnp.sum(row_sums_ref[...].astype(F32), axis=0)
    col_sums(expo_ref, weights, sums_ref)


def row_sums(expo_ref, weights_ref):
    def group(i, totals):
        rows = pl.ds(pl.multiple_of(i * LANES, LANES), LANES)
        wide = to_cols(weights_ref[pl.ds(i, 1), :])
        out = []
        for j in range(TROWS):
            term = expo_ref[rows, j * LANES : (j + 1) * LANES] * wide
            out.append(totals[j] + jnp.sum(term.reshape(LANES // 8, 8, LANES), axis=0))
        return tuple(out)

    zero = jnp.zeros((8, LANES), F32)
    totals = lax.fori_loop(0, PROWS, group, (zero,) * TROWS, unroll=2)
    return jnp.concatenate([jnp.sum(t, axis=0, keepdims=True) for t in totals], axis=0)


def row_kernel(col_sums_ref, expo_ref, sums_ref, weights_ref):
    weights_ref[...] = 1.0 / jnp.sum(col_sums_ref[...], axis=0)
    sums = row_sums(expo_ref, weights_ref).astype(BF16)
    for peer in range(PGROUP):
        sums_ref[peer] = sums


def last_row_kernel(*refs):
    pieces, (col_sums_ref, proto_ref, expo_ref), outs = refs[:4], refs[4:7], refs[7:]
    expz_ref, stud_out, sums_ref, weights_ref = outs
    place = lax.axis_index("z")
    offsets = [0]
    for piece, hop in zip(pieces, (0, 4, 2, 1)):
        hops = [o ^ hop for o in offsets]
        for i, hop_to in enumerate(hops):
            rows = pl.ds(pl.multiple_of((place ^ hop_to) * TOK_HALF, TOK_HALF), TOK_HALF)
            stud_out[rows, :] = piece[i * TOK_HALF : (i + 1) * TOK_HALF, :]
        if hop:
            offsets = offsets + hops
    stud = stud_out[...]
    weights_ref[...] = 1.0 / jnp.sum(col_sums_ref[...], axis=0)
    totals = [jnp.zeros((8, LANES), F32)] * TROWS
    for i in range(PRO // PRO_BLOCK):
        rows = slice(i * PRO_BLOCK, (i + 1) * PRO_BLOCK)
        logits = lax.dot_general(
            proto_ref[rows, :], stud, CONTRACT_LAST, preferred_element_type=F32
        )
        expz = jnp.exp2(logits * (LOG2E / TEMP_STUDENT))
        expz_ref[rows, :] = expz
        for j in range(TROWS):
            part = expz[:, j * LANES : (j + 1) * LANES]
            totals[j] = totals[j] + jnp.sum(part.reshape(PRO_BLOCK // 8, 8, LANES), axis=0)
    stud_sums = [jnp.sum(t, axis=0, keepdims=True) for t in totals]
    sums = jnp.concatenate([row_sums(expo_ref, weights_ref)] + stud_sums, axis=0).astype(BF16)
    for peer in range(PGROUP):
        sums_ref[peer] = sums


def grad_kernel(other, col_sums_ref, row_sums_ref, expo_ref, expz_ref, stud_ref, *refs):
    outs, weights_ref = refs[:NY], refs[NY]
    core = lax.axis_index("core")
    owner = 1 - core if other else core
    weights_ref[...] = 1.0 / jnp.sum(col_sums_ref[...], axis=0)
    totals = jnp.sum(row_sums_ref[...].astype(F32), axis=0)
    target_scale = SCALE / totals[:TROWS]
    prob_scale = SCALE / totals[TROWS:]
    stud = stud_ref[...]
    for step in range(NY):
        place = lax.rem(lax.axis_index("y") + step, NY)
        group = owner * (HALF // LANES) + place * (PRO_BLOCK // LANES)
        parts = []
        for k in range(PRO_BLOCK // LANES):
            wide = to_cols(weights_ref[pl.ds(group + k, 1), :])
            rows = pl.ds(pl.multiple_of((group + k) * LANES, LANES), LANES)
            cols = []
            for j in range(TROWS):
                lanes = slice(j * LANES, (j + 1) * LANES)
                target = (expo_ref[rows, lanes] * wide) * target_scale[j : j + 1, :]
                prob = expz_ref[rows, lanes] * prob_scale[j : j + 1, :]
                cols.append((prob - target).astype(BF16))
            parts.append(jnp.concatenate(cols, axis=1))
        grads = jnp.concatenate(parts, axis=0)
        outs[step][...] = jnp.dot(grads, stud, preferred_element_type=F32)


def call(kernel, out_shape, *args, scratch=(), specs=None):
    return pl.pallas_call(
        kernel,
        out_shape=out_shape,
        in_specs=specs or [VMEM] * len(args),
        out_specs=jax.tree.map(lambda _: VMEM, out_shape),
        scratch_shapes=scratch,
        compiler_params=PARAMS,
    )(*args)


def shift(x, axis, size, step):
    return lax.ppermute(x, axis, [(i, (i + step) % size) for i in range(size)])


def shards(teacher_feats, student_feats, prototypes):
    struct = jax.ShapeDtypeStruct
    other = shift(prototypes, "core", NC, 1)
    half = pltpu.VMEM((TOK_HALF, K), BF16)
    teach, stud = call(
        norm_kernel,
        (struct((NZ, TOK_HALF, K), BF16), struct((TOK_HALF, K), BF16)),
        pltpu.with_memory_space_constraint(teacher_feats, pltpu.HBM),
        pltpu.with_memory_space_constraint(student_feats, pltpu.HBM),
        scratch=(half, half, pltpu.SemaphoreType.DMA((2,))),
        specs=[pl.BlockSpec(memory_space=pl.ANY)] * 2,
    )
    pair = jnp.concatenate([prototypes, other], axis=0)
    pair, teach = lax.optimization_barrier((pair, teach))
    protos = [pair] + [shift(pair, "y", NY, step) for step in range(1, NY)]
    teach = lax.all_to_all(teach, "z", 0, 0, tiled=True)
    teach, stud = lax.optimization_barrier((teach, stud))

    col_shape = struct((TGROUP, PROWS, LANES), F32)
    row_shape = struct((PGROUP, TROWS, LANES), BF16)
    weights = pltpu.VMEM((PROWS, LANES), F32)

    expo, protos, cols = call(
        teacher_kernel,
        (pltpu.VMEM((PRO, TOK), F32), struct((PRO, K), BF16), col_shape),
        teach,
        *[pltpu.with_memory_space_constraint(p, pltpu.HBM) for p in protos],
        scratch=(pltpu.VMEM((NY, NC * PRO_BLOCK, K), BF16), pltpu.SemaphoreType.DMA((NY,))),
        specs=[VMEM] + [pl.BlockSpec(memory_space=pl.ANY)] * NY,
    )
    pieces = [stud]
    held = stud
    for step, hop in enumerate((4, 2, 1)):
        cols, held = lax.optimization_barrier((cols, held))
        got = lax.ppermute(held, "z", [(i, i ^ hop) for i in range(NZ)])
        cols = lax.all_to_all(cols, ("y", "core"), 0, 0, tiled=True)
        cols, got = lax.optimization_barrier((cols, got))
        pieces.append(got)
        if step + 1 < ITERS:
            rows = call(row_kernel, row_shape, cols, pinned(expo), scratch=(weights,))
            held = jnp.concatenate(pieces, axis=0)
            rows, held = lax.optimization_barrier((rows, held))
            rows = lax.all_to_all(rows, ("z", "x"), 0, 0, tiled=True)
            cols = call(col_kernel, col_shape, rows, pinned(expo))
    expz, stud, rows = call(
        last_row_kernel,
        (
            pltpu.VMEM((PRO, TOK), F32),
            struct((TOK, K), BF16),
            struct((PGROUP, 2 * TROWS, LANES), BF16),
        ),
        *pieces,
        cols,
        protos,
        pinned(expo),
        scratch=(weights,),
    )
    rows = lax.all_to_all(rows, ("z", "x"), 0, 0, tiled=True)

    def grad(for_other):
        return call(
            functools.partial(grad_kernel, for_other),
            (struct((PRO_BLOCK, K), F32),) * NY,
            cols,
            rows,
            pinned(expo),
            pinned(expz),
            stud,
            scratch=(weights,),
        )

    sent = [shift(part, "core", NC, 1) for part in grad(True)]
    parts = [mine + part for mine, part in zip(grad(False), sent)]
    total = parts[0]
    for step in (2, 1, 3):
        total = total + shift(parts[step].astype(BF16), "y", NY, step).astype(F32)
    return total


def solution(mesh):
    grid = Mesh(mesh.devices.reshape(NZ, NY, NX, NC), ("z", "y", "x", "core"))
    tokens = P(("z", "y"), None)
    protos = P(("z", "y", "x", "core"), None)
    return jax.shard_map(
        shards, mesh=grid, in_specs=(tokens, tokens, protos), out_specs=protos, check_vma=False
    )
```

time: 182 us -> 146 us (0.80)
  blocking collectives: 104 us -> 67.8 us
  between operations: 13.5 us -> 0.14 us
  starting transfers between devices: 14.1 us -> 26.3 us
  local copies, waits for them, and re-layouts: 10.9 us -> 1.6 us
  waiting for transfers between devices: 22.7 us -> 29.6 us
  Pallas kernels: 15.9 us -> 18.2 us
    all_to_all x2 -> x0, blocking collectives: 45.7 us -> none  [the longest x1 30.4 us: shards(): teach = lax.all_to_all(teach, 'z', 0, 0, tiled=True)]
    all_to_all x1, waiting for transfers between devices: 0.01 us -> 19.9 us  [shards(): teach = lax.all_to_all(teach, 'z', 0, 0, tiled=True)]
    ppermute x5 -> x14, waiting for transfers between devices: 22.7 us -> 9.73 us  [the longest x11 8.73 us: shift(): return lax.ppermute(x, axis, [(i, (i + step) % size) for i in range(size)])]
    ppermute x5 -> x14, starting transfers between devices: 8.63 us -> 19.9 us  [the longest x11 13.8 us: shift(): return lax.ppermute(x, axis, [(i, (i + step) % size) for i in range(size)])]
    all_to_all x2 -> x3, blocking collectives: 17.1 us -> 27.6 us  [shards(): cols = lax.all_to_all(cols, ('y', 'core'), 0, 0, tiled=True)]
    unnamed x17 -> x8, local copies, waits for them, and re-layouts: 10.8 us -> 1.6 us
    pallas_call x10 -> x9, Pallas kernels: 15.9 us -> 18.2 us  [call(): pl.pallas_call(kernel, out_shape=out_shape, in_specs=specs or [VMEM] * le...]
  transfers between devices with their start and end apart: 7 -> 15, of which waited for: 4 -> 4; matrix products, arithmetic and copies ran while one was open for 0% -> 0% of each run, Pallas kernels for 7% -> 2%
where the time goes in v2:
time: 146 us
  blocking collectives  67.8 us (46%)
  waiting for transfers between devices  29.6 us (20%)
  starting transfers between devices  26.3 us (18%)
  Pallas kernels  18.2 us (12%)
  other arithmetic  1.99 us (1%)
  local copies, waits for them, and re-layouts  1.6 us (1%)
    all_to_all x3, blocking collectives, shards(): rows = lax.all_to_all(rows, ('z', 'x'), 0, 0, tiled=True)  40.1 us
    all_to_all x3, blocking collectives, shards(): cols = lax.all_to_all(cols, ('y', 'core'), 0, 0, tiled=True)  27.6 us
    all_to_all x1, waiting for transfers between devices, shards(): teach = lax.all_to_all(teach, 'z', 0, 0, tiled=True)  19.9 us
    pallas_call x9, Pallas kernels, call(): pl.pallas_call(kernel, out_shape=out_shape, in_specs=specs or [VMEM] * le...  18.2 us
    ppermute x11, starting transfers between devices, shift(): return lax.ppermute(x, axis, [(i, (i + step) % size) for i in range(size)])  13.8 us
    ppermute x11, waiting for transfers between devices, shift(): return lax.ppermute(x, axis, [(i, (i + step) % size) for i in range(size)])  8.73 us
    all_to_all x1, starting transfers between devices, shards(): teach = lax.all_to_all(teach, 'z', 0, 0, tiled=True)  6.46 us
    ppermute x3, starting transfers between devices, shards(): got = lax.ppermute(held, 'z', [(i, i ^ hop) for i in range(NZ)])  6.08 us
  transfers between devices with their start and end apart: 15, of which 4 were waited for; matrix products, arithmetic and copies ran while one was open for 0% of the time, Pallas kernels for 2%

profile of v2, /device:TPU:1, one launch (start us, length us, event | category | flops | bytes accessed | tf_op | source)
XLA Modules:
  0.0 145.6 jit_solution(7080480685834484013)
XLA Ops:
  0.0 3.2 %collective-permute-start = (bf16[256,384]{1,0:T(8,128)(2,1)}, bf16[256,384]{1,0:T(8,128)(2,1)S(1)}, u32[]{:S(2)}, u32[]{:S(2)}) collective-permute-start(bf16[256,384]{1,0:T(8,128)(2,1)} %param.5), channel_id=1, source_target_pairs={{0,1},{1,0},{2,3},{3,2},{4,5},{5,4},{6,7},{7,6},{8,9},{9,8},{10,11... | collective-permute-start | bytes 589832 | tf_op jit(solution)/shard_map/ppermute | solution.py:214
  3.2 1.9 %shard_map.37 = (bf16[8,128,384]{2,1,0:T(8,128)(2,1)}, bf16[128,384]{1,0:T(8,128)(2,1)S(1)}) custom-call(bf16[256,384]{1,0:T(8,128)(2,1)} %teach_hbm.1, bf16[256,384]{1,0:T(8,128)(2,1)} %stud_hbm.1), custom_call_target="tpu_custom_call" | custom-call | tf_op jit(solution)/shard_map/pallas_call | solution.py:203
  5.2 0.0 collective-permute-done
  5.2 1.0 pad_maximum_fusion.refs_0_
  6.2 0.0 copy-start
  6.2 6.5 %all-to-all-start = ((bf16[8,128,384]{2,1,0:T(8,128)(2,1)}), bf16[8,128,384]{2,1,0:T(8,128)(2,1)S(1)}, u32[]{:S(2)}, u32[]{:S(2)}) async-start(bf16[8,128,384]{2,1,0:T(8,128)(2,1)} %get-tuple-element.42), calls=%async_computation | async-start | bytes 1572864 | tf_op jit(solution)/shard_map/all_to_all | solution.py:232
  12.7 2.7 %collective-permute-start.3 = (bf16[512,384]{1,0:T(8,128)(2,1)S(1)}, bf16[512,384]{1,0:T(8,128)(2,1)S(1)}, u32[]{:S(2)}, u32[]{:S(2)}) collective-permute-start(bf16[512,384]{1,0:T(8,128)(2,1)S(1)} %pad_maximum_fusion.refs_0_), channel_id=1, source_target_pairs={{0,24},{8,0},{16,8},{24,16},{1,25},{9,1},{17,9},{25,17},{2,26},{10... | collective-permute-start | bytes 1179656 | tf_op jit(solution)/shard_map/ppermute | solution.py:214
  15.4 0.3 collective-permute-start.2
  15.7 0.7 collective-permute-start.1
  16.4 19.9 %all-to-all-done.teach_ref = bf16[8,128,384]{2,1,0:T(8,128)(2,1)S(1)} async-done(((bf16[8,128,384]{2,1,0:T(8,128)(2,1)}), bf16[8,128,384]{2,1,0:T(8,128)(2,1)S(1)}, u32[]{:S(2)}, u32[]{:S(2)}) %all-to-all-start) | async-done | bytes 786464 | tf_op jit(solution)/shard_map/all_to_all | solution.py:232
  36.3 0.0 collective-permute-done.3.refs_3_
  36.3 0.0 copy-start.1
  36.3 0.0 collective-permute-done.2.refs_2_
  36.3 0.0 copy-start.2
  36.3 0.0 collective-permute-done.1.refs_1_
  36.4 0.0 copy-done
  36.4 0.7 copy-done.1
  37.1 0.1 copy-done.2
  37.2 0.0 copy-start.3
  37.2 0.7 copy-done.3
  37.9 5.2 %shard_map.38 = (f32[2048,1024]{1,0:T(8,128)S(1)}, bf16[2048,384]{1,0:T(8,128)(2,1)S(1)}, f32[8,16,128]{2,1,0:T(8,128)S(1)}) custom-call(bf16[8,128,384]{2,1,0:T(8,128)(2,1)S(1)} %all-to-all-done.teach_ref, bf16[512,384]{1,0:T(8,128)(2,1)} %copy-done, bf16[512,384]{1,0:T(8,128)(2,1)} %copy-done.3, bf16[512,384]{1,0:T(8,128)(2,1)} %copy-done.2, ...), custom_call_target="tpu_custom_call" | custom-call | tf_op jit(solution)/shard_map/pallas_call | solution.py:203
  43.2 4.6 %collective-permute-start.4 = (bf16[128,384]{1,0:T(8,128)(2,1)S(1)}, bf16[128,384]{1,0:T(8,128)(2,1)S(1)}, u32[]{:S(2)}, u32[]{:S(2)}) collective-permute-start(bf16[128,384]{1,0:T(8,128)(2,1)S(1)} %get-tuple-element.49.refs_0_), channel_id=1, source_target_pairs={{0,128},{32,160},{64,192},{96,224},{128,0},{160,32},{192,64},{224,... | collective-permute-start | bytes 294920 | tf_op jit(solution)/shard_map/ppermute | solution.py:251
  47.8 8.0 %all_to_all.35.col_sums_ref = f32[8,16,128]{2,1,0:T(8,128)S(1)} all-to-all(f32[8,16,128]{2,1,0:T(8,128)S(1)} %get-tuple-element.48), channel_id=1, replica_groups=mesh['z'=8,'y'=4,'x'=4,'core'=2] {'y','core'}, dimensions={0} | all-to-all | bytes 131072 | tf_op jit(solution)/shard_map/all_to_all | solution.py:252
  55.8 0.0 collective-permute-done.4.refs_1_
  55.8 1.2 shard_map.39
  57.0 15.4 %all_to_all.36.row_sums_ref = bf16[32,8,128]{2,1,0:T(8,128)(2,1)S(1)} all-to-all(bf16[32,8,128]{2,1,0:T(8,128)(2,1)S(1)} %shard_map.39), channel_id=1, replica_groups=mesh['z'=8,'y'=4,'x'=4,'core'=2] {'z','x'}, dimensions={0} | all-to-all | bytes 131072 | tf_op jit(solution)/shard_map/all_to_all | solution.py:259
  72.4 1.2 shard_map.40
  73.6 0.8 collective-permute-start.5
  74.4 9.7 %all_to_all.37.col_sums_ref = f32[8,16,128]{2,1,0:T(8,128)S(1)} all-to-all(f32[8,16,128]{2,1,0:T(8,128)S(1)} %shard_map.40), channel_id=1, replica_groups=mesh['z'=8,'y'=4,'x'=4,'core'=2] {'y','core'}, dimensions={0} | all-to-all | bytes 131072 | tf_op jit(solution)/shard_map/all_to_all | solution.py:252
  84.1 1.0 collective-permute-done.5.refs_2_
  85.1 1.2 shard_map.41
  86.3 11.9 %all_to_all.38.row_sums_ref = bf16[32,8,128]{2,1,0:T(8,128)(2,1)S(1)} all-to-all(bf16[32,8,128]{2,1,0:T(8,128)(2,1)S(1)} %shard_map.41), channel_id=1, replica_groups=mesh['z'=8,'y'=4,'x'=4,'core'=2] {'z','x'}, dimensions={0} | all-to-all | bytes 131072 | tf_op jit(solution)/shard_map/all_to_all | solution.py:259
  98.3 1.2 shard_map.42
  99.5 0.6 collective-permute-start.6
  100.1 10.0 %all_to_all.39.refs_4_.col_sums_ref = f32[8,16,128]{2,1,0:T(8,128)S(1)} all-to-all(f32[8,16,128]{2,1,0:T(8,128)S(1)} %shard_map.42), channel_id=1, replica_groups=mesh['z'=8,'y'=4,'x'=4,'core'=2] {'y','core'}, dimensions={0} | all-to-all | bytes 131072 | tf_op jit(solution)/shard_map/all_to_all | solution.py:252
  110.1 0.0 collective-permute-done.6.refs_3_
  110.1 3.6 %shard_map.43 = (f32[2048,1024]{1,0:T(8,128)S(1)}, bf16[1024,384]{1,0:T(8,128)(2,1)S(1)}, bf16[32,16,128]{2,1,0:T(8,128)(2,1)S(1)}) custom-call(bf16[128,384]{1,0:T(8,128)(2,1)S(1)} %get-tuple-element.49.refs_0_, bf16[128,384]{1,0:T(8,128)(2,1)S(1)} %collective-permute-done.4.refs_1_, bf16[256,384]{1,0:T(8,128)(2,1)S(1)} %collective-permute-done.5.refs_2_, ...), custom_call_target="tpu_custom_call" | custom-call | tf_op jit(solution)/shard_map/pallas_call | solution.py:203
  113.7 12.8 %all_to_all.40.row_sums_ref = bf16[32,16,128]{2,1,0:T(8,128)(2,1)S(1)} all-to-all(bf16[32,16,128]{2,1,0:T(8,128)(2,1)S(1)} %get-tuple-element.66), channel_id=1, replica_groups=mesh['z'=8,'y'=4,'x'=4,'core'=2] {'z','x'}, dimensions={0} | all-to-all | bytes 262144 | tf_op jit(solution)/shard_map/all_to_all | solution.py:274
  126.5 1.3 shard_map.45
  127.8 2.3 %collective-permute-start.8 = (f32[256,384]{1,0:T(8,128)S(1)}, f32[256,384]{1,0:T(8,128)S(1)}, u32[]{:S(2)}, u32[]{:S(2)}) collective-permute-start(f32[256,384]{1,0:T(8,128)S(1)} %get-tuple-element.72), channel_id=1, source_target_pairs={{0,1},{1,0},{2,3},{3,2},{4,5},{5,4},{6,7},{7,6},{8,9},{9,8},{10,11... | collective-permute-start | bytes 1179656 | tf_op jit(solution)/shard_map/ppermute | solution.py:214
  130.1 0.1 collective-permute-start.10
  130.2 0.4 collective-permute-start.7
  130.6 0.1 collective-permute-start.12
  130.7 1.3 shard_map.44
  132.1 0.0 collective-permute-done.8
  132.1 1.0 collective-permute-start.9
  133.1 0.0 collective-permute-done.10
  133.2 0.6 collective-permute-start.11
  133.8 0.0 collective-permute-done.12
  133.9 2.2 %collective-permute-start.13 = (bf16[256,384]{1,0:T(8,128)(2,1)S(1)}, bf16[256,384]{1,0:T(8,128)(2,1)S(1)}, u32[]{:S(2)}, u32[]{:S(2)}) collective-permute-start(bf16[256,384]{1,0:T(8,128)(2,1)S(1)} %add_convert_fusion), channel_id=1, source_target_pairs={{0,24},{8,0},{16,8},{24,16},{1,25},{9,1},{17,9},{25,17},{2,26},{10... | collective-permute-start | bytes 589832 | tf_op jit(solution)/shard_map/ppermute | solution.py:214
  136.1 0.0 collective-permute-done.7
  136.1 3.8 %collective-permute-done.9 = bf16[256,384]{1,0:T(8,128)(2,1)S(1)} collective-permute-done((bf16[256,384]{1,0:T(8,128)(2,1)S(1)}, bf16[256,384]{1,0:T(8,128)(2,1)S(1)}, u32[]{:S(2)}, u32[]{:S(2)}) %collective-permute-start.9) | collective-permute-done | bytes 196640 | tf_op jit(solution)/shard_map/ppermute | solution.py:214
  139.8 4.9 %collective-permute-done.11 = bf16[256,384]{1,0:T(8,128)(2,1)S(1)} collective-permute-done((bf16[256,384]{1,0:T(8,128)(2,1)S(1)}, bf16[256,384]{1,0:T(8,128)(2,1)S(1)}, u32[]{:S(2)}, u32[]{:S(2)}) %collective-permute-start.11) | collective-permute-done | bytes 196640 | tf_op jit(solution)/shard_map/ppermute | solution.py:214
  144.8 0.0 collective-permute-done.13
  144.8 0.8 convert_add_fusion
  (5 shorter events, 0.2 us)
Async XLA Ops:
  0.0 5.2 %collective-permute-start = (bf16[256,384]{1,0:T(8,128)(2,1)}, bf16[256,384]{1,0:T(8,128)(2,1)S(1)}, u32[]{:S(2)}, u32[]{:S(2)}) collective-permute-start(bf16[256,384]{1,0:T(8,128)(2,1)} %param.5), channel_id=1, source_target_pairs={{0,1},{1,0},{2,3},{3,2},{4,5},{5,4},{6,7},{7,6},{8,9},{9,8},{10,11... | collective-permute-start | bytes 589832 | tf_op jit(solution)/shard_map/ppermute | solution.py:214
  6.2 30.2 %copy-start = (bf16[512,384]{1,0:T(8,128)(2,1)}, bf16[512,384]{1,0:T(8,128)(2,1)S(1)}, u32[]{:S(2)}) copy-start(bf16[512,384]{1,0:T(8,128)(2,1)S(1)} %pad_maximum_fusion.refs_0_) | copy-start | bytes 1179652
  6.2 30.1 %all-to-all-start = ((bf16[8,128,384]{2,1,0:T(8,128)(2,1)}), bf16[8,128,384]{2,1,0:T(8,128)(2,1)S(1)}, u32[]{:S(2)}, u32[]{:S(2)}) async-start(bf16[8,128,384]{2,1,0:T(8,128)(2,1)} %get-tuple-element.42), calls=%async_computation | async-start | bytes 1572864 | tf_op jit(solution)/shard_map/all_to_all | solution.py:232
  12.7 23.6 %collective-permute-start.3 = (bf16[512,384]{1,0:T(8,128)(2,1)S(1)}, bf16[512,384]{1,0:T(8,128)(2,1)S(1)}, u32[]{:S(2)}, u32[]{:S(2)}) collective-permute-start(bf16[512,384]{1,0:T(8,128)(2,1)S(1)} %pad_maximum_fusion.refs_0_), channel_id=1, source_target_pairs={{0,24},{8,0},{16,8},{24,16},{1,25},{9,1},{17,9},{25,17},{2,26},{10... | collective-permute-start | bytes 1179656 | tf_op jit(solution)/shard_map/ppermute | solution.py:214
  15.4 20.9 %collective-permute-start.2 = (bf16[512,384]{1,0:T(8,128)(2,1)S(1)}, bf16[512,384]{1,0:T(8,128)(2,1)S(1)}, u32[]{:S(2)}, u32[]{:S(2)}) collective-permute-start(bf16[512,384]{1,0:T(8,128)(2,1)S(1)} %pad_maximum_fusion.refs_0_), channel_id=1, source_target_pairs={{0,16},{8,24},{16,0},{24,8},{1,17},{9,25},{17,1},{25,9},{2,18},{10... | collective-permute-start | bytes 1179656 | tf_op jit(solution)/shard_map/ppermute | solution.py:214
  15.7 20.6 %collective-permute-start.1 = (bf16[512,384]{1,0:T(8,128)(2,1)S(1)}, bf16[512,384]{1,0:T(8,128)(2,1)S(1)}, u32[]{:S(2)}, u32[]{:S(2)}) collective-permute-start(bf16[512,384]{1,0:T(8,128)(2,1)S(1)} %pad_maximum_fusion.refs_0_), channel_id=1, source_target_pairs={{0,8},{8,16},{16,24},{24,0},{1,9},{9,17},{17,25},{25,1},{2,10},{10... | collective-permute-start | bytes 1179656 | tf_op jit(solution)/shard_map/ppermute | solution.py:214
  36.3 0.8 copy-start.1
  36.3 0.9 copy-start.2
  37.2 0.7 copy-start.3
  43.2 12.6 %collective-permute-start.4 = (bf16[128,384]{1,0:T(8,128)(2,1)S(1)}, bf16[128,384]{1,0:T(8,128)(2,1)S(1)}, u32[]{:S(2)}, u32[]{:S(2)}) collective-permute-start(bf16[128,384]{1,0:T(8,128)(2,1)S(1)} %get-tuple-element.49.refs_0_), channel_id=1, source_target_pairs={{0,128},{32,160},{64,192},{96,224},{128,0},{160,32},{192,64},{224,... | collective-permute-start | bytes 294920 | tf_op jit(solution)/shard_map/ppermute | solution.py:251
  73.6 11.5 %collective-permute-start.5 = (bf16[256,384]{1,0:T(8,128)(2,1)S(1)}, bf16[256,384]{1,0:T(8,128)(2,1)S(1)}, u32[]{:S(2)}, u32[]{:S(2)}) collective-permute-start(bf16[256,384]{1,0:T(8,128)(2,1)S(1)} %pad_maximum_fusion.2), channel_id=1, source_target_pairs={{0,64},{32,96},{64,0},{96,32},{128,192},{160,224},{192,128},{224,1... | collective-permute-start | bytes 589832 | tf_op jit(solution)/shard_map/ppermute | solution.py:251
  99.5 10.6 %collective-permute-start.6 = (bf16[512,384]{1,0:T(8,128)(2,1)S(1)}, bf16[512,384]{1,0:T(8,128)(2,1)S(1)}, u32[]{:S(2)}, u32[]{:S(2)}) collective-permute-start(bf16[512,384]{1,0:T(8,128)(2,1)S(1)} %pad_maximum_fusion.1), channel_id=1, source_target_pairs={{0,32},{32,0},{64,96},{96,64},{128,160},{160,128},{192,224},{224,1... | collective-permute-start | bytes 1179656 | tf_op jit(solution)/shard_map/ppermute | solution.py:251
  127.8 4.3 %collective-permute-start.8 = (f32[256,384]{1,0:T(8,128)S(1)}, f32[256,384]{1,0:T(8,128)S(1)}, u32[]{:S(2)}, u32[]{:S(2)}) collective-permute-start(f32[256,384]{1,0:T(8,128)S(1)} %get-tuple-element.72), channel_id=1, source_target_pairs={{0,1},{1,0},{2,3},{3,2},{4,5},{5,4},{6,7},{7,6},{8,9},{9,8},{10,11... | collective-permute-start | bytes 1179656 | tf_op jit(solution)/shard_map/ppermute | solution.py:214
  130.1 3.0 %collective-permute-start.10 = (f32[256,384]{1,0:T(8,128)S(1)}, f32[256,384]{1,0:T(8,128)S(1)}, u32[]{:S(2)}, u32[]{:S(2)}) collective-permute-start(f32[256,384]{1,0:T(8,128)S(1)} %get-tuple-element.74), channel_id=1, source_target_pairs={{0,1},{1,0},{2,3},{3,2},{4,5},{5,4},{6,7},{7,6},{8,9},{9,8},{10,11... | collective-permute-start | bytes 1179656 | tf_op jit(solution)/shard_map/ppermute | solution.py:214
  130.2 5.9 %collective-permute-start.7 = (f32[256,384]{1,0:T(8,128)S(1)}, f32[256,384]{1,0:T(8,128)S(1)}, u32[]{:S(2)}, u32[]{:S(2)}) collective-permute-start(f32[256,384]{1,0:T(8,128)S(1)} %get-tuple-element.70), channel_id=1, source_target_pairs={{0,1},{1,0},{2,3},{3,2},{4,5},{5,4},{6,7},{7,6},{8,9},{9,8},{10,11... | collective-permute-start | bytes 1179656 | tf_op jit(solution)/shard_map/ppermute | solution.py:214
  130.6 3.2 %collective-permute-start.12 = (f32[256,384]{1,0:T(8,128)S(1)}, f32[256,384]{1,0:T(8,128)S(1)}, u32[]{:S(2)}, u32[]{:S(2)}) collective-permute-start(f32[256,384]{1,0:T(8,128)S(1)} %get-tuple-element.76), channel_id=1, source_target_pairs={{0,1},{1,0},{2,3},{3,2},{4,5},{5,4},{6,7},{7,6},{8,9},{9,8},{10,11... | collective-permute-start | bytes 1179656 | tf_op jit(solution)/shard_map/ppermute | solution.py:214
  132.1 7.7 %collective-permute-start.9 = (bf16[256,384]{1,0:T(8,128)(2,1)S(1)}, bf16[256,384]{1,0:T(8,128)(2,1)S(1)}, u32[]{:S(2)}, u32[]{:S(2)}) collective-permute-start(bf16[256,384]{1,0:T(8,128)(2,1)S(1)} %add_convert_fusion.2), channel_id=1, source_target_pairs={{0,16},{8,24},{16,0},{24,8},{1,17},{9,25},{17,1},{25,9},{2,18},{10... | collective-permute-start | bytes 589832 | tf_op jit(solution)/shard_map/ppermute | solution.py:214
  133.2 11.6 %collective-permute-start.11 = (bf16[256,384]{1,0:T(8,128)(2,1)S(1)}, bf16[256,384]{1,0:T(8,128)(2,1)S(1)}, u32[]{:S(2)}, u32[]{:S(2)}) collective-permute-start(bf16[256,384]{1,0:T(8,128)(2,1)S(1)} %add_convert_fusion.1), channel_id=1, source_target_pairs={{0,8},{8,16},{16,24},{24,0},{1,9},{9,17},{17,25},{25,1},{2,10},{10... | collective-permute-start | bytes 589832 | tf_op jit(solution)/shard_map/ppermute | solution.py:214
  133.9 10.9 %collective-permute-start.13 = (bf16[256,384]{1,0:T(8,128)(2,1)S(1)}, bf16[256,384]{1,0:T(8,128)(2,1)S(1)}, u32[]{:S(2)}, u32[]{:S(2)}) collective-permute-start(bf16[256,384]{1,0:T(8,128)(2,1)S(1)} %add_convert_fusion), channel_id=1, source_target_pairs={{0,24},{8,0},{16,8},{24,16},{1,25},{9,1},{17,9},{25,17},{2,26},{10... | collective-permute-start | bytes 589832 | tf_op jit(solution)/shard_map/ppermute | solution.py:214

commit v3 on v2

v3 whole, which is shorter than its diff:
```python
import functools
import math

import jax
import jax.numpy as jnp
from jax import lax
from jax.experimental import pallas as pl
from jax.experimental.pallas import tpu as pltpu
from jax.sharding import Mesh, PartitionSpec as P

K = 384
PROTO = 65536
TOKENS = 8192
ITERS = 3
TEMP_TEACHER = 0.07
TEMP_STUDENT = 0.1
LOG2E = math.log2(math.e)
SCALE = PROTO / (TEMP_STUDENT * math.sqrt(TOKENS))

NZ, NY, NX, NC = 8, 4, 4, 2
TOK_BLOCK = TOKENS // (NZ * NY)
TOK_HALF = TOK_BLOCK // NC
PRO_BLOCK = PROTO // (NZ * NY * NX * NC)
TOK = TOK_HALF * NZ
PRO = PRO_BLOCK * NY * NC
HALF = PRO // 2
LANES = 128
TROWS = TOK // LANES
PROWS = PRO // LANES
HROWS = HALF // LANES
TGROUP = NY * NC
PGROUP = NZ * NX

F32 = jnp.float32
BF16 = jnp.bfloat16
VMEM = pl.BlockSpec(memory_space=pltpu.VMEM)
PARAMS = pltpu.CompilerParams(vmem_limit_bytes=24 * 1024 * 1024)
CONTRACT_LAST = (((1,), (1,)), ((), ()))


def pinned(x):
    return pltpu.with_memory_space_constraint(x, pltpu.VMEM)


def unit(values):
    wide = values.astype(F32)
    return (wide * lax.rsqrt(jnp.sum(wide * wide, axis=1, keepdims=True) + 1e-06)).astype(BF16)


def norm_kernel(teach_hbm, stud_hbm, proto_hbm, teach_out, stud_out, proto_out, teach_buf, stud_buf, sems):
    half = pl.ds(pl.multiple_of(lax.axis_index("core") * TOK_HALF, TOK_HALF), TOK_HALF)
    copies = [
        pltpu.make_async_copy(teach_hbm.at[half, :], teach_buf, sems.at[0]),
        pltpu.make_async_copy(stud_hbm.at[half, :], stud_buf, sems.at[1]),
        pltpu.make_async_copy(proto_hbm, proto_out, sems.at[2]),
    ]
    for copy in copies:
        copy.start()
    copies[0].wait()
    teach = unit(teach_buf[...])
    for z in range(NZ):
        teach_out[z] = teach
    copies[1].wait()
    stud_out[...] = unit(stud_buf[...])
    copies[2].wait()


def to_rows(values):
    return jnp.sum(values.T, axis=0, keepdims=True)


def to_cols(row):
    return jnp.broadcast_to(row, (LANES, LANES)).T


def own_first(core, which):
    return core if which == 0 else 1 - core


def block_row(step):
    place = lax.rem(lax.axis_index("y") + (NY - step), NY)
    return pl.multiple_of(place * PRO_BLOCK, PRO_BLOCK)


def teacher_kernel(teach_ref, *refs):
    raw, (expo_ref, unit_ref, sums_ref) = refs[:NY], refs[NY:]
    teach = teach_ref[...].reshape(TOK, K)
    for step in range(NY):
        base = block_row(step)
        rows = pl.ds(base, PRO_BLOCK)
        proto = unit(raw[step][...])
        unit_ref[rows, :] = proto
        logits = lax.dot_general(proto, teach, CONTRACT_LAST, preferred_element_type=F32)
        expo = jnp.exp2(logits * (LOG2E / TEMP_TEACHER))
        expo_ref[rows, :] = expo
        total = sum(expo[:, j * LANES : (j + 1) * LANES] for j in range(TROWS))
        for k in range(PRO_BLOCK // LANES):
            sums_ref[pl.ds(base // LANES + k, 1), :] = to_rows(total[k * LANES : (k + 1) * LANES, :])


def second_teacher_kernel(teach_ref, *refs):
    raw, first_ref, (expo_ref, unit_ref, sums_ref, second_ref) = refs[:NY], refs[NY], refs[NY + 1 :]
    teacher_kernel(teach_ref, *raw, expo_ref, unit_ref, second_ref)
    core = lax.axis_index("core")
    for peer in range(TGROUP):
        for which, part_ref in enumerate((first_ref, second_ref)):
            base = pl.multiple_of(own_first(core, which) * HROWS, HROWS)
            sums_ref[peer, pl.ds(base, HROWS), :] = part_ref[...]


def col_sums(expo_refs, weights, sums_ref):
    core = lax.axis_index("core")
    for which, expo_ref in enumerate(expo_refs):
        base = own_first(core, which) * HROWS

        def group(i, carry):
            rows = pl.ds(pl.multiple_of(i * LANES, LANES), LANES)
            total = None
            for j in range(TROWS):
                term = expo_ref[rows, j * LANES : (j + 1) * LANES] * weights[j : j + 1, :]
                total = term if total is None else total + term
            sums_ref[0, pl.ds(base + i, 1), :] = to_rows(total)
            return carry

        lax.fori_loop(0, HROWS, group, 0, unroll=True)
    for peer in range(1, TGROUP):
        sums_ref[peer] = sums_ref[0]


def col_kernel(row_sums_ref, first_ref, second_ref, sums_ref):
    weights = 1.0 / jnp.sum(row_sums_ref[...].astype(F32), axis=0)
    col_sums((first_ref, second_ref), weights, sums_ref)


def row_sums(expo_refs, weights_ref):
    core = lax.axis_index("core")
    totals = (jnp.zeros((8, LANES), F32),) * TROWS
    for which, expo_ref in enumerate(expo_refs):
        base = own_first(core, which) * HROWS

        def group(i, totals):
            rows = pl.ds(pl.multiple_of(i * LANES, LANES), LANES)
            wide = to_cols(weights_ref[pl.ds(base + i, 1), :])
            out = []
            for j in range(TROWS):
                term = expo_ref[rows, j * LANES : (j + 1) * LANES] * wide
                out.append(totals[j] + jnp.sum(term.reshape(LANES // 8, 8, LANES), axis=0))
            return tuple(out)

        totals = lax.fori_loop(0, HROWS, group, totals, unroll=True)
    return jnp.concatenate([jnp.sum(t, axis=0, keepdims=True) for t in totals], axis=0)


def row_kernel(col_sums_ref, first_ref, second_ref, sums_ref, weights_ref):
    weights_ref[...] = 1.0 / jnp.sum(col_sums_ref[...], axis=0)
    sums = row_sums((first_ref, second_ref), weights_ref).astype(BF16)
    for peer in range(PGROUP):
        sums_ref[peer] = sums


def last_row_kernel(*refs):
    pieces, (col_sums_ref, *protos), expos, outs = refs[:4], refs[4:7], refs[7:9], refs[9:]
    *expzs, stud_out, sums_ref, weights_ref = outs
    place = lax.axis_index("z")
    offsets = [0]
    for piece, hop in zip(pieces, (0, 4, 2, 1)):
        hops = [o ^ hop for o in offsets]
        for i, hop_to in enumerate(hops):
            rows = pl.ds(pl.multiple_of((place ^ hop_to) * TOK_HALF, TOK_HALF), TOK_HALF)
            stud_out[rows, :] = piece[i * TOK_HALF : (i + 1) * TOK_HALF, :]
        if hop:
            offsets = offsets + hops
    stud = stud_out[...]
    weights_ref[...] = 1.0 / jnp.sum(col_sums_ref[...], axis=0)
    totals = [jnp.zeros((8, LANES), F32)] * TROWS
    for i in range(PRO // PRO_BLOCK):
        proto_ref, expz_ref = protos[i // NY], expzs[i // NY]
        rows = slice(i % NY * PRO_BLOCK, (i % NY + 1) * PRO_BLOCK)
        logits = lax.dot_general(
            proto_ref[rows, :], stud, CONTRACT_LAST, preferred_element_type=F32
        )
        expz = jnp.exp2(logits * (LOG2E / TEMP_STUDENT))
        expz_ref[rows, :] = expz
        for j in range(TROWS):
            part = expz[:, j * LANES : (j + 1) * LANES]
            totals[j] = totals[j] + jnp.sum(part.reshape(PRO_BLOCK // 8, 8, LANES), axis=0)
    stud_sums = [jnp.sum(t, axis=0, keepdims=True) for t in totals]
    sums = jnp.concatenate([row_sums(expos, weights_ref)] + stud_sums, axis=0).astype(BF16)
    for peer in range(PGROUP):
        sums_ref[peer] = sums


def grad_kernel(tasks, col_sums_ref, row_sums_ref, stud_ref, *refs):
    expos, expzs, outs, weights_ref = refs[:2], refs[2:4], refs[4:-1], refs[-1]
    core = lax.axis_index("core")
    weights_ref[...] = 1.0 / jnp.sum(col_sums_ref[...], axis=0)
    totals = jnp.sum(row_sums_ref[...].astype(F32), axis=0)
    target_scale = SCALE / totals[:TROWS]
    prob_scale = SCALE / totals[TROWS:]
    stud = stud_ref[...]
    for (which, step), out_ref in zip(tasks, outs):
        expo_ref, expz_ref = expos[which], expzs[which]
        base = own_first(core, which) * HROWS
        group = lax.rem(lax.axis_index("y") + step, NY) * (PRO_BLOCK // LANES)
        parts = []
        for k in range(PRO_BLOCK // LANES):
            wide = to_cols(weights_ref[pl.ds(base + group + k, 1), :])
            rows = pl.ds(pl.multiple_of((group + k) * LANES, LANES), LANES)
            cols = []
            for j in range(TROWS):
                lanes = slice(j * LANES, (j + 1) * LANES)
                target = (expo_ref[rows, lanes] * wide) * target_scale[j : j + 1, :]
                prob = expz_ref[rows, lanes] * prob_scale[j : j + 1, :]
                cols.append((prob - target).astype(BF16))
            parts.append(jnp.concatenate(cols, axis=1))
        grads = jnp.concatenate(parts, axis=0)
        out_ref[...] = jnp.dot(grads, stud, preferred_element_type=F32)


def call(kernel, out_shape, *args, scratch=(), specs=None):
    return pl.pallas_call(
        kernel,
        out_shape=out_shape,
        in_specs=specs or [VMEM] * len(args),
        out_specs=jax.tree.map(lambda _: VMEM, out_shape),
        scratch_shapes=scratch,
        compiler_params=PARAMS,
    )(*args)


def shift(x, axis, size, step):
    return lax.ppermute(x, axis, [(i, (i + step) % size) for i in range(size)])


def shards(teacher_feats, student_feats, prototypes):
    struct = jax.ShapeDtypeStruct
    near = [prototypes] + [shift(prototypes, "y", NY, step) for step in range(1, NY)]
    half = pltpu.VMEM((TOK_HALF, K), BF16)
    teach, stud, near[0] = call(
        norm_kernel,
        (
            struct((NZ, TOK_HALF, K), BF16),
            struct((TOK_HALF, K), BF16),
            struct((PRO_BLOCK, K), BF16),
        ),
        *[
            pltpu.with_memory_space_constraint(x, pltpu.HBM)
            for x in (teacher_feats, student_feats, prototypes)
        ],
        scratch=(half, half, pltpu.SemaphoreType.DMA((3,))),
        specs=[pl.BlockSpec(memory_space=pl.ANY)] * 3,
    )
    teach = lax.all_to_all(teach, "z", 0, 0, tiled=True)
    teach, stud = lax.optimization_barrier((teach, stud))
    far = [shift(proto, "core", NC, 1) for proto in near]

    col_shape = struct((TGROUP, PROWS, LANES), F32)
    row_shape = struct((PGROUP, TROWS, LANES), BF16)
    weights = pltpu.VMEM((PROWS, LANES), F32)

    square = pltpu.VMEM((HALF, TOK), F32)
    unit_shape = struct((HALF, K), BF16)
    half_sums = struct((HROWS, LANES), F32)
    near_expo, near, near_sums = call(
        teacher_kernel, (square, unit_shape, half_sums), teach, *near
    )
    far_expo, far, cols = call(
        second_teacher_kernel,
        (square, unit_shape, col_shape),
        teach,
        *far,
        near_sums,
        scratch=(pltpu.VMEM((HROWS, LANES), F32),),
    )
    pieces = [stud]
    held = stud
    for step, hop in enumerate((4, 2, 1)):
        if step:
            cols, held = lax.optimization_barrier((cols, held))
        got = lax.ppermute(held, "z", [(i, i ^ hop) for i in range(NZ)])
        cols = lax.all_to_all(cols, ("y", "core"), 0, 0, tiled=True)
        cols, got = lax.optimization_barrier((cols, got))
        pieces.append(got)
        if step + 1 < ITERS:
            rows = call(
                row_kernel, row_shape, cols, pinned(near_expo), pinned(far_expo), scratch=(weights,)
            )
            held = jnp.concatenate(pieces, axis=0)
            rows, held = lax.optimization_barrier((rows, held))
            rows = lax.all_to_all(rows, ("z", "x"), 0, 0, tiled=True)
            cols = call(col_kernel, col_shape, rows, pinned(near_expo), pinned(far_expo))
    near_expz, far_expz, stud, rows = call(
        last_row_kernel,
        (
            square,
            square,
            struct((TOK, K), BF16),
            struct((PGROUP, 2 * TROWS, LANES), BF16),
        ),
        *pieces,
        cols,
        near,
        far,
        pinned(near_expo),
        pinned(far_expo),
        scratch=(weights,),
    )
    rows = lax.all_to_all(rows, ("z", "x"), 0, 0, tiled=True)

    def grad(*tasks):
        return call(
            functools.partial(grad_kernel, tasks),
            (struct((PRO_BLOCK, K), F32),) * len(tasks),
            cols,
            rows,
            stud,
            *[pinned(x) for x in (near_expo, far_expo, near_expz, far_expz)],
            scratch=(weights,),
        )

    far = [shift(part, "core", NC, 1) for part in grad((1, 2), (1, 1), (1, 3), (1, 0))]
    parts = [near + part for near, part in zip(grad((0, 2), (0, 1), (0, 3), (0, 0)), far)]
    total = parts[3]
    for part, step in zip(parts, (2, 1, 3)):
        total = total + shift(part.astype(BF16), "y", NY, step).astype(F32)
    return total


def solution(mesh):
    grid = Mesh(mesh.devices.reshape(NZ, NY, NX, NC), ("z", "y", "x", "core"))
    tokens = P(("z", "y"), None)
    protos = P(("z", "y", "x", "core"), None)
    return jax.shard_map(
        shards, mesh=grid, in_specs=(tokens, tokens, protos), out_specs=protos, check_vma=False
    )
```

time: 146 us -> 137 us (0.938)
  waiting for transfers between devices: 29.6 us -> 19.9 us
  Pallas kernels: 18.2 us -> 13.1 us
  blocking collectives: 67.8 us -> 72.4 us
  starting transfers between devices: 26.3 us -> 30.6 us
  local copies, waits for them, and re-layouts: 1.6 us -> 0 us
    all_to_all x1, waiting for transfers between devices: 19.9 us -> 9.38 us  [shards(): teach = lax.all_to_all(teach, 'z', 0, 0, tiled=True)]
    ppermute x11 -> x14, starting transfers between devices: 13.8 us -> 20.1 us  [shift(): return lax.ppermute(x, axis, [(i, (i + step) % size) for i in range(size)])]
    pallas_call x9 -> x10, Pallas kernels: 18.2 us -> 13.1 us  [call(): pl.pallas_call(kernel, out_shape=out_shape, in_specs=specs or [VMEM] * le...]
    ppermute x3, starting transfers between devices: 6.08 us -> 1.45 us  [shards(): got = lax.ppermute(held, 'z', [(i, i ^ hop) for i in range(NZ)])]
    all_to_all x1, starting transfers between devices: 6.46 us -> 9.03 us  [shards(): teach = lax.all_to_all(teach, 'z', 0, 0, tiled=True)]
    all_to_all x3, blocking collectives: 40.1 us -> 42.5 us  [shards(): rows = lax.all_to_all(rows, ('z', 'x'), 0, 0, tiled=True)]
    all_to_all x3, blocking collectives: 27.6 us -> 29.8 us  [shards(): cols = lax.all_to_all(cols, ('y', 'core'), 0, 0, tiled=True)]
    unnamed x8 -> x0, local copies, waits for them, and re-layouts: 1.6 us -> none
  transfers between devices with their start and end apart: 15 -> 18, of which waited for: 4 -> 5; matrix products, arithmetic and copies ran while one was open for 0% -> 0% of each run, Pallas kernels for 2% -> 3%
where the time goes in v3:
time: 137 us
  blocking collectives  72.4 us (53%)
  starting transfers between devices  30.6 us (22%)
  waiting for transfers between devices  19.9 us (15%)
  Pallas kernels  13.1 us (10%)
    all_to_all x3, blocking collectives, shards(): rows = lax.all_to_all(rows, ('z', 'x'), 0, 0, tiled=True)  42.5 us
    all_to_all x3, blocking collectives, shards(): cols = lax.all_to_all(cols, ('y', 'core'), 0, 0, tiled=True)  29.8 us
    ppermute x14, starting transfers between devices, shift(): return lax.ppermute(x, axis, [(i, (i + step) % size) for i in range(size)])  20.1 us
    pallas_call x10, Pallas kernels, call(): pl.pallas_call(kernel, out_shape=out_shape, in_specs=specs or [VMEM] * le...  13.1 us
    ppermute x14, waiting for transfers between devices, shift(): return lax.ppermute(x, axis, [(i, (i + step) % size) for i in range(size)])  9.53 us
    all_to_all x1, waiting for transfers between devices, shards(): teach = lax.all_to_all(teach, 'z', 0, 0, tiled=True)  9.38 us
    all_to_all x1, starting transfers between devices, shards(): teach = lax.all_to_all(teach, 'z', 0, 0, tiled=True)  9.03 us
  transfers between devices with their start and end apart: 18, of which 5 were waited for; matrix products, arithmetic and copies ran while one was open for 0% of the time, Pallas kernels for 3%

profile of v3, /device:TPU:1, one launch (start us, length us, event | category | flops | bytes accessed | tf_op | source)
XLA Modules:
  0.0 137.1 jit_solution(15653982325741861448)
XLA Ops:
  0.0 2.1 %shard_map.37 = (bf16[8,128,384]{2,1,0:T(8,128)(2,1)}, bf16[128,384]{1,0:T(8,128)(2,1)S(1)}, bf16[256,384]{1,0:T(8,128)(2,1)S(1)}) custom-call(bf16[256,384]{1,0:T(8,128)(2,1)} %teach_hbm.1, bf16[256,384]{1,0:T(8,128)(2,1)} %stud_hbm.1, bf16[256,384]{1,0:T(8,128)(2,1)} %proto_hbm.1), custom_call_target="tpu_custom_call" | custom-call | tf_op jit(solution)/shard_map/pallas_call | solution.py:221
  2.1 9.0 %all-to-all-start = ((bf16[8,128,384]{2,1,0:T(8,128)(2,1)}), bf16[8,128,384]{2,1,0:T(8,128)(2,1)S(1)}, u32[]{:S(2)}, u32[]{:S(2)}) async-start(bf16[8,128,384]{2,1,0:T(8,128)(2,1)} %get-tuple-element.42), calls=%async_computation | async-start | bytes 1572864 | tf_op jit(solution)/shard_map/all_to_all | solution.py:253
  11.1 1.3 collective-permute-start.1
  12.4 1.5 %collective-permute-start.5 = (bf16[256,384]{1,0:T(8,128)(2,1)}, bf16[256,384]{1,0:T(8,128)(2,1)S(1)}, u32[]{:S(2)}, u32[]{:S(2)}) collective-permute-start(bf16[256,384]{1,0:T(8,128)(2,1)} %proto_hbm.1), channel_id=1, source_target_pairs={{0,24},{8,0},{16,8},{24,16},{1,25},{9,1},{17,9},{25,17},{2,26},{10... | collective-permute-start | bytes 589832 | tf_op jit(solution)/shard_map/ppermute | solution.py:232
  13.9 1.6 %collective-permute-start.3 = (bf16[256,384]{1,0:T(8,128)(2,1)}, bf16[256,384]{1,0:T(8,128)(2,1)S(1)}, u32[]{:S(2)}, u32[]{:S(2)}) collective-permute-start(bf16[256,384]{1,0:T(8,128)(2,1)} %proto_hbm.1), channel_id=1, source_target_pairs={{0,16},{8,24},{16,0},{24,8},{1,17},{9,25},{17,1},{25,9},{2,18},{10... | collective-permute-start | bytes 589832 | tf_op jit(solution)/shard_map/ppermute | solution.py:232
  15.5 1.8 %collective-permute-start = (bf16[256,384]{1,0:T(8,128)(2,1)S(1)}, bf16[256,384]{1,0:T(8,128)(2,1)S(1)}, u32[]{:S(2)}, u32[]{:S(2)}) collective-permute-start(bf16[256,384]{1,0:T(8,128)(2,1)S(1)} %get-tuple-element.45.refs_0_), channel_id=1, source_target_pairs={{0,1},{1,0},{2,3},{3,2},{4,5},{5,4},{6,7},{7,6},{8,9},{9,8},{10,11... | collective-permute-start | bytes 589832 | tf_op jit(solution)/shard_map/ppermute | solution.py:232
  17.3 0.8 collective-permute-done.1.refs_1_
  18.1 2.1 %collective-permute-start.2 = (bf16[256,384]{1,0:T(8,128)(2,1)S(1)}, bf16[256,384]{1,0:T(8,128)(2,1)S(1)}, u32[]{:S(2)}, u32[]{:S(2)}) collective-permute-start(bf16[256,384]{1,0:T(8,128)(2,1)S(1)} %collective-permute-done.1.refs_1_), channel_id=1, source_target_pairs={{0,1},{1,0},{2,3},{3,2},{4,5},{5,4},{6,7},{7,6},{8,9},{9,8},{10,11... | collective-permute-start | bytes 589832 | tf_op jit(solution)/shard_map/ppermute | solution.py:232
  20.2 0.0 collective-permute-done.5.refs_3_
  20.2 3.4 %collective-permute-start.6 = (bf16[256,384]{1,0:T(8,128)(2,1)S(1)}, bf16[256,384]{1,0:T(8,128)(2,1)S(1)}, u32[]{:S(2)}, u32[]{:S(2)}) collective-permute-start(bf16[256,384]{1,0:T(8,128)(2,1)S(1)} %collective-permute-done.5.refs_3_), channel_id=1, source_target_pairs={{0,1},{1,0},{2,3},{3,2},{4,5},{5,4},{6,7},{7,6},{8,9},{9,8},{10,11... | collective-permute-start | bytes 589832 | tf_op jit(solution)/shard_map/ppermute | solution.py:232
  23.6 0.0 collective-permute-done.3.refs_2_
  23.6 1.7 %collective-permute-start.4 = (bf16[256,384]{1,0:T(8,128)(2,1)S(1)}, bf16[256,384]{1,0:T(8,128)(2,1)S(1)}, u32[]{:S(2)}, u32[]{:S(2)}) collective-permute-start(bf16[256,384]{1,0:T(8,128)(2,1)S(1)} %collective-permute-done.3.refs_2_), channel_id=1, source_target_pairs={{0,1},{1,0},{2,3},{3,2},{4,5},{5,4},{6,7},{7,6},{8,9},{9,8},{10,11... | collective-permute-start | bytes 589832 | tf_op jit(solution)/shard_map/ppermute | solution.py:232
  25.3 9.4 %all-to-all-done.teach_ref = bf16[8,128,384]{2,1,0:T(8,128)(2,1)S(1)} async-done(((bf16[8,128,384]{2,1,0:T(8,128)(2,1)}), bf16[8,128,384]{2,1,0:T(8,128)(2,1)S(1)}, u32[]{:S(2)}, u32[]{:S(2)}) %all-to-all-start) | async-done | bytes 786464 | tf_op jit(solution)/shard_map/all_to_all | solution.py:253
  34.7 0.0 collective-permute-start.7
  34.7 1.4 %shard_map.38 = (f32[1024,1024]{1,0:T(8,128)S(1)}, bf16[1024,384]{1,0:T(8,128)(2,1)S(1)}, f32[8,128]{1,0:T(8,128)S(1)}) custom-call(bf16[8,128,384]{2,1,0:T(8,128)(2,1)S(1)} %all-to-all-done.teach_ref, bf16[256,384]{1,0:T(8,128)(2,1)S(1)} %get-tuple-element.45.refs_0_, bf16[256,384]{1,0:T(8,128)(2,1)S(1)} %collective-permute-done.1.refs_1_, ...), custom_call_target="tpu_custom_call" | custom-call | tf_op jit(solution)/shard_map/pallas_call | solution.py:221
  36.1 0.0 collective-permute-done.refs_0_
  36.1 0.0 collective-permute-done.2.refs_1_
  36.1 0.0 collective-permute-done.6.refs_3_
  36.1 0.0 collective-permute-done.4.refs_2_
  36.1 1.4 %shard_map.39 = (f32[1024,1024]{1,0:T(8,128)S(1)}, bf16[1024,384]{1,0:T(8,128)(2,1)S(1)}, f32[8,16,128]{2,1,0:T(8,128)S(1)}) custom-call(bf16[8,128,384]{2,1,0:T(8,128)(2,1)S(1)} %all-to-all-done.teach_ref, bf16[256,384]{1,0:T(8,128)(2,1)S(1)} %collective-permute-done.refs_0_, bf16[256,384]{1,0:T(8,128)(2,1)S(1)} %collective-permute-done.2.refs_1_, ...), custom_call_target="tpu_custom_call" | custom-call | tf_op jit(solution)/shard_map/pallas_call | solution.py:221
  37.6 10.2 %all_to_all.35.col_sums_ref = f32[8,16,128]{2,1,0:T(8,128)S(1)} all-to-all(f32[8,16,128]{2,1,0:T(8,128)S(1)} %get-tuple-element.47), channel_id=1, replica_groups=mesh['z'=8,'y'=4,'x'=4,'core'=2] {'y','core'}, dimensions={0} | all-to-all | bytes 131072 | tf_op jit(solution)/shard_map/all_to_all | solution.py:281
  47.8 0.0 collective-permute-done.7.refs_1_
  47.8 0.6 shard_map.40
  48.4 17.8 %all_to_all.36.row_sums_ref = bf16[32,8,128]{2,1,0:T(8,128)(2,1)S(1)} all-to-all(bf16[32,8,128]{2,1,0:T(8,128)(2,1)S(1)} %shard_map.40), channel_id=1, replica_groups=mesh['z'=8,'y'=4,'x'=4,'core'=2] {'z','x'}, dimensions={0} | all-to-all | bytes 131072 | tf_op jit(solution)/shard_map/all_to_all | solution.py:290
  66.3 0.7 shard_map.41
  66.9 0.8 collective-permute-start.8
  67.7 9.7 %all_to_all.37.col_sums_ref = f32[8,16,128]{2,1,0:T(8,128)S(1)} all-to-all(f32[8,16,128]{2,1,0:T(8,128)S(1)} %shard_map.41), channel_id=1, replica_groups=mesh['z'=8,'y'=4,'x'=4,'core'=2] {'y','core'}, dimensions={0} | all-to-all | bytes 131072 | tf_op jit(solution)/shard_map/all_to_all | solution.py:281
  77.4 1.0 collective-permute-done.8.refs_2_
  78.4 0.6 shard_map.42
  79.1 11.9 %all_to_all.38.row_sums_ref = bf16[32,8,128]{2,1,0:T(8,128)(2,1)S(1)} all-to-all(bf16[32,8,128]{2,1,0:T(8,128)(2,1)S(1)} %shard_map.42), channel_id=1, replica_groups=mesh['z'=8,'y'=4,'x'=4,'core'=2] {'z','x'}, dimensions={0} | all-to-all | bytes 131072 | tf_op jit(solution)/shard_map/all_to_all | solution.py:290
  91.1 0.7 shard_map.43
  91.7 0.6 collective-permute-start.9
  92.4 10.0 %all_to_all.39.refs_4_.col_sums_ref = f32[8,16,128]{2,1,0:T(8,128)S(1)} all-to-all(f32[8,16,128]{2,1,0:T(8,128)S(1)} %shard_map.43), channel_id=1, replica_groups=mesh['z'=8,'y'=4,'x'=4,'core'=2] {'y','core'}, dimensions={0} | all-to-all | bytes 131072 | tf_op jit(solution)/shard_map/all_to_all | solution.py:281
  102.3 0.0 collective-permute-done.9.refs_3_
  102.3 2.8 %shard_map.44 = (f32[1024,1024]{1,0:T(8,128)S(1)}, f32[1024,1024]{1,0:T(8,128)S(1)}, bf16[1024,384]{1,0:T(8,128)(2,1)S(1)}, bf16[32,16,128]{2,1,0:T(8,128)(2,1)S(1)}) custom-call(bf16[128,384]{1,0:T(8,128)(2,1)S(1)} %get-tuple-element.48.refs_0_, bf16[128,384]{1,0:T(8,128)(2,1)S(1)} %collective-permute-done.7.refs_1_, ...), custom_call_target="tpu_custom_call" | custom-call | tf_op jit(solution)/shard_map/pallas_call | solution.py:221
  105.2 12.8 %all_to_all.40.row_sums_ref = bf16[32,16,128]{2,1,0:T(8,128)(2,1)S(1)} all-to-all(bf16[32,16,128]{2,1,0:T(8,128)(2,1)S(1)} %get-tuple-element.67), channel_id=1, replica_groups=mesh['z'=8,'y'=4,'x'=4,'core'=2] {'z','x'}, dimensions={0} | all-to-all | bytes 262144 | tf_op jit(solution)/shard_map/all_to_all | solution.py:308
  117.9 1.3 shard_map.46
  119.3 2.3 %collective-permute-start.11 = (f32[256,384]{1,0:T(8,128)S(1)}, f32[256,384]{1,0:T(8,128)S(1)}, u32[]{:S(2)}, u32[]{:S(2)}) collective-permute-start(f32[256,384]{1,0:T(8,128)S(1)} %get-tuple-element.74), channel_id=1, source_target_pairs={{0,1},{1,0},{2,3},{3,2},{4,5},{5,4},{6,7},{7,6},{8,9},{9,8},{10,11... | collective-permute-start | bytes 1179656 | tf_op jit(solution)/shard_map/ppermute | solution.py:232
  121.6 0.1 collective-permute-start.13
  121.7 0.4 collective-permute-start.10
  122.1 0.1 collective-permute-start.15
  122.2 1.3 shard_map.45
  123.6 0.0 collective-permute-done.11
  123.6 1.0 collective-permute-start.12
  124.6 0.0 collective-permute-done.13
  124.7 0.6 collective-permute-start.14
  125.3 0.0 collective-permute-done.15
  125.3 2.2 %collective-permute-start.16 = (bf16[256,384]{1,0:T(8,128)(2,1)S(1)}, bf16[256,384]{1,0:T(8,128)(2,1)S(1)}, u32[]{:S(2)}, u32[]{:S(2)}) collective-permute-start(bf16[256,384]{1,0:T(8,128)(2,1)S(1)} %add_convert_fusion), channel_id=1, source_target_pairs={{0,24},{8,0},{16,8},{24,16},{1,25},{9,1},{17,9},{25,17},{2,26},{10... | collective-permute-start | bytes 589832 | tf_op jit(solution)/shard_map/ppermute | solution.py:232
  127.6 0.0 collective-permute-done.10
  127.6 3.8 %collective-permute-done.12 = bf16[256,384]{1,0:T(8,128)(2,1)S(1)} collective-permute-done((bf16[256,384]{1,0:T(8,128)(2,1)S(1)}, bf16[256,384]{1,0:T(8,128)(2,1)S(1)}, u32[]{:S(2)}, u32[]{:S(2)}) %collective-permute-start.12) | collective-permute-done | bytes 196640 | tf_op jit(solution)/shard_map/ppermute | solution.py:232
  131.3 4.9 %collective-permute-done.14 = bf16[256,384]{1,0:T(8,128)(2,1)S(1)} collective-permute-done((bf16[256,384]{1,0:T(8,128)(2,1)S(1)}, bf16[256,384]{1,0:T(8,128)(2,1)S(1)}, u32[]{:S(2)}, u32[]{:S(2)}) %collective-permute-start.14) | collective-permute-done | bytes 196640 | tf_op jit(solution)/shard_map/ppermute | solution.py:232
  136.2 0.0 collective-permute-done.16
  136.2 0.8 convert_add_fusion
  (5 shorter events, 0.2 us)
Async XLA Ops:
  2.1 32.6 %all-to-all-start = ((bf16[8,128,384]{2,1,0:T(8,128)(2,1)}), bf16[8,128,384]{2,1,0:T(8,128)(2,1)S(1)}, u32[]{:S(2)}, u32[]{:S(2)}) async-start(bf16[8,128,384]{2,1,0:T(8,128)(2,1)} %get-tuple-element.42), calls=%async_computation | async-start | bytes 1572864 | tf_op jit(solution)/shard_map/all_to_all | solution.py:253
  11.1 7.0 %collective-permute-start.1 = (bf16[256,384]{1,0:T(8,128)(2,1)}, bf16[256,384]{1,0:T(8,128)(2,1)S(1)}, u32[]{:S(2)}, u32[]{:S(2)}) collective-permute-start(bf16[256,384]{1,0:T(8,128)(2,1)} %proto_hbm.1), channel_id=1, source_target_pairs={{0,8},{8,16},{16,24},{24,0},{1,9},{9,17},{17,25},{25,1},{2,10},{10... | collective-permute-start | bytes 589832 | tf_op jit(solution)/shard_map/ppermute | solution.py:232
  12.4 7.8 %collective-permute-start.5 = (bf16[256,384]{1,0:T(8,128)(2,1)}, bf16[256,384]{1,0:T(8,128)(2,1)S(1)}, u32[]{:S(2)}, u32[]{:S(2)}) collective-permute-start(bf16[256,384]{1,0:T(8,128)(2,1)} %proto_hbm.1), channel_id=1, source_target_pairs={{0,24},{8,0},{16,8},{24,16},{1,25},{9,1},{17,9},{25,17},{2,26},{10... | collective-permute-start | bytes 589832 | tf_op jit(solution)/shard_map/ppermute | solution.py:232
  13.9 9.7 %collective-permute-start.3 = (bf16[256,384]{1,0:T(8,128)(2,1)}, bf16[256,384]{1,0:T(8,128)(2,1)S(1)}, u32[]{:S(2)}, u32[]{:S(2)}) collective-permute-start(bf16[256,384]{1,0:T(8,128)(2,1)} %proto_hbm.1), channel_id=1, source_target_pairs={{0,16},{8,24},{16,0},{24,8},{1,17},{9,25},{17,1},{25,9},{2,18},{10... | collective-permute-start | bytes 589832 | tf_op jit(solution)/shard_map/ppermute | solution.py:232
  15.5 20.6 %collective-permute-start = (bf16[256,384]{1,0:T(8,128)(2,1)S(1)}, bf16[256,384]{1,0:T(8,128)(2,1)S(1)}, u32[]{:S(2)}, u32[]{:S(2)}) collective-permute-start(bf16[256,384]{1,0:T(8,128)(2,1)S(1)} %get-tuple-element.45.refs_0_), channel_id=1, source_target_pairs={{0,1},{1,0},{2,3},{3,2},{4,5},{5,4},{6,7},{7,6},{8,9},{9,8},{10,11... | collective-permute-start | bytes 589832 | tf_op jit(solution)/shard_map/ppermute | solution.py:232
  18.1 18.0 %collective-permute-start.2 = (bf16[256,384]{1,0:T(8,128)(2,1)S(1)}, bf16[256,384]{1,0:T(8,128)(2,1)S(1)}, u32[]{:S(2)}, u32[]{:S(2)}) collective-permute-start(bf16[256,384]{1,0:T(8,128)(2,1)S(1)} %collective-permute-done.1.refs_1_), channel_id=1, source_target_pairs={{0,1},{1,0},{2,3},{3,2},{4,5},{5,4},{6,7},{7,6},{8,9},{9,8},{10,11... | collective-permute-start | bytes 589832 | tf_op jit(solution)/shard_map/ppermute | solution.py:232
  20.2 15.9 %collective-permute-start.6 = (bf16[256,384]{1,0:T(8,128)(2,1)S(1)}, bf16[256,384]{1,0:T(8,128)(2,1)S(1)}, u32[]{:S(2)}, u32[]{:S(2)}) collective-permute-start(bf16[256,384]{1,0:T(8,128)(2,1)S(1)} %collective-permute-done.5.refs_3_), channel_id=1, source_target_pairs={{0,1},{1,0},{2,3},{3,2},{4,5},{5,4},{6,7},{7,6},{8,9},{9,8},{10,11... | collective-permute-start | bytes 589832 | tf_op jit(solution)/shard_map/ppermute | solution.py:232
  23.6 12.5 %collective-permute-start.4 = (bf16[256,384]{1,0:T(8,128)(2,1)S(1)}, bf16[256,384]{1,0:T(8,128)(2,1)S(1)}, u32[]{:S(2)}, u32[]{:S(2)}) collective-permute-start(bf16[256,384]{1,0:T(8,128)(2,1)S(1)} %collective-permute-done.3.refs_2_), channel_id=1, source_target_pairs={{0,1},{1,0},{2,3},{3,2},{4,5},{5,4},{6,7},{7,6},{8,9},{9,8},{10,11... | collective-permute-start | bytes 589832 | tf_op jit(solution)/shard_map/ppermute | solution.py:232
  34.7 13.1 %collective-permute-start.7 = (bf16[128,384]{1,0:T(8,128)(2,1)S(1)}, bf16[128,384]{1,0:T(8,128)(2,1)S(1)}, u32[]{:S(2)}, u32[]{:S(2)}) collective-permute-start(bf16[128,384]{1,0:T(8,128)(2,1)S(1)} %get-tuple-element.48.refs_0_), channel_id=1, source_target_pairs={{0,128},{32,160},{64,192},{96,224},{128,0},{160,32},{192,64},{224,... | collective-permute-start | bytes 294920 | tf_op jit(solution)/shard_map/ppermute | solution.py:280
  66.9 11.5 %collective-permute-start.8 = (bf16[256,384]{1,0:T(8,128)(2,1)S(1)}, bf16[256,384]{1,0:T(8,128)(2,1)S(1)}, u32[]{:S(2)}, u32[]{:S(2)}) collective-permute-start(bf16[256,384]{1,0:T(8,128)(2,1)S(1)} %pad_maximum_fusion.1), channel_id=1, source_target_pairs={{0,64},{32,96},{64,0},{96,32},{128,192},{160,224},{192,128},{224,1... | collective-permute-start | bytes 589832 | tf_op jit(solution)/shard_map/ppermute | solution.py:280
  91.7 10.6 %collective-permute-start.9 = (bf16[512,384]{1,0:T(8,128)(2,1)S(1)}, bf16[512,384]{1,0:T(8,128)(2,1)S(1)}, u32[]{:S(2)}, u32[]{:S(2)}) collective-permute-start(bf16[512,384]{1,0:T(8,128)(2,1)S(1)} %pad_maximum_fusion), channel_id=1, source_target_pairs={{0,32},{32,0},{64,96},{96,64},{128,160},{160,128},{192,224},{224,1... | collective-permute-start | bytes 1179656 | tf_op jit(solution)/shard_map/ppermute | solution.py:280
  119.3 4.3 %collective-permute-start.11 = (f32[256,384]{1,0:T(8,128)S(1)}, f32[256,384]{1,0:T(8,128)S(1)}, u32[]{:S(2)}, u32[]{:S(2)}) collective-permute-start(f32[256,384]{1,0:T(8,128)S(1)} %get-tuple-element.74), channel_id=1, source_target_pairs={{0,1},{1,0},{2,3},{3,2},{4,5},{5,4},{6,7},{7,6},{8,9},{9,8},{10,11... | collective-permute-start | bytes 1179656 | tf_op jit(solution)/shard_map/ppermute | solution.py:232
  121.6 3.0 %collective-permute-start.13 = (f32[256,384]{1,0:T(8,128)S(1)}, f32[256,384]{1,0:T(8,128)S(1)}, u32[]{:S(2)}, u32[]{:S(2)}) collective-permute-start(f32[256,384]{1,0:T(8,128)S(1)} %get-tuple-element.76), channel_id=1, source_target_pairs={{0,1},{1,0},{2,3},{3,2},{4,5},{5,4},{6,7},{7,6},{8,9},{9,8},{10,11... | collective-permute-start | bytes 1179656 | tf_op jit(solution)/shard_map/ppermute | solution.py:232
  121.7 5.9 %collective-permute-start.10 = (f32[256,384]{1,0:T(8,128)S(1)}, f32[256,384]{1,0:T(8,128)S(1)}, u32[]{:S(2)}, u32[]{:S(2)}) collective-permute-start(f32[256,384]{1,0:T(8,128)S(1)} %get-tuple-element.72), channel_id=1, source_target_pairs={{0,1},{1,0},{2,3},{3,2},{4,5},{5,4},{6,7},{7,6},{8,9},{9,8},{10,11... | collective-permute-start | bytes 1179656 | tf_op jit(solution)/shard_map/ppermute | solution.py:232
  122.1 3.2 %collective-permute-start.15 = (f32[256,384]{1,0:T(8,128)S(1)}, f32[256,384]{1,0:T(8,128)S(1)}, u32[]{:S(2)}, u32[]{:S(2)}) collective-permute-start(f32[256,384]{1,0:T(8,128)S(1)} %get-tuple-element.78), channel_id=1, source_target_pairs={{0,1},{1,0},{2,3},{3,2},{4,5},{5,4},{6,7},{7,6},{8,9},{9,8},{10,11... | collective-permute-start | bytes 1179656 | tf_op jit(solution)/shard_map/ppermute | solution.py:232
  123.6 7.7 %collective-permute-start.12 = (bf16[256,384]{1,0:T(8,128)(2,1)S(1)}, bf16[256,384]{1,0:T(8,128)(2,1)S(1)}, u32[]{:S(2)}, u32[]{:S(2)}) collective-permute-start(bf16[256,384]{1,0:T(8,128)(2,1)S(1)} %add_convert_fusion.2), channel_id=1, source_target_pairs={{0,16},{8,24},{16,0},{24,8},{1,17},{9,25},{17,1},{25,9},{2,18},{10... | collective-permute-start | bytes 589832 | tf_op jit(solution)/shard_map/ppermute | solution.py:232
  124.7 11.6 %collective-permute-start.14 = (bf16[256,384]{1,0:T(8,128)(2,1)S(1)}, bf16[256,384]{1,0:T(8,128)(2,1)S(1)}, u32[]{:S(2)}, u32[]{:S(2)}) collective-permute-start(bf16[256,384]{1,0:T(8,128)(2,1)S(1)} %add_convert_fusion.1), channel_id=1, source_target_pairs={{0,8},{8,16},{16,24},{24,0},{1,9},{9,17},{17,25},{25,1},{2,10},{10... | collective-permute-start | bytes 589832 | tf_op jit(solution)/shard_map/ppermute | solution.py:232
  125.3 10.9 %collective-permute-start.16 = (bf16[256,384]{1,0:T(8,128)(2,1)S(1)}, bf16[256,384]{1,0:T(8,128)(2,1)S(1)}, u32[]{:S(2)}, u32[]{:S(2)}) collective-permute-start(bf16[256,384]{1,0:T(8,128)(2,1)S(1)} %add_convert_fusion), channel_id=1, source_target_pairs={{0,24},{8,0},{16,8},{24,16},{1,25},{9,1},{17,9},{25,17},{2,26},{10... | collective-permute-start | bytes 589832 | tf_op jit(solution)/shard_map/ppermute | solution.py:232

commit v4 on v3

--- a/solution.py
+++ b/solution.py
@@ -34,6 +34,7 @@
 F32 = jnp.float32
 BF16 = jnp.bfloat16
 VMEM = pl.BlockSpec(memory_space=pltpu.VMEM)
+ANY = pl.BlockSpec(memory_space=pl.ANY)
 PARAMS = pltpu.CompilerParams(vmem_limit_bytes=24 * 1024 * 1024)
 CONTRACT_LAST = (((1,), (1,)), ((), ()))
 
@@ -57,12 +58,15 @@
     for copy in copies:
         copy.start()
     copies[0].wait()
-    teach = unit(teach_buf[...])
-    for z in range(NZ):
-        teach_out[z] = teach
+    teach_buf[...] = unit(teach_buf[...])
+    spread = [pltpu.make_async_copy(teach_buf, teach_out.at[z], sems.at[3 + z]) for z in range(NZ)]
+    for copy in spread:
+        copy.start()
     copies[1].wait()
     stud_out[...] = unit(stud_buf[...])
     copies[2].wait()
+    for copy in spread:
+        copy.wait()
 
 
 def to_rows(values):
@@ -217,12 +221,12 @@
         out_ref[...] = jnp.dot(grads, stud, preferred_element_type=F32)
 
 
-def call(kernel, out_shape, *args, scratch=(), specs=None):
+def call(kernel, out_shape, *args, scratch=(), specs=None, out_specs=None):
     return pl.pallas_call(
         kernel,
         out_shape=out_shape,
         in_specs=specs or [VMEM] * len(args),
-        out_specs=jax.tree.map(lambda _: VMEM, out_shape),
+        out_specs=out_specs or jax.tree.map(lambda _: VMEM, out_shape),
         scratch_shapes=scratch,
         compiler_params=PARAMS,
     )(*args)
@@ -247,8 +251,9 @@
             pltpu.with_memory_space_constraint(x, pltpu.HBM)
             for x in (teacher_feats, student_feats, prototypes)
         ],
-        scratch=(half, half, pltpu.SemaphoreType.DMA((3,))),
-        specs=[pl.BlockSpec(memory_space=pl.ANY)] * 3,
+        scratch=(half, half, pltpu.SemaphoreType.DMA((3 + NZ,))),
+        specs=[ANY] * 3,
+        out_specs=(ANY, VMEM, VMEM),
     )
     teach = lax.all_to_all(teach, "z", 0, 0, tiled=True)
     teach, stud = lax.optimization_barrier((teach, stud))
@@ -279,7 +284,6 @@
             cols, held = lax.optimization_barrier((cols, held))
         got = lax.ppermute(held, "z", [(i, i ^ hop) for i in range(NZ)])
         cols = lax.all_to_all(cols, ("y", "core"), 0, 0, tiled=True)
-        cols, got = lax.optimization_barrier((cols, got))
         pieces.append(got)
         if step + 1 < ITERS:
             rows = call(
@@ -307,22 +311,32 @@
     )
     rows = lax.all_to_all(rows, ("z", "x"), 0, 0, tiled=True)
 
-    def grad(*tasks):
+    def grad(*tasks, after=()):
+        sums, _ = lax.optimization_barrier((rows, after))
         return call(
             functools.partial(grad_kernel, tasks),
             (struct((PRO_BLOCK, K), F32),) * len(tasks),
             cols,
-            rows,
+            sums,
             stud,
             *[pinned(x) for x in (near_expo, far_expo, near_expz, far_expz)],
             scratch=(weights,),
         )
 
-    far = [shift(part, "core", NC, 1) for part in grad((1, 2), (1, 1), (1, 3), (1, 0))]
-    parts = [near + part for near, part in zip(grad((0, 2), (0, 1), (0, 3), (0, 0)), far)]
-    total = parts[3]
+    def swap(part):
+        return shift(part, "core", NC, 1)
+
+    def merge(near, far):
+        return (near + swap(far)).astype(BF16)
+
+    (far2,) = grad((1, 2))
+    near2, far1, far3 = grad((0, 2), (1, 1), (1, 3), after=far2)
+    parts = [merge(near2, far2)]
+    near1, near3, near0, far0 = grad((0, 1), (0, 3), (0, 0), (1, 0), after=parts)
+    parts += [merge(near1, far1), merge(near3, far3)]
+    total = near0 + swap(far0)
     for part, step in zip(parts, (2, 1, 3)):
-        total = total + shift(part.astype(BF16), "y", NY, step).astype(F32)
+        total = total + shift(part, "y", NY, step).astype(F32)
     return total
 
 

time: 137 us -> 136 us (level)
  waiting for transfers between devices: 19.9 us -> 17.4 us
    ppermute x14, waiting for transfers between devices: 9.53 us -> 7.69 us  [shift(): return lax.ppermute(x, axis, [(i, (i + step) % size) for i in range(size)])]
    pallas_call x10 -> x11, Pallas kernels: 13.1 us -> 13.2 us  [call(): pl.pallas_call(kernel, out_shape=out_shape, in_specs=specs or [VMEM] * le...]
  transfers between devices with their start and end apart: 18 -> 18, of which waited for: 5 -> 5; matrix products, arithmetic and copies ran while one was open for 0% -> 0% of each run, Pallas kernels for 3% -> 5%
where the time goes in v4:
time: 136 us
  blocking collectives  72.8 us (54%)
  starting transfers between devices  31.3 us (23%)
  waiting for transfers between devices  17.4 us (13%)
  Pallas kernels  13.2 us (10%)
    all_to_all x3, blocking collectives, shards(): rows = lax.all_to_all(rows, ('z', 'x'), 0, 0, tiled=True)  43.3 us
    all_to_all x3, blocking collectives, shards(): cols = lax.all_to_all(cols, ('y', 'core'), 0, 0, tiled=True)  29.5 us
    ppermute x14, starting transfers between devices, shift(): return lax.ppermute(x, axis, [(i, (i + step) % size) for i in range(size)])  20.8 us
    pallas_call x11, Pallas kernels, call(): pl.pallas_call(kernel, out_shape=out_shape, in_specs=specs or [VMEM] * le...  13.2 us
    all_to_all x1, waiting for transfers between devices, shards(): teach = lax.all_to_all(teach, 'z', 0, 0, tiled=True)  9.38 us
    all_to_all x1, starting transfers between devices, shards(): teach = lax.all_to_all(teach, 'z', 0, 0, tiled=True)  9.03 us
    ppermute x14, waiting for transfers between devices, shift(): return lax.ppermute(x, axis, [(i, (i + step) % size) for i in range(size)])  7.69 us
  transfers between devices with their start and end apart: 18, of which 5 were waited for; matrix products, arithmetic and copies ran while one was open for 0% of the time, Pallas kernels for 5%

profile of v4, /device:TPU:1, one launch (start us, length us, event | category | flops | bytes accessed | tf_op | source)
XLA Modules:
  0.0 135.9 jit_solution(18308481333538346916)
XLA Ops:
  0.0 2.0 %shard_map.37 = (bf16[8,128,384]{2,1,0:T(8,128)(2,1)}, bf16[128,384]{1,0:T(8,128)(2,1)S(1)}, bf16[256,384]{1,0:T(8,128)(2,1)S(1)}) custom-call(bf16[256,384]{1,0:T(8,128)(2,1)} %teach_hbm.1, bf16[256,384]{1,0:T(8,128)(2,1)} %stud_hbm.1, bf16[256,384]{1,0:T(8,128)(2,1)} %proto_hbm.1), custom_call_target="tpu_custom_call" | custom-call | tf_op jit(solution)/shard_map/pallas_call | solution.py:225
  2.0 9.0 %all-to-all-start = ((bf16[8,128,384]{2,1,0:T(8,128)(2,1)}), bf16[8,128,384]{2,1,0:T(8,128)(2,1)S(1)}, u32[]{:S(2)}, u32[]{:S(2)}) async-start(bf16[8,128,384]{2,1,0:T(8,128)(2,1)} %get-tuple-element.37), calls=%async_computation | async-start | bytes 1572864 | tf_op jit(solution)/shard_map/all_to_all | solution.py:258
  11.0 1.3 collective-permute-start.1
  12.3 1.5 %collective-permute-start.5 = (bf16[256,384]{1,0:T(8,128)(2,1)}, bf16[256,384]{1,0:T(8,128)(2,1)S(1)}, u32[]{:S(2)}, u32[]{:S(2)}) collective-permute-start(bf16[256,384]{1,0:T(8,128)(2,1)} %proto_hbm.1), channel_id=1, source_target_pairs={{0,24},{8,0},{16,8},{24,16},{1,25},{9,1},{17,9},{25,17},{2,26},{10... | collective-permute-start | bytes 589832 | tf_op jit(solution)/shard_map/ppermute | solution.py:236
  13.8 1.6 %collective-permute-start.3 = (bf16[256,384]{1,0:T(8,128)(2,1)}, bf16[256,384]{1,0:T(8,128)(2,1)S(1)}, u32[]{:S(2)}, u32[]{:S(2)}) collective-permute-start(bf16[256,384]{1,0:T(8,128)(2,1)} %proto_hbm.1), channel_id=1, source_target_pairs={{0,16},{8,24},{16,0},{24,8},{1,17},{9,25},{17,1},{25,9},{2,18},{10... | collective-permute-start | bytes 589832 | tf_op jit(solution)/shard_map/ppermute | solution.py:236
  15.4 1.8 %collective-permute-start = (bf16[256,384]{1,0:T(8,128)(2,1)S(1)}, bf16[256,384]{1,0:T(8,128)(2,1)S(1)}, u32[]{:S(2)}, u32[]{:S(2)}) collective-permute-start(bf16[256,384]{1,0:T(8,128)(2,1)S(1)} %get-tuple-element.40.refs_0_), channel_id=1, source_target_pairs={{0,1},{1,0},{2,3},{3,2},{4,5},{5,4},{6,7},{7,6},{8,9},{9,8},{10,11... | collective-permute-start | bytes 589832 | tf_op jit(solution)/shard_map/ppermute | solution.py:236
  17.2 0.8 collective-permute-done.1.refs_1_
  18.0 2.1 %collective-permute-start.2 = (bf16[256,384]{1,0:T(8,128)(2,1)S(1)}, bf16[256,384]{1,0:T(8,128)(2,1)S(1)}, u32[]{:S(2)}, u32[]{:S(2)}) collective-permute-start(bf16[256,384]{1,0:T(8,128)(2,1)S(1)} %collective-permute-done.1.refs_1_), channel_id=1, source_target_pairs={{0,1},{1,0},{2,3},{3,2},{4,5},{5,4},{6,7},{7,6},{8,9},{9,8},{10,11... | collective-permute-start | bytes 589832 | tf_op jit(solution)/shard_map/ppermute | solution.py:236
  20.1 0.0 collective-permute-done.5.refs_3_
  20.1 3.4 %collective-permute-start.6 = (bf16[256,384]{1,0:T(8,128)(2,1)S(1)}, bf16[256,384]{1,0:T(8,128)(2,1)S(1)}, u32[]{:S(2)}, u32[]{:S(2)}) collective-permute-start(bf16[256,384]{1,0:T(8,128)(2,1)S(1)} %collective-permute-done.5.refs_3_), channel_id=1, source_target_pairs={{0,1},{1,0},{2,3},{3,2},{4,5},{5,4},{6,7},{7,6},{8,9},{9,8},{10,11... | collective-permute-start | bytes 589832 | tf_op jit(solution)/shard_map/ppermute | solution.py:236
  23.5 0.0 collective-permute-done.3.refs_2_
  23.5 1.7 %collective-permute-start.4 = (bf16[256,384]{1,0:T(8,128)(2,1)S(1)}, bf16[256,384]{1,0:T(8,128)(2,1)S(1)}, u32[]{:S(2)}, u32[]{:S(2)}) collective-permute-start(bf16[256,384]{1,0:T(8,128)(2,1)S(1)} %collective-permute-done.3.refs_2_), channel_id=1, source_target_pairs={{0,1},{1,0},{2,3},{3,2},{4,5},{5,4},{6,7},{7,6},{8,9},{9,8},{10,11... | collective-permute-start | bytes 589832 | tf_op jit(solution)/shard_map/ppermute | solution.py:236
  25.2 9.4 %all-to-all-done.teach_ref = bf16[8,128,384]{2,1,0:T(8,128)(2,1)S(1)} async-done(((bf16[8,128,384]{2,1,0:T(8,128)(2,1)}), bf16[8,128,384]{2,1,0:T(8,128)(2,1)S(1)}, u32[]{:S(2)}, u32[]{:S(2)}) %all-to-all-start) | async-done | bytes 786464 | tf_op jit(solution)/shard_map/all_to_all | solution.py:258
  34.6 0.0 collective-permute-start.7
  34.6 1.4 %shard_map.38 = (f32[1024,1024]{1,0:T(8,128)S(1)}, bf16[1024,384]{1,0:T(8,128)(2,1)S(1)}, f32[8,128]{1,0:T(8,128)S(1)}) custom-call(bf16[8,128,384]{2,1,0:T(8,128)(2,1)S(1)} %all-to-all-done.teach_ref, bf16[256,384]{1,0:T(8,128)(2,1)S(1)} %get-tuple-element.40.refs_0_, bf16[256,384]{1,0:T(8,128)(2,1)S(1)} %collective-permute-done.1.refs_1_, ...), custom_call_target="tpu_custom_call" | custom-call | tf_op jit(solution)/shard_map/pallas_call | solution.py:225
  36.0 0.0 collective-permute-done.refs_0_
  36.0 0.0 collective-permute-done.2.refs_1_
  36.0 0.0 collective-permute-done.6.refs_3_
  36.0 0.0 collective-permute-done.4.refs_2_
  36.1 1.4 %shard_map.39 = (f32[1024,1024]{1,0:T(8,128)S(1)}, bf16[1024,384]{1,0:T(8,128)(2,1)S(1)}, f32[8,16,128]{2,1,0:T(8,128)S(1)}) custom-call(bf16[8,128,384]{2,1,0:T(8,128)(2,1)S(1)} %all-to-all-done.teach_ref, bf16[256,384]{1,0:T(8,128)(2,1)S(1)} %collective-permute-done.refs_0_, bf16[256,384]{1,0:T(8,128)(2,1)S(1)} %collective-permute-done.2.refs_1_, ...), custom_call_target="tpu_custom_call" | custom-call | tf_op jit(solution)/shard_map/pallas_call | solution.py:225
  37.5 10.2 %all_to_all.35.col_sums_ref = f32[8,16,128]{2,1,0:T(8,128)S(1)} all-to-all(f32[8,16,128]{2,1,0:T(8,128)S(1)} %get-tuple-element.42), channel_id=1, replica_groups=mesh['z'=8,'y'=4,'x'=4,'core'=2] {'y','core'}, dimensions={0} | all-to-all | bytes 131072 | tf_op jit(solution)/shard_map/all_to_all | solution.py:286
  47.7 0.6 shard_map.40
  48.3 0.0 collective-permute-done.7.refs_1_
  48.4 17.8 %all_to_all.36.row_sums_ref = bf16[32,8,128]{2,1,0:T(8,128)(2,1)S(1)} all-to-all(bf16[32,8,128]{2,1,0:T(8,128)(2,1)S(1)} %shard_map.40), channel_id=1, replica_groups=mesh['z'=8,'y'=4,'x'=4,'core'=2] {'z','x'}, dimensions={0} | all-to-all | bytes 131072 | tf_op jit(solution)/shard_map/all_to_all | solution.py:294
  66.2 0.7 shard_map.41
  66.9 0.8 collective-permute-start.8
  67.7 9.7 %all_to_all.37.col_sums_ref = f32[8,16,128]{2,1,0:T(8,128)S(1)} all-to-all(f32[8,16,128]{2,1,0:T(8,128)S(1)} %shard_map.41), channel_id=1, replica_groups=mesh['z'=8,'y'=4,'x'=4,'core'=2] {'y','core'}, dimensions={0} | all-to-all | bytes 131072 | tf_op jit(solution)/shard_map/all_to_all | solution.py:286
  77.4 0.6 shard_map.42
  78.0 0.3 collective-permute-done.8.refs_2_
  78.4 12.6 %all_to_all.38.row_sums_ref = bf16[32,8,128]{2,1,0:T(8,128)(2,1)S(1)} all-to-all(bf16[32,8,128]{2,1,0:T(8,128)(2,1)S(1)} %shard_map.42), channel_id=1, replica_groups=mesh['z'=8,'y'=4,'x'=4,'core'=2] {'z','x'}, dimensions={0} | all-to-all | bytes 131072 | tf_op jit(solution)/shard_map/all_to_all | solution.py:294
  91.0 0.7 shard_map.43
  91.6 0.7 collective-permute-start.9
  92.3 9.7 %all_to_all.39.refs_4_.col_sums_ref = f32[8,16,128]{2,1,0:T(8,128)S(1)} all-to-all(f32[8,16,128]{2,1,0:T(8,128)S(1)} %shard_map.43), channel_id=1, replica_groups=mesh['z'=8,'y'=4,'x'=4,'core'=2] {'y','core'}, dimensions={0} | all-to-all | bytes 131072 | tf_op jit(solution)/shard_map/all_to_all | solution.py:286
  102.0 0.0 collective-permute-done.9.refs_3_
  102.0 2.8 %shard_map.44 = (f32[1024,1024]{1,0:T(8,128)S(1)}, f32[1024,1024]{1,0:T(8,128)S(1)}, bf16[1024,384]{1,0:T(8,128)(2,1)S(1)}, bf16[32,16,128]{2,1,0:T(8,128)(2,1)S(1)}) custom-call(bf16[128,384]{1,0:T(8,128)(2,1)S(1)} %get-tuple-element.45.refs_0_, bf16[128,384]{1,0:T(8,128)(2,1)S(1)} %collective-permute-done.7.refs_1_, ...), custom_call_target="tpu_custom_call" | custom-call | tf_op jit(solution)/shard_map/pallas_call | solution.py:225
  104.8 12.8 %all_to_all.40.row_sums_ref = bf16[32,16,128]{2,1,0:T(8,128)(2,1)S(1)} all-to-all(bf16[32,16,128]{2,1,0:T(8,128)(2,1)S(1)} %get-tuple-element.56), channel_id=1, replica_groups=mesh['z'=8,'y'=4,'x'=4,'core'=2] {'z','x'}, dimensions={0} | all-to-all | bytes 262144 | tf_op jit(solution)/shard_map/all_to_all | solution.py:312
  117.6 0.5 shard_map.45
  118.1 2.5 %collective-permute-start.10 = (f32[256,384]{1,0:T(8,128)S(1)}, f32[256,384]{1,0:T(8,128)S(1)}, u32[]{:S(2)}, u32[]{:S(2)}) collective-permute-start(f32[256,384]{1,0:T(8,128)S(1)} %shard_map.45), channel_id=1, source_target_pairs={{0,1},{1,0},{2,3},{3,2},{4,5},{5,4},{6,7},{7,6},{8,9},{9,8},{10,11... | collective-permute-start | bytes 1179656 | tf_op jit(solution)/shard_map/ppermute | solution.py:236
  120.6 1.1 shard_map.46
  121.7 0.1 collective-permute-start.13
  121.8 0.5 collective-permute-start.15
  122.3 0.0 collective-permute-done.10
  122.4 1.1 collective-permute-start.12
  123.5 1.3 shard_map.47
  124.8 0.5 collective-permute-start.11
  125.3 0.0 collective-permute-done.13
  125.3 0.5 collective-permute-start.14
  125.8 0.0 collective-permute-done.15
  125.9 2.3 %collective-permute-start.16 = (bf16[256,384]{1,0:T(8,128)(2,1)S(1)}, bf16[256,384]{1,0:T(8,128)(2,1)S(1)}, u32[]{:S(2)}, u32[]{:S(2)}) collective-permute-start(bf16[256,384]{1,0:T(8,128)(2,1)S(1)} %add_convert_fusion), channel_id=1, source_target_pairs={{0,24},{8,0},{16,8},{24,16},{1,25},{9,1},{17,9},{25,17},{2,26},{10... | collective-permute-start | bytes 589832 | tf_op jit(solution)/shard_map/ppermute | solution.py:236
  128.2 2.2 %collective-permute-done.12 = bf16[256,384]{1,0:T(8,128)(2,1)S(1)} collective-permute-done((bf16[256,384]{1,0:T(8,128)(2,1)S(1)}, bf16[256,384]{1,0:T(8,128)(2,1)S(1)}, u32[]{:S(2)}, u32[]{:S(2)}) %collective-permute-start.12) | collective-permute-done | bytes 196640 | tf_op jit(solution)/shard_map/ppermute | solution.py:236
  130.4 4.6 %collective-permute-done.14 = bf16[256,384]{1,0:T(8,128)(2,1)S(1)} collective-permute-done((bf16[256,384]{1,0:T(8,128)(2,1)S(1)}, bf16[256,384]{1,0:T(8,128)(2,1)S(1)}, u32[]{:S(2)}, u32[]{:S(2)}) %collective-permute-start.14) | collective-permute-done | bytes 196640 | tf_op jit(solution)/shard_map/ppermute | solution.py:236
  135.0 0.0 collective-permute-done.16
  135.0 0.0 collective-permute-done.11
  135.0 0.8 convert_add_fusion
  (5 shorter events, 0.2 us)
Async XLA Ops:
  2.0 32.6 %all-to-all-start = ((bf16[8,128,384]{2,1,0:T(8,128)(2,1)}), bf16[8,128,384]{2,1,0:T(8,128)(2,1)S(1)}, u32[]{:S(2)}, u32[]{:S(2)}) async-start(bf16[8,128,384]{2,1,0:T(8,128)(2,1)} %get-tuple-element.37), calls=%async_computation | async-start | bytes 1572864 | tf_op jit(solution)/shard_map/all_to_all | solution.py:258
  11.0 7.0 %collective-permute-start.1 = (bf16[256,384]{1,0:T(8,128)(2,1)}, bf16[256,384]{1,0:T(8,128)(2,1)S(1)}, u32[]{:S(2)}, u32[]{:S(2)}) collective-permute-start(bf16[256,384]{1,0:T(8,128)(2,1)} %proto_hbm.1), channel_id=1, source_target_pairs={{0,8},{8,16},{16,24},{24,0},{1,9},{9,17},{17,25},{25,1},{2,10},{10... | collective-permute-start | bytes 589832 | tf_op jit(solution)/shard_map/ppermute | solution.py:236
  12.3 7.8 %collective-permute-start.5 = (bf16[256,384]{1,0:T(8,128)(2,1)}, bf16[256,384]{1,0:T(8,128)(2,1)S(1)}, u32[]{:S(2)}, u32[]{:S(2)}) collective-permute-start(bf16[256,384]{1,0:T(8,128)(2,1)} %proto_hbm.1), channel_id=1, source_target_pairs={{0,24},{8,0},{16,8},{24,16},{1,25},{9,1},{17,9},{25,17},{2,26},{10... | collective-permute-start | bytes 589832 | tf_op jit(solution)/shard_map/ppermute | solution.py:236
  13.8 9.7 %collective-permute-start.3 = (bf16[256,384]{1,0:T(8,128)(2,1)}, bf16[256,384]{1,0:T(8,128)(2,1)S(1)}, u32[]{:S(2)}, u32[]{:S(2)}) collective-permute-start(bf16[256,384]{1,0:T(8,128)(2,1)} %proto_hbm.1), channel_id=1, source_target_pairs={{0,16},{8,24},{16,0},{24,8},{1,17},{9,25},{17,1},{25,9},{2,18},{10... | collective-permute-start | bytes 589832 | tf_op jit(solution)/shard_map/ppermute | solution.py:236
  15.4 20.6 %collective-permute-start = (bf16[256,384]{1,0:T(8,128)(2,1)S(1)}, bf16[256,384]{1,0:T(8,128)(2,1)S(1)}, u32[]{:S(2)}, u32[]{:S(2)}) collective-permute-start(bf16[256,384]{1,0:T(8,128)(2,1)S(1)} %get-tuple-element.40.refs_0_), channel_id=1, source_target_pairs={{0,1},{1,0},{2,3},{3,2},{4,5},{5,4},{6,7},{7,6},{8,9},{9,8},{10,11... | collective-permute-start | bytes 589832 | tf_op jit(solution)/shard_map/ppermute | solution.py:236
  18.0 18.0 %collective-permute-start.2 = (bf16[256,384]{1,0:T(8,128)(2,1)S(1)}, bf16[256,384]{1,0:T(8,128)(2,1)S(1)}, u32[]{:S(2)}, u32[]{:S(2)}) collective-permute-start(bf16[256,384]{1,0:T(8,128)(2,1)S(1)} %collective-permute-done.1.refs_1_), channel_id=1, source_target_pairs={{0,1},{1,0},{2,3},{3,2},{4,5},{5,4},{6,7},{7,6},{8,9},{9,8},{10,11... | collective-permute-start | bytes 589832 | tf_op jit(solution)/shard_map/ppermute | solution.py:236
  20.1 15.9 %collective-permute-start.6 = (bf16[256,384]{1,0:T(8,128)(2,1)S(1)}, bf16[256,384]{1,0:T(8,128)(2,1)S(1)}, u32[]{:S(2)}, u32[]{:S(2)}) collective-permute-start(bf16[256,384]{1,0:T(8,128)(2,1)S(1)} %collective-permute-done.5.refs_3_), channel_id=1, source_target_pairs={{0,1},{1,0},{2,3},{3,2},{4,5},{5,4},{6,7},{7,6},{8,9},{9,8},{10,11... | collective-permute-start | bytes 589832 | tf_op jit(solution)/shard_map/ppermute | solution.py:236
  23.5 12.5 %collective-permute-start.4 = (bf16[256,384]{1,0:T(8,128)(2,1)S(1)}, bf16[256,384]{1,0:T(8,128)(2,1)S(1)}, u32[]{:S(2)}, u32[]{:S(2)}) collective-permute-start(bf16[256,384]{1,0:T(8,128)(2,1)S(1)} %collective-permute-done.3.refs_2_), channel_id=1, source_target_pairs={{0,1},{1,0},{2,3},{3,2},{4,5},{5,4},{6,7},{7,6},{8,9},{9,8},{10,11... | collective-permute-start | bytes 589832 | tf_op jit(solution)/shard_map/ppermute | solution.py:236
  34.6 13.7 %collective-permute-start.7 = (bf16[128,384]{1,0:T(8,128)(2,1)S(1)}, bf16[128,384]{1,0:T(8,128)(2,1)S(1)}, u32[]{:S(2)}, u32[]{:S(2)}) collective-permute-start(bf16[128,384]{1,0:T(8,128)(2,1)S(1)} %get-tuple-element.45.refs_0_), channel_id=1, source_target_pairs={{0,128},{32,160},{64,192},{96,224},{128,0},{160,32},{192,64},{224,... | collective-permute-start | bytes 294920 | tf_op jit(solution)/shard_map/ppermute | solution.py:285
  66.9 11.5 %collective-permute-start.8 = (bf16[256,384]{1,0:T(8,128)(2,1)S(1)}, bf16[256,384]{1,0:T(8,128)(2,1)S(1)}, u32[]{:S(2)}, u32[]{:S(2)}) collective-permute-start(bf16[256,384]{1,0:T(8,128)(2,1)S(1)} %pad_maximum_fusion.1), channel_id=1, source_target_pairs={{0,64},{32,96},{64,0},{96,32},{128,192},{160,224},{192,128},{224,1... | collective-permute-start | bytes 589832 | tf_op jit(solution)/shard_map/ppermute | solution.py:285
  91.6 10.3 %collective-permute-start.9 = (bf16[512,384]{1,0:T(8,128)(2,1)S(1)}, bf16[512,384]{1,0:T(8,128)(2,1)S(1)}, u32[]{:S(2)}, u32[]{:S(2)}) collective-permute-start(bf16[512,384]{1,0:T(8,128)(2,1)S(1)} %pad_maximum_fusion), channel_id=1, source_target_pairs={{0,32},{32,0},{64,96},{96,64},{128,160},{160,128},{192,224},{224,1... | collective-permute-start | bytes 1179656 | tf_op jit(solution)/shard_map/ppermute | solution.py:285
  118.1 4.2 %collective-permute-start.10 = (f32[256,384]{1,0:T(8,128)S(1)}, f32[256,384]{1,0:T(8,128)S(1)}, u32[]{:S(2)}, u32[]{:S(2)}) collective-permute-start(f32[256,384]{1,0:T(8,128)S(1)} %shard_map.45), channel_id=1, source_target_pairs={{0,1},{1,0},{2,3},{3,2},{4,5},{5,4},{6,7},{7,6},{8,9},{9,8},{10,11... | collective-permute-start | bytes 1179656 | tf_op jit(solution)/shard_map/ppermute | solution.py:236
  121.7 3.6 %collective-permute-start.13 = (f32[256,384]{1,0:T(8,128)S(1)}, f32[256,384]{1,0:T(8,128)S(1)}, u32[]{:S(2)}, u32[]{:S(2)}) collective-permute-start(f32[256,384]{1,0:T(8,128)S(1)} %get-tuple-element.66), channel_id=1, source_target_pairs={{0,1},{1,0},{2,3},{3,2},{4,5},{5,4},{6,7},{7,6},{8,9},{9,8},{10,11... | collective-permute-start | bytes 1179656 | tf_op jit(solution)/shard_map/ppermute | solution.py:236
  121.8 4.0 %collective-permute-start.15 = (f32[256,384]{1,0:T(8,128)S(1)}, f32[256,384]{1,0:T(8,128)S(1)}, u32[]{:S(2)}, u32[]{:S(2)}) collective-permute-start(f32[256,384]{1,0:T(8,128)S(1)} %get-tuple-element.68), channel_id=1, source_target_pairs={{0,1},{1,0},{2,3},{3,2},{4,5},{5,4},{6,7},{7,6},{8,9},{9,8},{10,11... | collective-permute-start | bytes 1179656 | tf_op jit(solution)/shard_map/ppermute | solution.py:236
  122.4 8.1 %collective-permute-start.12 = (bf16[256,384]{1,0:T(8,128)(2,1)S(1)}, bf16[256,384]{1,0:T(8,128)(2,1)S(1)}, u32[]{:S(2)}, u32[]{:S(2)}) collective-permute-start(bf16[256,384]{1,0:T(8,128)(2,1)S(1)} %add_convert_fusion.2), channel_id=1, source_target_pairs={{0,16},{8,24},{16,0},{24,8},{1,17},{9,25},{17,1},{25,9},{2,18},{10... | collective-permute-start | bytes 589832 | tf_op jit(solution)/shard_map/ppermute | solution.py:236
  124.8 10.2 %collective-permute-start.11 = (f32[256,384]{1,0:T(8,128)S(1)}, f32[256,384]{1,0:T(8,128)S(1)}, u32[]{:S(2)}, u32[]{:S(2)}) collective-permute-start(f32[256,384]{1,0:T(8,128)S(1)} %get-tuple-element.64), channel_id=1, source_target_pairs={{0,1},{1,0},{2,3},{3,2},{4,5},{5,4},{6,7},{7,6},{8,9},{9,8},{10,11... | collective-permute-start | bytes 1179656 | tf_op jit(solution)/shard_map/ppermute | solution.py:236
  125.3 9.7 %collective-permute-start.14 = (bf16[256,384]{1,0:T(8,128)(2,1)S(1)}, bf16[256,384]{1,0:T(8,128)(2,1)S(1)}, u32[]{:S(2)}, u32[]{:S(2)}) collective-permute-start(bf16[256,384]{1,0:T(8,128)(2,1)S(1)} %add_convert_fusion.1), channel_id=1, source_target_pairs={{0,8},{8,16},{16,24},{24,0},{1,9},{9,17},{17,25},{25,1},{2,10},{10... | collective-permute-start | bytes 589832 | tf_op jit(solution)/shard_map/ppermute | solution.py:236
  125.9 9.2 %collective-permute-start.16 = (bf16[256,384]{1,0:T(8,128)(2,1)S(1)}, bf16[256,384]{1,0:T(8,128)(2,1)S(1)}, u32[]{:S(2)}, u32[]{:S(2)}) collective-permute-start(bf16[256,384]{1,0:T(8,128)(2,1)S(1)} %add_convert_fusion), channel_id=1, source_target_pairs={{0,24},{8,0},{16,8},{24,16},{1,25},{9,1},{17,9},{25,17},{2,26},{10... | collective-permute-start | bytes 589832 | tf_op jit(solution)/shard_map/ppermute | solution.py:236

commit v5 on v4

--- a/solution.py
+++ b/solution.py
@@ -256,7 +256,7 @@
         out_specs=(ANY, VMEM, VMEM),
     )
     teach = lax.all_to_all(teach, "z", 0, 0, tiled=True)
-    teach, stud = lax.optimization_barrier((teach, stud))
+    got = lax.ppermute(stud, "z", [(i, i ^ 4) for i in range(NZ)])
     far = [shift(proto, "core", NC, 1) for proto in near]
 
     col_shape = struct((TGROUP, PROWS, LANES), F32)
@@ -277,13 +277,15 @@
         near_sums,
         scratch=(pltpu.VMEM((HROWS, LANES), F32),),
     )
+    cols, got = lax.optimization_barrier((cols, got))
     pieces = [stud]
-    held = stud
     for step, hop in enumerate((4, 2, 1)):
         if step:
             cols, held = lax.optimization_barrier((cols, held))
-        got = lax.ppermute(held, "z", [(i, i ^ hop) for i in range(NZ)])
+            got = lax.ppermute(held, "z", [(i, i ^ hop) for i in range(NZ)])
         cols = lax.all_to_all(cols, ("y", "core"), 0, 0, tiled=True)
+        if step == 0:
+            cols, got = lax.optimization_barrier((cols, got))
         pieces.append(got)
         if step + 1 < ITERS:
             rows = call(

time: 136 us -> 135 us (level)
  starting transfers between devices: 31.3 us -> 36.7 us
  waiting for transfers between devices: 17.4 us -> 13.3 us
  blocking collectives: 72.8 us -> 70.2 us
    all_to_all x1, waiting for transfers between devices: 9.38 us -> 4.01 us  [shards(): teach = lax.all_to_all(teach, 'z', 0, 0, tiled=True)]
    ppermute x0 -> x1, starting transfers between devices: none -> 5.37 us  [shards(): got = lax.ppermute(stud, 'z', [(i, i ^ 4) for i in range(NZ)])]
    all_to_all x3, blocking collectives: 43.3 us -> 41.2 us  [shards(): rows = lax.all_to_all(rows, ('z', 'x'), 0, 0, tiled=True)]
  transfers between devices with their start and end apart: 18 -> 18, of which waited for: 5 -> 6; matrix products, arithmetic and copies ran while one was open for 0% -> 0% of each run, Pallas kernels for 5% -> 4%
where the time goes in v5:
time: 135 us
  blocking collectives  70.2 us (52%)
  starting transfers between devices  36.7 us (27%)
  waiting for transfers between devices  13.3 us (10%)
  Pallas kernels  13.2 us (10%)
    all_to_all x3, blocking collectives, shards(): rows = lax.all_to_all(rows, ('z', 'x'), 0, 0, tiled=True)  41.2 us
    all_to_all x3, blocking collectives, shards(): cols = lax.all_to_all(cols, ('y', 'core'), 0, 0, tiled=True)  29 us
    ppermute x14, starting transfers between devices, shift(): return lax.ppermute(x, axis, [(i, (i + step) % size) for i in range(size)])  20.9 us
    pallas_call x11, Pallas kernels, call(): pl.pallas_call(kernel, out_shape=out_shape, in_specs=specs or [VMEM] * le...  13.2 us
    all_to_all x1, starting transfers between devices, shards(): teach = lax.all_to_all(teach, 'z', 0, 0, tiled=True)  9.03 us
    ppermute x14, waiting for transfers between devices, shift(): return lax.ppermute(x, axis, [(i, (i + step) % size) for i in range(size)])  7.69 us
    ppermute x1, starting transfers between devices, shards(): got = lax.ppermute(stud, 'z', [(i, i ^ 4) for i in range(NZ)])  5.37 us
    all_to_all x1, waiting for transfers between devices, shards(): teach = lax.all_to_all(teach, 'z', 0, 0, tiled=True)  4.01 us
  transfers between devices with their start and end apart: 18, of which 6 were waited for; matrix products, arithmetic and copies ran while one was open for 0% of the time, Pallas kernels for 4%

profile of v5, /device:TPU:1, one launch (start us, length us, event | category | flops | bytes accessed | tf_op | source)
XLA Modules:
  0.0 134.6 jit_solution(3093188019824207775)
XLA Ops:
  0.0 2.0 %shard_map.37 = (bf16[8,128,384]{2,1,0:T(8,128)(2,1)}, bf16[128,384]{1,0:T(8,128)(2,1)S(1)}, bf16[256,384]{1,0:T(8,128)(2,1)S(1)}) custom-call(bf16[256,384]{1,0:T(8,128)(2,1)} %teach_hbm.1, bf16[256,384]{1,0:T(8,128)(2,1)} %stud_hbm.1, bf16[256,384]{1,0:T(8,128)(2,1)} %proto_hbm.1), custom_call_target="tpu_custom_call" | custom-call | tf_op jit(solution)/shard_map/pallas_call | solution.py:225
  2.0 9.0 %all-to-all-start = ((bf16[8,128,384]{2,1,0:T(8,128)(2,1)}), bf16[8,128,384]{2,1,0:T(8,128)(2,1)S(1)}, u32[]{:S(2)}, u32[]{:S(2)}) async-start(bf16[8,128,384]{2,1,0:T(8,128)(2,1)} %get-tuple-element.39), calls=%async_computation | async-start | bytes 1572864 | tf_op jit(solution)/shard_map/all_to_all | solution.py:258
  11.0 1.3 collective-permute-start.1
  12.3 1.5 %collective-permute-start.5 = (bf16[256,384]{1,0:T(8,128)(2,1)}, bf16[256,384]{1,0:T(8,128)(2,1)S(1)}, u32[]{:S(2)}, u32[]{:S(2)}) collective-permute-start(bf16[256,384]{1,0:T(8,128)(2,1)} %proto_hbm.1), channel_id=1, source_target_pairs={{0,24},{8,0},{16,8},{24,16},{1,25},{9,1},{17,9},{25,17},{2,26},{10... | collective-permute-start | bytes 589832 | tf_op jit(solution)/shard_map/ppermute | solution.py:236
  13.8 1.6 %collective-permute-start.3 = (bf16[256,384]{1,0:T(8,128)(2,1)}, bf16[256,384]{1,0:T(8,128)(2,1)S(1)}, u32[]{:S(2)}, u32[]{:S(2)}) collective-permute-start(bf16[256,384]{1,0:T(8,128)(2,1)} %proto_hbm.1), channel_id=1, source_target_pairs={{0,16},{8,24},{16,0},{24,8},{1,17},{9,25},{17,1},{25,9},{2,18},{10... | collective-permute-start | bytes 589832 | tf_op jit(solution)/shard_map/ppermute | solution.py:236
  15.4 1.8 %collective-permute-start = (bf16[256,384]{1,0:T(8,128)(2,1)S(1)}, bf16[256,384]{1,0:T(8,128)(2,1)S(1)}, u32[]{:S(2)}, u32[]{:S(2)}) collective-permute-start(bf16[256,384]{1,0:T(8,128)(2,1)S(1)} %get-tuple-element.40.refs_0_), channel_id=1, source_target_pairs={{0,1},{1,0},{2,3},{3,2},{4,5},{5,4},{6,7},{7,6},{8,9},{9,8},{10,11... | collective-permute-start | bytes 589832 | tf_op jit(solution)/shard_map/ppermute | solution.py:236
  17.2 0.8 collective-permute-done.1.refs_1_
  18.0 2.1 %collective-permute-start.2 = (bf16[256,384]{1,0:T(8,128)(2,1)S(1)}, bf16[256,384]{1,0:T(8,128)(2,1)S(1)}, u32[]{:S(2)}, u32[]{:S(2)}) collective-permute-start(bf16[256,384]{1,0:T(8,128)(2,1)S(1)} %collective-permute-done.1.refs_1_), channel_id=1, source_target_pairs={{0,1},{1,0},{2,3},{3,2},{4,5},{5,4},{6,7},{7,6},{8,9},{9,8},{10,11... | collective-permute-start | bytes 589832 | tf_op jit(solution)/shard_map/ppermute | solution.py:236
  20.1 0.0 collective-permute-done.5.refs_3_
  20.1 3.4 %collective-permute-start.6 = (bf16[256,384]{1,0:T(8,128)(2,1)S(1)}, bf16[256,384]{1,0:T(8,128)(2,1)S(1)}, u32[]{:S(2)}, u32[]{:S(2)}) collective-permute-start(bf16[256,384]{1,0:T(8,128)(2,1)S(1)} %collective-permute-done.5.refs_3_), channel_id=1, source_target_pairs={{0,1},{1,0},{2,3},{3,2},{4,5},{5,4},{6,7},{7,6},{8,9},{9,8},{10,11... | collective-permute-start | bytes 589832 | tf_op jit(solution)/shard_map/ppermute | solution.py:236
  23.5 0.0 collective-permute-done.3.refs_2_
  23.5 1.7 %collective-permute-start.4 = (bf16[256,384]{1,0:T(8,128)(2,1)S(1)}, bf16[256,384]{1,0:T(8,128)(2,1)S(1)}, u32[]{:S(2)}, u32[]{:S(2)}) collective-permute-start(bf16[256,384]{1,0:T(8,128)(2,1)S(1)} %collective-permute-done.3.refs_2_), channel_id=1, source_target_pairs={{0,1},{1,0},{2,3},{3,2},{4,5},{5,4},{6,7},{7,6},{8,9},{9,8},{10,11... | collective-permute-start | bytes 589832 | tf_op jit(solution)/shard_map/ppermute | solution.py:236
  25.2 5.4 %collective-permute-start.7 = (bf16[128,384]{1,0:T(8,128)(2,1)S(1)}, bf16[128,384]{1,0:T(8,128)(2,1)S(1)}, u32[]{:S(2)}, u32[]{:S(2)}) collective-permute-start(bf16[128,384]{1,0:T(8,128)(2,1)S(1)} %get-tuple-element.43.refs_0_), channel_id=1, source_target_pairs={{0,128},{32,160},{64,192},{96,224},{128,0},{160,32},{192,64},{224,... | collective-permute-start | bytes 294920 | tf_op jit(solution)/shard_map/ppermute | solution.py:259
  30.6 4.0 %all-to-all-done.teach_ref = bf16[8,128,384]{2,1,0:T(8,128)(2,1)S(1)} async-done(((bf16[8,128,384]{2,1,0:T(8,128)(2,1)}), bf16[8,128,384]{2,1,0:T(8,128)(2,1)S(1)}, u32[]{:S(2)}, u32[]{:S(2)}) %all-to-all-start) | async-done | bytes 786464 | tf_op jit(solution)/shard_map/all_to_all | solution.py:258
  34.6 1.4 %shard_map.38 = (f32[1024,1024]{1,0:T(8,128)S(1)}, bf16[1024,384]{1,0:T(8,128)(2,1)S(1)}, f32[8,128]{1,0:T(8,128)S(1)}) custom-call(bf16[8,128,384]{2,1,0:T(8,128)(2,1)S(1)} %all-to-all-done.teach_ref, bf16[256,384]{1,0:T(8,128)(2,1)S(1)} %get-tuple-element.40.refs_0_, bf16[256,384]{1,0:T(8,128)(2,1)S(1)} %collective-permute-done.1.refs_1_, ...), custom_call_target="tpu_custom_call" | custom-call | tf_op jit(solution)/shard_map/pallas_call | solution.py:225
  36.0 0.0 collective-permute-done.refs_0_
  36.0 0.0 collective-permute-done.2.refs_1_
  36.0 0.0 collective-permute-done.6.refs_3_
  36.0 0.0 collective-permute-done.4.refs_2_
  36.0 1.4 %shard_map.39 = (f32[1024,1024]{1,0:T(8,128)S(1)}, bf16[1024,384]{1,0:T(8,128)(2,1)S(1)}, f32[8,16,128]{2,1,0:T(8,128)S(1)}) custom-call(bf16[8,128,384]{2,1,0:T(8,128)(2,1)S(1)} %all-to-all-done.teach_ref, bf16[256,384]{1,0:T(8,128)(2,1)S(1)} %collective-permute-done.refs_0_, bf16[256,384]{1,0:T(8,128)(2,1)S(1)} %collective-permute-done.2.refs_1_, ...), custom_call_target="tpu_custom_call" | custom-call | tf_op jit(solution)/shard_map/pallas_call | solution.py:225
  37.5 1.3 collective-permute-done.7.refs_1_
  38.8 9.6 %all_to_all.35.col_sums_ref = f32[8,16,128]{2,1,0:T(8,128)S(1)} all-to-all(f32[8,16,128]{2,1,0:T(8,128)S(1)} %get-tuple-element.44), channel_id=1, replica_groups=mesh['z'=8,'y'=4,'x'=4,'core'=2] {'y','core'}, dimensions={0} | all-to-all | bytes 131072 | tf_op jit(solution)/shard_map/all_to_all | solution.py:286
  48.4 0.6 shard_map.40
  49.1 15.8 %all_to_all.36.row_sums_ref = bf16[32,8,128]{2,1,0:T(8,128)(2,1)S(1)} all-to-all(bf16[32,8,128]{2,1,0:T(8,128)(2,1)S(1)} %shard_map.40), channel_id=1, replica_groups=mesh['z'=8,'y'=4,'x'=4,'core'=2] {'z','x'}, dimensions={0} | all-to-all | bytes 131072 | tf_op jit(solution)/shard_map/all_to_all | solution.py:296
  64.9 0.7 shard_map.41
  65.5 0.8 collective-permute-start.8
  66.3 9.7 %all_to_all.37.col_sums_ref = f32[8,16,128]{2,1,0:T(8,128)S(1)} all-to-all(f32[8,16,128]{2,1,0:T(8,128)S(1)} %shard_map.41), channel_id=1, replica_groups=mesh['z'=8,'y'=4,'x'=4,'core'=2] {'y','core'}, dimensions={0} | all-to-all | bytes 131072 | tf_op jit(solution)/shard_map/all_to_all | solution.py:286
  76.0 0.6 shard_map.42
  76.7 0.3 collective-permute-done.8.refs_2_
  77.1 12.6 %all_to_all.38.row_sums_ref = bf16[32,8,128]{2,1,0:T(8,128)(2,1)S(1)} all-to-all(bf16[32,8,128]{2,1,0:T(8,128)(2,1)S(1)} %shard_map.42), channel_id=1, replica_groups=mesh['z'=8,'y'=4,'x'=4,'core'=2] {'z','x'}, dimensions={0} | all-to-all | bytes 131072 | tf_op jit(solution)/shard_map/all_to_all | solution.py:296
  89.7 0.7 shard_map.43
  90.3 0.7 collective-permute-start.9
  91.0 9.7 %all_to_all.39.refs_4_.col_sums_ref = f32[8,16,128]{2,1,0:T(8,128)S(1)} all-to-all(f32[8,16,128]{2,1,0:T(8,128)S(1)} %shard_map.43), channel_id=1, replica_groups=mesh['z'=8,'y'=4,'x'=4,'core'=2] {'y','core'}, dimensions={0} | all-to-all | bytes 131072 | tf_op jit(solution)/shard_map/all_to_all | solution.py:286
  100.7 0.0 collective-permute-done.9.refs_3_
  100.7 2.8 %shard_map.44 = (f32[1024,1024]{1,0:T(8,128)S(1)}, f32[1024,1024]{1,0:T(8,128)S(1)}, bf16[1024,384]{1,0:T(8,128)(2,1)S(1)}, bf16[32,16,128]{2,1,0:T(8,128)(2,1)S(1)}) custom-call(bf16[128,384]{1,0:T(8,128)(2,1)S(1)} %get-tuple-element.43.refs_0_, bf16[128,384]{1,0:T(8,128)(2,1)S(1)} %collective-permute-done.7.refs_1_, ...), custom_call_target="tpu_custom_call" | custom-call | tf_op jit(solution)/shard_map/pallas_call | solution.py:225
  103.5 12.8 %all_to_all.40.row_sums_ref = bf16[32,16,128]{2,1,0:T(8,128)(2,1)S(1)} all-to-all(bf16[32,16,128]{2,1,0:T(8,128)(2,1)S(1)} %get-tuple-element.60), channel_id=1, replica_groups=mesh['z'=8,'y'=4,'x'=4,'core'=2] {'z','x'}, dimensions={0} | all-to-all | bytes 262144 | tf_op jit(solution)/shard_map/all_to_all | solution.py:314
  116.3 0.5 shard_map.45
  116.8 2.5 %collective-permute-start.10 = (f32[256,384]{1,0:T(8,128)S(1)}, f32[256,384]{1,0:T(8,128)S(1)}, u32[]{:S(2)}, u32[]{:S(2)}) collective-permute-start(f32[256,384]{1,0:T(8,128)S(1)} %shard_map.45), channel_id=1, source_target_pairs={{0,1},{1,0},{2,3},{3,2},{4,5},{5,4},{6,7},{7,6},{8,9},{9,8},{10,11... | collective-permute-start | bytes 1179656 | tf_op jit(solution)/shard_map/ppermute | solution.py:236
  119.3 1.1 shard_map.46
  120.4 0.1 collective-permute-start.13
  120.5 0.5 collective-permute-start.15
  121.0 0.0 collective-permute-done.10
  121.0 1.1 collective-permute-start.12
  122.1 1.3 shard_map.47
  123.5 0.5 collective-permute-start.11
  123.9 0.0 collective-permute-done.13
  124.0 0.5 collective-permute-start.14
  124.5 0.0 collective-permute-done.15
  124.5 2.3 %collective-permute-start.16 = (bf16[256,384]{1,0:T(8,128)(2,1)S(1)}, bf16[256,384]{1,0:T(8,128)(2,1)S(1)}, u32[]{:S(2)}, u32[]{:S(2)}) collective-permute-start(bf16[256,384]{1,0:T(8,128)(2,1)S(1)} %add_convert_fusion), channel_id=1, source_target_pairs={{0,24},{8,0},{16,8},{24,16},{1,25},{9,1},{17,9},{25,17},{2,26},{10... | collective-permute-start | bytes 589832 | tf_op jit(solution)/shard_map/ppermute | solution.py:236
  126.9 2.2 %collective-permute-done.12 = bf16[256,384]{1,0:T(8,128)(2,1)S(1)} collective-permute-done((bf16[256,384]{1,0:T(8,128)(2,1)S(1)}, bf16[256,384]{1,0:T(8,128)(2,1)S(1)}, u32[]{:S(2)}, u32[]{:S(2)}) %collective-permute-start.12) | collective-permute-done | bytes 196640 | tf_op jit(solution)/shard_map/ppermute | solution.py:236
  129.1 4.6 %collective-permute-done.14 = bf16[256,384]{1,0:T(8,128)(2,1)S(1)} collective-permute-done((bf16[256,384]{1,0:T(8,128)(2,1)S(1)}, bf16[256,384]{1,0:T(8,128)(2,1)S(1)}, u32[]{:S(2)}, u32[]{:S(2)}) %collective-permute-start.14) | collective-permute-done | bytes 196640 | tf_op jit(solution)/shard_map/ppermute | solution.py:236
  133.7 0.0 collective-permute-done.16
  133.7 0.0 collective-permute-done.11
  133.7 0.8 convert_add_fusion
  (5 shorter events, 0.2 us)
Async XLA Ops:
  2.0 32.6 %all-to-all-start = ((bf16[8,128,384]{2,1,0:T(8,128)(2,1)}), bf16[8,128,384]{2,1,0:T(8,128)(2,1)S(1)}, u32[]{:S(2)}, u32[]{:S(2)}) async-start(bf16[8,128,384]{2,1,0:T(8,128)(2,1)} %get-tuple-element.39), calls=%async_computation | async-start | bytes 1572864 | tf_op jit(solution)/shard_map/all_to_all | solution.py:258
  11.0 7.0 %collective-permute-start.1 = (bf16[256,384]{1,0:T(8,128)(2,1)}, bf16[256,384]{1,0:T(8,128)(2,1)S(1)}, u32[]{:S(2)}, u32[]{:S(2)}) collective-permute-start(bf16[256,384]{1,0:T(8,128)(2,1)} %proto_hbm.1), channel_id=1, source_target_pairs={{0,8},{8,16},{16,24},{24,0},{1,9},{9,17},{17,25},{25,1},{2,10},{10... | collective-permute-start | bytes 589832 | tf_op jit(solution)/shard_map/ppermute | solution.py:236
  12.3 7.8 %collective-permute-start.5 = (bf16[256,384]{1,0:T(8,128)(2,1)}, bf16[256,384]{1,0:T(8,128)(2,1)S(1)}, u32[]{:S(2)}, u32[]{:S(2)}) collective-permute-start(bf16[256,384]{1,0:T(8,128)(2,1)} %proto_hbm.1), channel_id=1, source_target_pairs={{0,24},{8,0},{16,8},{24,16},{1,25},{9,1},{17,9},{25,17},{2,26},{10... | collective-permute-start | bytes 589832 | tf_op jit(solution)/shard_map/ppermute | solution.py:236
  13.8 9.7 %collective-permute-start.3 = (bf16[256,384]{1,0:T(8,128)(2,1)}, bf16[256,384]{1,0:T(8,128)(2,1)S(1)}, u32[]{:S(2)}, u32[]{:S(2)}) collective-permute-start(bf16[256,384]{1,0:T(8,128)(2,1)} %proto_hbm.1), channel_id=1, source_target_pairs={{0,16},{8,24},{16,0},{24,8},{1,17},{9,25},{17,1},{25,9},{2,18},{10... | collective-permute-start | bytes 589832 | tf_op jit(solution)/shard_map/ppermute | solution.py:236
  15.4 20.6 %collective-permute-start = (bf16[256,384]{1,0:T(8,128)(2,1)S(1)}, bf16[256,384]{1,0:T(8,128)(2,1)S(1)}, u32[]{:S(2)}, u32[]{:S(2)}) collective-permute-start(bf16[256,384]{1,0:T(8,128)(2,1)S(1)} %get-tuple-element.40.refs_0_), channel_id=1, source_target_pairs={{0,1},{1,0},{2,3},{3,2},{4,5},{5,4},{6,7},{7,6},{8,9},{9,8},{10,11... | collective-permute-start | bytes 589832 | tf_op jit(solution)/shard_map/ppermute | solution.py:236
  18.0 18.0 %collective-permute-start.2 = (bf16[256,384]{1,0:T(8,128)(2,1)S(1)}, bf16[256,384]{1,0:T(8,128)(2,1)S(1)}, u32[]{:S(2)}, u32[]{:S(2)}) collective-permute-start(bf16[256,384]{1,0:T(8,128)(2,1)S(1)} %collective-permute-done.1.refs_1_), channel_id=1, source_target_pairs={{0,1},{1,0},{2,3},{3,2},{4,5},{5,4},{6,7},{7,6},{8,9},{9,8},{10,11... | collective-permute-start | bytes 589832 | tf_op jit(solution)/shard_map/ppermute | solution.py:236
  20.1 15.9 %collective-permute-start.6 = (bf16[256,384]{1,0:T(8,128)(2,1)S(1)}, bf16[256,384]{1,0:T(8,128)(2,1)S(1)}, u32[]{:S(2)}, u32[]{:S(2)}) collective-permute-start(bf16[256,384]{1,0:T(8,128)(2,1)S(1)} %collective-permute-done.5.refs_3_), channel_id=1, source_target_pairs={{0,1},{1,0},{2,3},{3,2},{4,5},{5,4},{6,7},{7,6},{8,9},{9,8},{10,11... | collective-permute-start | bytes 589832 | tf_op jit(solution)/shard_map/ppermute | solution.py:236
  23.5 12.5 %collective-permute-start.4 = (bf16[256,384]{1,0:T(8,128)(2,1)S(1)}, bf16[256,384]{1,0:T(8,128)(2,1)S(1)}, u32[]{:S(2)}, u32[]{:S(2)}) collective-permute-start(bf16[256,384]{1,0:T(8,128)(2,1)S(1)} %collective-permute-done.3.refs_2_), channel_id=1, source_target_pairs={{0,1},{1,0},{2,3},{3,2},{4,5},{5,4},{6,7},{7,6},{8,9},{9,8},{10,11... | collective-permute-start | bytes 589832 | tf_op jit(solution)/shard_map/ppermute | solution.py:236
  25.2 13.6 %collective-permute-start.7 = (bf16[128,384]{1,0:T(8,128)(2,1)S(1)}, bf16[128,384]{1,0:T(8,128)(2,1)S(1)}, u32[]{:S(2)}, u32[]{:S(2)}) collective-permute-start(bf16[128,384]{1,0:T(8,128)(2,1)S(1)} %get-tuple-element.43.refs_0_), channel_id=1, source_target_pairs={{0,128},{32,160},{64,192},{96,224},{128,0},{160,32},{192,64},{224,... | collective-permute-start | bytes 294920 | tf_op jit(solution)/shard_map/ppermute | solution.py:259
  65.5 11.5 %collective-permute-start.8 = (bf16[256,384]{1,0:T(8,128)(2,1)S(1)}, bf16[256,384]{1,0:T(8,128)(2,1)S(1)}, u32[]{:S(2)}, u32[]{:S(2)}) collective-permute-start(bf16[256,384]{1,0:T(8,128)(2,1)S(1)} %pad_maximum_fusion.1), channel_id=1, source_target_pairs={{0,64},{32,96},{64,0},{96,32},{128,192},{160,224},{192,128},{224,1... | collective-permute-start | bytes 589832 | tf_op jit(solution)/shard_map/ppermute | solution.py:285
  90.3 10.3 %collective-permute-start.9 = (bf16[512,384]{1,0:T(8,128)(2,1)S(1)}, bf16[512,384]{1,0:T(8,128)(2,1)S(1)}, u32[]{:S(2)}, u32[]{:S(2)}) collective-permute-start(bf16[512,384]{1,0:T(8,128)(2,1)S(1)} %pad_maximum_fusion), channel_id=1, source_target_pairs={{0,32},{32,0},{64,96},{96,64},{128,160},{160,128},{192,224},{224,1... | collective-permute-start | bytes 1179656 | tf_op jit(solution)/shard_map/ppermute | solution.py:285
  116.8 4.2 %collective-permute-start.10 = (f32[256,384]{1,0:T(8,128)S(1)}, f32[256,384]{1,0:T(8,128)S(1)}, u32[]{:S(2)}, u32[]{:S(2)}) collective-permute-start(f32[256,384]{1,0:T(8,128)S(1)} %shard_map.45), channel_id=1, source_target_pairs={{0,1},{1,0},{2,3},{3,2},{4,5},{5,4},{6,7},{7,6},{8,9},{9,8},{10,11... | collective-permute-start | bytes 1179656 | tf_op jit(solution)/shard_map/ppermute | solution.py:236
  120.4 3.6 %collective-permute-start.13 = (f32[256,384]{1,0:T(8,128)S(1)}, f32[256,384]{1,0:T(8,128)S(1)}, u32[]{:S(2)}, u32[]{:S(2)}) collective-permute-start(f32[256,384]{1,0:T(8,128)S(1)} %get-tuple-element.70), channel_id=1, source_target_pairs={{0,1},{1,0},{2,3},{3,2},{4,5},{5,4},{6,7},{7,6},{8,9},{9,8},{10,11... | collective-permute-start | bytes 1179656 | tf_op jit(solution)/shard_map/ppermute | solution.py:236
  120.5 4.0 %collective-permute-start.15 = (f32[256,384]{1,0:T(8,128)S(1)}, f32[256,384]{1,0:T(8,128)S(1)}, u32[]{:S(2)}, u32[]{:S(2)}) collective-permute-start(f32[256,384]{1,0:T(8,128)S(1)} %get-tuple-element.72), channel_id=1, source_target_pairs={{0,1},{1,0},{2,3},{3,2},{4,5},{5,4},{6,7},{7,6},{8,9},{9,8},{10,11... | collective-permute-start | bytes 1179656 | tf_op jit(solution)/shard_map/ppermute | solution.py:236
  121.0 8.1 %collective-permute-start.12 = (bf16[256,384]{1,0:T(8,128)(2,1)S(1)}, bf16[256,384]{1,0:T(8,128)(2,1)S(1)}, u32[]{:S(2)}, u32[]{:S(2)}) collective-permute-start(bf16[256,384]{1,0:T(8,128)(2,1)S(1)} %add_convert_fusion.2), channel_id=1, source_target_pairs={{0,16},{8,24},{16,0},{24,8},{1,17},{9,25},{17,1},{25,9},{2,18},{10... | collective-permute-start | bytes 589832 | tf_op jit(solution)/shard_map/ppermute | solution.py:236
  123.5 10.2 %collective-permute-start.11 = (f32[256,384]{1,0:T(8,128)S(1)}, f32[256,384]{1,0:T(8,128)S(1)}, u32[]{:S(2)}, u32[]{:S(2)}) collective-permute-start(f32[256,384]{1,0:T(8,128)S(1)} %get-tuple-element.68), channel_id=1, source_target_pairs={{0,1},{1,0},{2,3},{3,2},{4,5},{5,4},{6,7},{7,6},{8,9},{9,8},{10,11... | collective-permute-start | bytes 1179656 | tf_op jit(solution)/shard_map/ppermute | solution.py:236
  124.0 9.7 %collective-permute-start.14 = (bf16[256,384]{1,0:T(8,128)(2,1)S(1)}, bf16[256,384]{1,0:T(8,128)(2,1)S(1)}, u32[]{:S(2)}, u32[]{:S(2)}) collective-permute-start(bf16[256,384]{1,0:T(8,128)(2,1)S(1)} %add_convert_fusion.1), channel_id=1, source_target_pairs={{0,8},{8,16},{16,24},{24,0},{1,9},{9,17},{17,25},{25,1},{2,10},{10... | collective-permute-start | bytes 589832 | tf_op jit(solution)/shard_map/ppermute | solution.py:236
  124.5 9.2 %collective-permute-start.16 = (bf16[256,384]{1,0:T(8,128)(2,1)S(1)}, bf16[256,384]{1,0:T(8,128)(2,1)S(1)}, u32[]{:S(2)}, u32[]{:S(2)}) collective-permute-start(bf16[256,384]{1,0:T(8,128)(2,1)S(1)} %add_convert_fusion), channel_id=1, source_target_pairs={{0,24},{8,0},{16,8},{24,16},{1,25},{9,1},{17,9},{25,17},{2,26},{10... | collective-permute-start | bytes 589832 | tf_op jit(solution)/shard_map/ppermute | solution.py:236

commit v6 on v5

--- a/solution.py
+++ b/solution.py
@@ -277,22 +277,20 @@
         near_sums,
         scratch=(pltpu.VMEM((HROWS, LANES), F32),),
     )
-    cols, got = lax.optimization_barrier((cols, got))
-    pieces = [stud]
-    for step, hop in enumerate((4, 2, 1)):
-        if step:
+    pieces = [stud, got]
+    for step in range(ITERS):
+        if step + 1 < ITERS:
+            cols, pieces = lax.optimization_barrier((cols, pieces))
+            held = jnp.concatenate(pieces, axis=0)
             cols, held = lax.optimization_barrier((cols, held))
+            hop = (2, 1)[step]
             got = lax.ppermute(held, "z", [(i, i ^ hop) for i in range(NZ)])
         cols = lax.all_to_all(cols, ("y", "core"), 0, 0, tiled=True)
-        if step == 0:
-            cols, got = lax.optimization_barrier((cols, got))
-        pieces.append(got)
         if step + 1 < ITERS:
+            pieces = pieces + [got]
             rows = call(
                 row_kernel, row_shape, cols, pinned(near_expo), pinned(far_expo), scratch=(weights,)
             )
-            held = jnp.concatenate(pieces, axis=0)
-            rows, held = lax.optimization_barrier((rows, held))
             rows = lax.all_to_all(rows, ("z", "x"), 0, 0, tiled=True)
             cols = call(col_kernel, col_shape, rows, pinned(near_expo), pinned(far_expo))
     near_expz, far_expz, stud, rows = call(

time: 135 us -> 134 us (level)
  starting transfers between devices: 36.7 us -> 35.3 us
  transfers between devices with their start and end apart: 18 -> 18, of which waited for: 6 -> 5; matrix products, arithmetic and copies ran while one was open for 0% -> 0% of each run, Pallas kernels for 4% -> 6%
where the time goes in v6:
time: 134 us; the launch traced here: 133 us
  blocking collectives  70.6 us (53%)
  starting transfers between devices  35.3 us (26%)
  waiting for transfers between devices  13.3 us (10%)
  Pallas kernels  13.2 us (10%)
    all_to_all x3, blocking collectives, shards(): rows = lax.all_to_all(rows, ('z', 'x'), 0, 0, tiled=True)  41.8 us
    all_to_all x3, blocking collectives, shards(): cols = lax.all_to_all(cols, ('y', 'core'), 0, 0, tiled=True)  28.7 us
    ppermute x14, starting transfers between devices, shift(): return lax.ppermute(x, axis, [(i, (i + step) % size) for i in range(size)])  20.1 us
    pallas_call x11, Pallas kernels, call(): pl.pallas_call(kernel, out_shape=out_shape, in_specs=specs or [VMEM] * le...  13.2 us
    all_to_all x1, starting transfers between devices, shards(): teach = lax.all_to_all(teach, 'z', 0, 0, tiled=True)  9.03 us
    ppermute x14, waiting for transfers between devices, shift(): return lax.ppermute(x, axis, [(i, (i + step) % size) for i in range(size)])  7.99 us
    ppermute x1, starting transfers between devices, shards(): got = lax.ppermute(stud, 'z', [(i, i ^ 4) for i in range(NZ)])  5.37 us
    all_to_all x1, waiting for transfers between devices, shards(): teach = lax.all_to_all(teach, 'z', 0, 0, tiled=True)  4.01 us
  transfers between devices with their start and end apart: 18, of which 5 were waited for; matrix products, arithmetic and copies ran while one was open for 0% of the time, Pallas kernels for 6%

profile of v6, /device:TPU:1, one launch (start us, length us, event | category | flops | bytes accessed | tf_op | source)
XLA Modules:
  0.0 133.5 jit_solution(11706573567260008480)
XLA Ops:
  0.0 2.0 %shard_map.37 = (bf16[8,128,384]{2,1,0:T(8,128)(2,1)}, bf16[128,384]{1,0:T(8,128)(2,1)S(1)}, bf16[256,384]{1,0:T(8,128)(2,1)S(1)}) custom-call(bf16[256,384]{1,0:T(8,128)(2,1)} %teach_hbm.1, bf16[256,384]{1,0:T(8,128)(2,1)} %stud_hbm.1, bf16[256,384]{1,0:T(8,128)(2,1)} %proto_hbm.1), custom_call_target="tpu_custom_call" | custom-call | tf_op jit(solution)/shard_map/pallas_call | solution.py:225
  2.0 9.0 %all-to-all-start = ((bf16[8,128,384]{2,1,0:T(8,128)(2,1)}), bf16[8,128,384]{2,1,0:T(8,128)(2,1)S(1)}, u32[]{:S(2)}, u32[]{:S(2)}) async-start(bf16[8,128,384]{2,1,0:T(8,128)(2,1)} %get-tuple-element.38), calls=%async_computation | async-start | bytes 1572864 | tf_op jit(solution)/shard_map/all_to_all | solution.py:258
  11.0 1.3 collective-permute-start.1
  12.3 1.5 %collective-permute-start.5 = (bf16[256,384]{1,0:T(8,128)(2,1)}, bf16[256,384]{1,0:T(8,128)(2,1)S(1)}, u32[]{:S(2)}, u32[]{:S(2)}) collective-permute-start(bf16[256,384]{1,0:T(8,128)(2,1)} %proto_hbm.1), channel_id=1, source_target_pairs={{0,24},{8,0},{16,8},{24,16},{1,25},{9,1},{17,9},{25,17},{2,26},{10... | collective-permute-start | bytes 589832 | tf_op jit(solution)/shard_map/ppermute | solution.py:236
  13.8 1.6 %collective-permute-start.3 = (bf16[256,384]{1,0:T(8,128)(2,1)}, bf16[256,384]{1,0:T(8,128)(2,1)S(1)}, u32[]{:S(2)}, u32[]{:S(2)}) collective-permute-start(bf16[256,384]{1,0:T(8,128)(2,1)} %proto_hbm.1), channel_id=1, source_target_pairs={{0,16},{8,24},{16,0},{24,8},{1,17},{9,25},{17,1},{25,9},{2,18},{10... | collective-permute-start | bytes 589832 | tf_op jit(solution)/shard_map/ppermute | solution.py:236
  15.4 1.8 %collective-permute-start = (bf16[256,384]{1,0:T(8,128)(2,1)S(1)}, bf16[256,384]{1,0:T(8,128)(2,1)S(1)}, u32[]{:S(2)}, u32[]{:S(2)}) collective-permute-start(bf16[256,384]{1,0:T(8,128)(2,1)S(1)} %get-tuple-element.39.refs_0_), channel_id=1, source_target_pairs={{0,1},{1,0},{2,3},{3,2},{4,5},{5,4},{6,7},{7,6},{8,9},{9,8},{10,11... | collective-permute-start | bytes 589832 | tf_op jit(solution)/shard_map/ppermute | solution.py:236
  17.2 0.8 collective-permute-done.1.refs_1_
  18.0 2.1 %collective-permute-start.2 = (bf16[256,384]{1,0:T(8,128)(2,1)S(1)}, bf16[256,384]{1,0:T(8,128)(2,1)S(1)}, u32[]{:S(2)}, u32[]{:S(2)}) collective-permute-start(bf16[256,384]{1,0:T(8,128)(2,1)S(1)} %collective-permute-done.1.refs_1_), channel_id=1, source_target_pairs={{0,1},{1,0},{2,3},{3,2},{4,5},{5,4},{6,7},{7,6},{8,9},{9,8},{10,11... | collective-permute-start | bytes 589832 | tf_op jit(solution)/shard_map/ppermute | solution.py:236
  20.1 0.0 collective-permute-done.5.refs_3_
  20.1 3.4 %collective-permute-start.6 = (bf16[256,384]{1,0:T(8,128)(2,1)S(1)}, bf16[256,384]{1,0:T(8,128)(2,1)S(1)}, u32[]{:S(2)}, u32[]{:S(2)}) collective-permute-start(bf16[256,384]{1,0:T(8,128)(2,1)S(1)} %collective-permute-done.5.refs_3_), channel_id=1, source_target_pairs={{0,1},{1,0},{2,3},{3,2},{4,5},{5,4},{6,7},{7,6},{8,9},{9,8},{10,11... | collective-permute-start | bytes 589832 | tf_op jit(solution)/shard_map/ppermute | solution.py:236
  23.5 0.0 collective-permute-done.3.refs_2_
  23.5 1.7 %collective-permute-start.4 = (bf16[256,384]{1,0:T(8,128)(2,1)S(1)}, bf16[256,384]{1,0:T(8,128)(2,1)S(1)}, u32[]{:S(2)}, u32[]{:S(2)}) collective-permute-start(bf16[256,384]{1,0:T(8,128)(2,1)S(1)} %collective-permute-done.3.refs_2_), channel_id=1, source_target_pairs={{0,1},{1,0},{2,3},{3,2},{4,5},{5,4},{6,7},{7,6},{8,9},{9,8},{10,11... | collective-permute-start | bytes 589832 | tf_op jit(solution)/shard_map/ppermute | solution.py:236
  25.2 5.4 %collective-permute-start.7 = (bf16[128,384]{1,0:T(8,128)(2,1)S(1)}, bf16[128,384]{1,0:T(8,128)(2,1)S(1)}, u32[]{:S(2)}, u32[]{:S(2)}) collective-permute-start(bf16[128,384]{1,0:T(8,128)(2,1)S(1)} %get-tuple-element.51.refs_0_), channel_id=1, source_target_pairs={{0,128},{32,160},{64,192},{96,224},{128,0},{160,32},{192,64},{224,... | collective-permute-start | bytes 294920 | tf_op jit(solution)/shard_map/ppermute | solution.py:259
  30.6 4.0 %all-to-all-done.teach_ref = bf16[8,128,384]{2,1,0:T(8,128)(2,1)S(1)} async-done(((bf16[8,128,384]{2,1,0:T(8,128)(2,1)}), bf16[8,128,384]{2,1,0:T(8,128)(2,1)S(1)}, u32[]{:S(2)}, u32[]{:S(2)}) %all-to-all-start) | async-done | bytes 786464 | tf_op jit(solution)/shard_map/all_to_all | solution.py:258
  34.6 1.4 %shard_map.38 = (f32[1024,1024]{1,0:T(8,128)S(1)}, bf16[1024,384]{1,0:T(8,128)(2,1)S(1)}, f32[8,128]{1,0:T(8,128)S(1)}) custom-call(bf16[8,128,384]{2,1,0:T(8,128)(2,1)S(1)} %all-to-all-done.teach_ref, bf16[256,384]{1,0:T(8,128)(2,1)S(1)} %get-tuple-element.39.refs_0_, bf16[256,384]{1,0:T(8,128)(2,1)S(1)} %collective-permute-done.1.refs_1_, ...), custom_call_target="tpu_custom_call" | custom-call | tf_op jit(solution)/shard_map/pallas_call | solution.py:225
  36.0 0.0 collective-permute-done.refs_0_
  36.0 0.0 collective-permute-done.2.refs_1_
  36.0 0.0 collective-permute-done.6.refs_3_
  36.0 0.0 collective-permute-done.4.refs_2_
  36.0 1.4 %shard_map.39 = (f32[1024,1024]{1,0:T(8,128)S(1)}, bf16[1024,384]{1,0:T(8,128)(2,1)S(1)}, f32[8,16,128]{2,1,0:T(8,128)S(1)}) custom-call(bf16[8,128,384]{2,1,0:T(8,128)(2,1)S(1)} %all-to-all-done.teach_ref, bf16[256,384]{1,0:T(8,128)(2,1)S(1)} %collective-permute-done.refs_0_, bf16[256,384]{1,0:T(8,128)(2,1)S(1)} %collective-permute-done.2.refs_1_, ...), custom_call_target="tpu_custom_call" | custom-call | tf_op jit(solution)/shard_map/pallas_call | solution.py:225
  37.5 1.3 collective-permute-done.7.refs_1_
  38.8 0.1 collective-permute-start.8
  38.9 9.6 %all_to_all.35.col_sums_ref = f32[8,16,128]{2,1,0:T(8,128)S(1)} all-to-all(f32[8,16,128]{2,1,0:T(8,128)S(1)} %get-tuple-element.46), channel_id=1, replica_groups=mesh['z'=8,'y'=4,'x'=4,'core'=2] {'y','core'}, dimensions={0} | all-to-all | bytes 131072 | tf_op jit(solution)/shard_map/all_to_all | solution.py:288
  48.5 0.6 shard_map.40
  49.2 17.2 %all_to_all.36.row_sums_ref = bf16[32,8,128]{2,1,0:T(8,128)(2,1)S(1)} all-to-all(bf16[32,8,128]{2,1,0:T(8,128)(2,1)S(1)} %shard_map.40), channel_id=1, replica_groups=mesh['z'=8,'y'=4,'x'=4,'core'=2] {'z','x'}, dimensions={0} | all-to-all | bytes 131072 | tf_op jit(solution)/shard_map/all_to_all | solution.py:294
  66.4 0.7 shard_map.41
  67.1 0.0 collective-permute-done.8.refs_2_
  67.1 0.7 collective-permute-start.9
  67.8 9.7 %all_to_all.37.col_sums_ref = f32[8,16,128]{2,1,0:T(8,128)S(1)} all-to-all(f32[8,16,128]{2,1,0:T(8,128)S(1)} %shard_map.41), channel_id=1, replica_groups=mesh['z'=8,'y'=4,'x'=4,'core'=2] {'y','core'}, dimensions={0} | all-to-all | bytes 131072 | tf_op jit(solution)/shard_map/all_to_all | solution.py:288
  77.5 0.6 shard_map.42
  78.1 12.2 %all_to_all.38.row_sums_ref = bf16[32,8,128]{2,1,0:T(8,128)(2,1)S(1)} all-to-all(bf16[32,8,128]{2,1,0:T(8,128)(2,1)S(1)} %shard_map.42), channel_id=1, replica_groups=mesh['z'=8,'y'=4,'x'=4,'core'=2] {'z','x'}, dimensions={0} | all-to-all | bytes 131072 | tf_op jit(solution)/shard_map/all_to_all | solution.py:294
  90.4 0.7 shard_map.43
  91.0 9.4 %all_to_all.39.refs_4_.col_sums_ref = f32[8,16,128]{2,1,0:T(8,128)S(1)} all-to-all(f32[8,16,128]{2,1,0:T(8,128)S(1)} %shard_map.43), channel_id=1, replica_groups=mesh['z'=8,'y'=4,'x'=4,'core'=2] {'y','core'}, dimensions={0} | all-to-all | bytes 131072 | tf_op jit(solution)/shard_map/all_to_all | solution.py:288
  100.4 0.0 collective-permute-done.9.refs_3_
  100.5 2.8 %shard_map.44 = (f32[1024,1024]{1,0:T(8,128)S(1)}, f32[1024,1024]{1,0:T(8,128)S(1)}, bf16[1024,384]{1,0:T(8,128)(2,1)S(1)}, bf16[32,16,128]{2,1,0:T(8,128)(2,1)S(1)}) custom-call(bf16[128,384]{1,0:T(8,128)(2,1)S(1)} %get-tuple-element.51.refs_0_, bf16[128,384]{1,0:T(8,128)(2,1)S(1)} %collective-permute-done.7.refs_1_, ...), custom_call_target="tpu_custom_call" | custom-call | tf_op jit(solution)/shard_map/pallas_call | solution.py:225
  103.3 12.4 %all_to_all.40.row_sums_ref = bf16[32,16,128]{2,1,0:T(8,128)(2,1)S(1)} all-to-all(bf16[32,16,128]{2,1,0:T(8,128)(2,1)S(1)} %get-tuple-element.58), channel_id=1, replica_groups=mesh['z'=8,'y'=4,'x'=4,'core'=2] {'z','x'}, dimensions={0} | all-to-all | bytes 262144 | tf_op jit(solution)/shard_map/all_to_all | solution.py:312
  115.7 0.5 shard_map.45
  116.2 2.0 %collective-permute-start.10 = (f32[256,384]{1,0:T(8,128)S(1)}, f32[256,384]{1,0:T(8,128)S(1)}, u32[]{:S(2)}, u32[]{:S(2)}) collective-permute-start(f32[256,384]{1,0:T(8,128)S(1)} %shard_map.45), channel_id=1, source_target_pairs={{0,1},{1,0},{2,3},{3,2},{4,5},{5,4},{6,7},{7,6},{8,9},{9,8},{10,11... | collective-permute-start | bytes 1179656 | tf_op jit(solution)/shard_map/ppermute | solution.py:236
  118.2 1.1 shard_map.46
  119.3 0.1 collective-permute-start.13
  119.4 0.5 collective-permute-start.15
  119.9 0.0 collective-permute-done.10
  119.9 0.8 collective-permute-start.12
  120.8 1.3 %shard_map.47 = (f32[256,384]{1,0:T(8,128)S(1)}, f32[256,384]{1,0:T(8,128)S(1)}, f32[256,384]{1,0:T(8,128)S(1)}, f32[256,384]{1,0:T(8,128)S(1)}) custom-call(f32[8,16,128]{2,1,0:T(8,128)S(1)} %all_to_all.39.refs_4_.col_sums_ref, bf16[32,16,128]{2,1,0:T(8,128)(2,1)S(1)} %all_to_all.40.row_sums_ref, bf16[1024,384]{1,0:T(8,128)(2,1)S(1)} %get-tuple-element.59.stud_ref, ...), custom_call_target="tpu_custom_call" | custom-call | tf_op jit(solution)/shard_map/pallas_call | solution.py:225
  122.1 0.4 collective-permute-start.11
  122.6 0.0 collective-permute-done.13
  122.6 0.8 collective-permute-start.14
  123.4 0.0 collective-permute-done.15
  123.4 2.1 %collective-permute-start.16 = (bf16[256,384]{1,0:T(8,128)(2,1)S(1)}, bf16[256,384]{1,0:T(8,128)(2,1)S(1)}, u32[]{:S(2)}, u32[]{:S(2)}) collective-permute-start(bf16[256,384]{1,0:T(8,128)(2,1)S(1)} %add_convert_fusion), channel_id=1, source_target_pairs={{0,24},{8,0},{16,8},{24,16},{1,25},{9,1},{17,9},{25,17},{2,26},{10... | collective-permute-start | bytes 589832 | tf_op jit(solution)/shard_map/ppermute | solution.py:236
  125.5 2.5 %collective-permute-done.12 = bf16[256,384]{1,0:T(8,128)(2,1)S(1)} collective-permute-done((bf16[256,384]{1,0:T(8,128)(2,1)S(1)}, bf16[256,384]{1,0:T(8,128)(2,1)S(1)}, u32[]{:S(2)}, u32[]{:S(2)}) %collective-permute-start.12) | collective-permute-done | bytes 196640 | tf_op jit(solution)/shard_map/ppermute | solution.py:236
  128.0 4.6 %collective-permute-done.14 = bf16[256,384]{1,0:T(8,128)(2,1)S(1)} collective-permute-done((bf16[256,384]{1,0:T(8,128)(2,1)S(1)}, bf16[256,384]{1,0:T(8,128)(2,1)S(1)}, u32[]{:S(2)}, u32[]{:S(2)}) %collective-permute-start.14) | collective-permute-done | bytes 196640 | tf_op jit(solution)/shard_map/ppermute | solution.py:236
  132.6 0.0 collective-permute-done.16
  132.6 0.0 collective-permute-done.11
  132.6 0.8 convert_add_fusion
  (5 shorter events, 0.2 us)
Async XLA Ops:
  2.0 32.6 %all-to-all-start = ((bf16[8,128,384]{2,1,0:T(8,128)(2,1)}), bf16[8,128,384]{2,1,0:T(8,128)(2,1)S(1)}, u32[]{:S(2)}, u32[]{:S(2)}) async-start(bf16[8,128,384]{2,1,0:T(8,128)(2,1)} %get-tuple-element.38), calls=%async_computation | async-start | bytes 1572864 | tf_op jit(solution)/shard_map/all_to_all | solution.py:258
  11.0 7.0 %collective-permute-start.1 = (bf16[256,384]{1,0:T(8,128)(2,1)}, bf16[256,384]{1,0:T(8,128)(2,1)S(1)}, u32[]{:S(2)}, u32[]{:S(2)}) collective-permute-start(bf16[256,384]{1,0:T(8,128)(2,1)} %proto_hbm.1), channel_id=1, source_target_pairs={{0,8},{8,16},{16,24},{24,0},{1,9},{9,17},{17,25},{25,1},{2,10},{10... | collective-permute-start | bytes 589832 | tf_op jit(solution)/shard_map/ppermute | solution.py:236
  12.3 7.8 %collective-permute-start.5 = (bf16[256,384]{1,0:T(8,128)(2,1)}, bf16[256,384]{1,0:T(8,128)(2,1)S(1)}, u32[]{:S(2)}, u32[]{:S(2)}) collective-permute-start(bf16[256,384]{1,0:T(8,128)(2,1)} %proto_hbm.1), channel_id=1, source_target_pairs={{0,24},{8,0},{16,8},{24,16},{1,25},{9,1},{17,9},{25,17},{2,26},{10... | collective-permute-start | bytes 589832 | tf_op jit(solution)/shard_map/ppermute | solution.py:236
  13.8 9.7 %collective-permute-start.3 = (bf16[256,384]{1,0:T(8,128)(2,1)}, bf16[256,384]{1,0:T(8,128)(2,1)S(1)}, u32[]{:S(2)}, u32[]{:S(2)}) collective-permute-start(bf16[256,384]{1,0:T(8,128)(2,1)} %proto_hbm.1), channel_id=1, source_target_pairs={{0,16},{8,24},{16,0},{24,8},{1,17},{9,25},{17,1},{25,9},{2,18},{10... | collective-permute-start | bytes 589832 | tf_op jit(solution)/shard_map/ppermute | solution.py:236
  15.4 20.6 %collective-permute-start = (bf16[256,384]{1,0:T(8,128)(2,1)S(1)}, bf16[256,384]{1,0:T(8,128)(2,1)S(1)}, u32[]{:S(2)}, u32[]{:S(2)}) collective-permute-start(bf16[256,384]{1,0:T(8,128)(2,1)S(1)} %get-tuple-element.39.refs_0_), channel_id=1, source_target_pairs={{0,1},{1,0},{2,3},{3,2},{4,5},{5,4},{6,7},{7,6},{8,9},{9,8},{10,11... | collective-permute-start | bytes 589832 | tf_op jit(solution)/shard_map/ppermute | solution.py:236
  18.0 18.0 %collective-permute-start.2 = (bf16[256,384]{1,0:T(8,128)(2,1)S(1)}, bf16[256,384]{1,0:T(8,128)(2,1)S(1)}, u32[]{:S(2)}, u32[]{:S(2)}) collective-permute-start(bf16[256,384]{1,0:T(8,128)(2,1)S(1)} %collective-permute-done.1.refs_1_), channel_id=1, source_target_pairs={{0,1},{1,0},{2,3},{3,2},{4,5},{5,4},{6,7},{7,6},{8,9},{9,8},{10,11... | collective-permute-start | bytes 589832 | tf_op jit(solution)/shard_map/ppermute | solution.py:236
  20.1 15.9 %collective-permute-start.6 = (bf16[256,384]{1,0:T(8,128)(2,1)S(1)}, bf16[256,384]{1,0:T(8,128)(2,1)S(1)}, u32[]{:S(2)}, u32[]{:S(2)}) collective-permute-start(bf16[256,384]{1,0:T(8,128)(2,1)S(1)} %collective-permute-done.5.refs_3_), channel_id=1, source_target_pairs={{0,1},{1,0},{2,3},{3,2},{4,5},{5,4},{6,7},{7,6},{8,9},{9,8},{10,11... | collective-permute-start | bytes 589832 | tf_op jit(solution)/shard_map/ppermute | solution.py:236
  23.5 12.5 %collective-permute-start.4 = (bf16[256,384]{1,0:T(8,128)(2,1)S(1)}, bf16[256,384]{1,0:T(8,128)(2,1)S(1)}, u32[]{:S(2)}, u32[]{:S(2)}) collective-permute-start(bf16[256,384]{1,0:T(8,128)(2,1)S(1)} %collective-permute-done.3.refs_2_), channel_id=1, source_target_pairs={{0,1},{1,0},{2,3},{3,2},{4,5},{5,4},{6,7},{7,6},{8,9},{9,8},{10,11... | collective-permute-start | bytes 589832 | tf_op jit(solution)/shard_map/ppermute | solution.py:236
  25.2 13.6 %collective-permute-start.7 = (bf16[128,384]{1,0:T(8,128)(2,1)S(1)}, bf16[128,384]{1,0:T(8,128)(2,1)S(1)}, u32[]{:S(2)}, u32[]{:S(2)}) collective-permute-start(bf16[128,384]{1,0:T(8,128)(2,1)S(1)} %get-tuple-element.51.refs_0_), channel_id=1, source_target_pairs={{0,128},{32,160},{64,192},{96,224},{128,0},{160,32},{192,64},{224,... | collective-permute-start | bytes 294920 | tf_op jit(solution)/shard_map/ppermute | solution.py:259
  38.8 28.3 %collective-permute-start.8 = (bf16[256,384]{1,0:T(8,128)(2,1)S(1)}, bf16[256,384]{1,0:T(8,128)(2,1)S(1)}, u32[]{:S(2)}, u32[]{:S(2)}) collective-permute-start(bf16[256,384]{1,0:T(8,128)(2,1)S(1)} %pad_maximum_fusion.1), channel_id=1, source_target_pairs={{0,64},{32,96},{64,0},{96,32},{128,192},{160,224},{192,128},{224,1... | collective-permute-start | bytes 589832 | tf_op jit(solution)/shard_map/ppermute | solution.py:287
  67.1 33.3 %collective-permute-start.9 = (bf16[512,384]{1,0:T(8,128)(2,1)S(1)}, bf16[512,384]{1,0:T(8,128)(2,1)S(1)}, u32[]{:S(2)}, u32[]{:S(2)}) collective-permute-start(bf16[512,384]{1,0:T(8,128)(2,1)S(1)} %pad_maximum_fusion), channel_id=1, source_target_pairs={{0,32},{32,0},{64,96},{96,64},{128,160},{160,128},{192,224},{224,1... | collective-permute-start | bytes 1179656 | tf_op jit(solution)/shard_map/ppermute | solution.py:287
  116.2 3.7 %collective-permute-start.10 = (f32[256,384]{1,0:T(8,128)S(1)}, f32[256,384]{1,0:T(8,128)S(1)}, u32[]{:S(2)}, u32[]{:S(2)}) collective-permute-start(f32[256,384]{1,0:T(8,128)S(1)} %shard_map.45), channel_id=1, source_target_pairs={{0,1},{1,0},{2,3},{3,2},{4,5},{5,4},{6,7},{7,6},{8,9},{9,8},{10,11... | collective-permute-start | bytes 1179656 | tf_op jit(solution)/shard_map/ppermute | solution.py:236
  119.3 3.3 %collective-permute-start.13 = (f32[256,384]{1,0:T(8,128)S(1)}, f32[256,384]{1,0:T(8,128)S(1)}, u32[]{:S(2)}, u32[]{:S(2)}) collective-permute-start(f32[256,384]{1,0:T(8,128)S(1)} %get-tuple-element.68), channel_id=1, source_target_pairs={{0,1},{1,0},{2,3},{3,2},{4,5},{5,4},{6,7},{7,6},{8,9},{9,8},{10,11... | collective-permute-start | bytes 1179656 | tf_op jit(solution)/shard_map/ppermute | solution.py:236
  119.4 4.0 %collective-permute-start.15 = (f32[256,384]{1,0:T(8,128)S(1)}, f32[256,384]{1,0:T(8,128)S(1)}, u32[]{:S(2)}, u32[]{:S(2)}) collective-permute-start(f32[256,384]{1,0:T(8,128)S(1)} %get-tuple-element.70), channel_id=1, source_target_pairs={{0,1},{1,0},{2,3},{3,2},{4,5},{5,4},{6,7},{7,6},{8,9},{9,8},{10,11... | collective-permute-start | bytes 1179656 | tf_op jit(solution)/shard_map/ppermute | solution.py:236
  119.9 8.1 %collective-permute-start.12 = (bf16[256,384]{1,0:T(8,128)(2,1)S(1)}, bf16[256,384]{1,0:T(8,128)(2,1)S(1)}, u32[]{:S(2)}, u32[]{:S(2)}) collective-permute-start(bf16[256,384]{1,0:T(8,128)(2,1)S(1)} %add_convert_fusion.2), channel_id=1, source_target_pairs={{0,16},{8,24},{16,0},{24,8},{1,17},{9,25},{17,1},{25,9},{2,18},{10... | collective-permute-start | bytes 589832 | tf_op jit(solution)/shard_map/ppermute | solution.py:236
  122.1 10.5 %collective-permute-start.11 = (f32[256,384]{1,0:T(8,128)S(1)}, f32[256,384]{1,0:T(8,128)S(1)}, u32[]{:S(2)}, u32[]{:S(2)}) collective-permute-start(f32[256,384]{1,0:T(8,128)S(1)} %get-tuple-element.66), channel_id=1, source_target_pairs={{0,1},{1,0},{2,3},{3,2},{4,5},{5,4},{6,7},{7,6},{8,9},{9,8},{10,11... | collective-permute-start | bytes 1179656 | tf_op jit(solution)/shard_map/ppermute | solution.py:236
  122.6 10.0 %collective-permute-start.14 = (bf16[256,384]{1,0:T(8,128)(2,1)S(1)}, bf16[256,384]{1,0:T(8,128)(2,1)S(1)}, u32[]{:S(2)}, u32[]{:S(2)}) collective-permute-start(bf16[256,384]{1,0:T(8,128)(2,1)S(1)} %add_convert_fusion.1), channel_id=1, source_target_pairs={{0,8},{8,16},{16,24},{24,0},{1,9},{9,17},{17,25},{25,1},{2,10},{10... | collective-permute-start | bytes 589832 | tf_op jit(solution)/shard_map/ppermute | solution.py:236
  123.4 9.2 %collective-permute-start.16 = (bf16[256,384]{1,0:T(8,128)(2,1)S(1)}, bf16[256,384]{1,0:T(8,128)(2,1)S(1)}, u32[]{:S(2)}, u32[]{:S(2)}) collective-permute-start(bf16[256,384]{1,0:T(8,128)(2,1)S(1)} %add_convert_fusion), channel_id=1, source_target_pairs={{0,24},{8,0},{16,8},{24,16},{1,25},{9,1},{17,9},{25,17},{2,26},{10... | collective-permute-start | bytes 589832 | tf_op jit(solution)/shard_map/ppermute | solution.py:236

commit v7 on v6

--- a/solution.py
+++ b/solution.py
@@ -102,12 +102,14 @@
             sums_ref[pl.ds(base // LANES + k, 1), :] = to_rows(total[k * LANES : (k + 1) * LANES, :])
 
 
-def second_teacher_kernel(teach_ref, *refs):
-    raw, first_ref, (expo_ref, unit_ref, sums_ref, second_ref) = refs[:NY], refs[NY], refs[NY + 1 :]
-    teacher_kernel(teach_ref, *raw, expo_ref, unit_ref, second_ref)
+def both_teacher_kernel(teach_ref, *refs):
+    near, far, outs = refs[:NY], refs[NY : 2 * NY], refs[2 * NY :]
+    near_ref, near_unit, far_ref, far_unit, sums_ref, near_sums, far_sums = outs
+    teacher_kernel(teach_ref, *near, near_ref, near_unit, near_sums)
+    teacher_kernel(teach_ref, *far, far_ref, far_unit, far_sums)
     core = lax.axis_index("core")
     for peer in range(TGROUP):
-        for which, part_ref in enumerate((first_ref, second_ref)):
+        for which, part_ref in enumerate((near_sums, far_sums)):
             base = pl.multiple_of(own_first(core, which) * HROWS, HROWS)
             sums_ref[peer, pl.ds(base, HROWS), :] = part_ref[...]
 
@@ -265,17 +267,14 @@
 
     square = pltpu.VMEM((HALF, TOK), F32)
     unit_shape = struct((HALF, K), BF16)
-    half_sums = struct((HROWS, LANES), F32)
-    near_expo, near, near_sums = call(
-        teacher_kernel, (square, unit_shape, half_sums), teach, *near
-    )
-    far_expo, far, cols = call(
-        second_teacher_kernel,
-        (square, unit_shape, col_shape),
+    half_sums = pltpu.VMEM((HROWS, LANES), F32)
+    near_expo, near, far_expo, far, cols = call(
+        both_teacher_kernel,
+        (square, unit_shape, square, unit_shape, col_shape),
         teach,
+        *near,
         *far,
-        near_sums,
-        scratch=(pltpu.VMEM((HROWS, LANES), F32),),
+        scratch=(half_sums, half_sums),
     )
     pieces = [stud, got]
     for step in range(ITERS):

time: 134 us -> 134 us (level)
    pallas_call x11 -> x10, Pallas kernels: 13.2 us -> 13.1 us  [call(): pl.pallas_call(kernel, out_shape=out_shape, in_specs=specs or [VMEM] * le...]
where the time goes in v7:
time: 134 us; the launch traced here: 133 us
  blocking collectives  70.4 us (53%)
  starting transfers between devices  35.3 us (26%)
  waiting for transfers between devices  13.5 us (10%)
  Pallas kernels  13.1 us (10%)
    all_to_all x3, blocking collectives, shards(): rows = lax.all_to_all(rows, ('z', 'x'), 0, 0, tiled=True)  41.7 us
    all_to_all x3, blocking collectives, shards(): cols = lax.all_to_all(cols, ('y', 'core'), 0, 0, tiled=True)  28.7 us
    ppermute x14, starting transfers between devices, shift(): return lax.ppermute(x, axis, [(i, (i + step) % size) for i in range(size)])  20.1 us
    pallas_call x10, Pallas kernels, call(): pl.pallas_call(kernel, out_shape=out_shape, in_specs=specs or [VMEM] * le...  13.1 us
    all_to_all x1, starting transfers between devices, shards(): teach = lax.all_to_all(teach, 'z', 0, 0, tiled=True)  9.03 us
    ppermute x14, waiting for transfers between devices, shift(): return lax.ppermute(x, axis, [(i, (i + step) % size) for i in range(size)])  7.97 us
    ppermute x1, starting transfers between devices, shards(): got = lax.ppermute(stud, 'z', [(i, i ^ 4) for i in range(NZ)])  5.37 us
    all_to_all x1, waiting for transfers between devices, shards(): teach = lax.all_to_all(teach, 'z', 0, 0, tiled=True)  3.99 us
  transfers between devices with their start and end apart: 18, of which 5 were waited for; matrix products, arithmetic and copies ran while one was open for 0% of the time, Pallas kernels for 6%

profile of v7, /device:TPU:1, one launch (start us, length us, event | category | flops | bytes accessed | tf_op | source)
XLA Modules:
  0.0 133.3 jit_solution(11294274353995064571)
XLA Ops:
  0.0 2.0 %shard_map.37 = (bf16[8,128,384]{2,1,0:T(8,128)(2,1)}, bf16[128,384]{1,0:T(8,128)(2,1)S(1)}, bf16[256,384]{1,0:T(8,128)(2,1)S(1)}) custom-call(bf16[256,384]{1,0:T(8,128)(2,1)} %teach_hbm.1, bf16[256,384]{1,0:T(8,128)(2,1)} %stud_hbm.1, bf16[256,384]{1,0:T(8,128)(2,1)} %proto_hbm.1), custom_call_target="tpu_custom_call" | custom-call | tf_op jit(solution)/shard_map/pallas_call | solution.py:227
  2.0 9.0 %all-to-all-start = ((bf16[8,128,384]{2,1,0:T(8,128)(2,1)}), bf16[8,128,384]{2,1,0:T(8,128)(2,1)S(1)}, u32[]{:S(2)}, u32[]{:S(2)}) async-start(bf16[8,128,384]{2,1,0:T(8,128)(2,1)} %get-tuple-element.37), calls=%async_computation | async-start | bytes 1572864 | tf_op jit(solution)/shard_map/all_to_all | solution.py:260
  11.0 1.3 collective-permute-start
  12.3 1.5 %collective-permute-start.2 = (bf16[256,384]{1,0:T(8,128)(2,1)}, bf16[256,384]{1,0:T(8,128)(2,1)S(1)}, u32[]{:S(2)}, u32[]{:S(2)}) collective-permute-start(bf16[256,384]{1,0:T(8,128)(2,1)} %proto_hbm.1), channel_id=1, source_target_pairs={{0,24},{8,0},{16,8},{24,16},{1,25},{9,1},{17,9},{25,17},{2,26},{10... | collective-permute-start | bytes 589832 | tf_op jit(solution)/shard_map/ppermute | solution.py:238
  13.8 1.6 %collective-permute-start.1 = (bf16[256,384]{1,0:T(8,128)(2,1)}, bf16[256,384]{1,0:T(8,128)(2,1)S(1)}, u32[]{:S(2)}, u32[]{:S(2)}) collective-permute-start(bf16[256,384]{1,0:T(8,128)(2,1)} %proto_hbm.1), channel_id=1, source_target_pairs={{0,16},{8,24},{16,0},{24,8},{1,17},{9,25},{17,1},{25,9},{2,18},{10... | collective-permute-start | bytes 589832 | tf_op jit(solution)/shard_map/ppermute | solution.py:238
  15.4 1.8 %collective-permute-start.3 = (bf16[256,384]{1,0:T(8,128)(2,1)S(1)}, bf16[256,384]{1,0:T(8,128)(2,1)S(1)}, u32[]{:S(2)}, u32[]{:S(2)}) collective-permute-start(bf16[256,384]{1,0:T(8,128)(2,1)S(1)} %get-tuple-element.38.refs_0_), channel_id=1, source_target_pairs={{0,1},{1,0},{2,3},{3,2},{4,5},{5,4},{6,7},{7,6},{8,9},{9,8},{10,11... | collective-permute-start | bytes 589832 | tf_op jit(solution)/shard_map/ppermute | solution.py:238
  17.2 0.8 collective-permute-done.refs_1_
  18.0 2.1 %collective-permute-start.4 = (bf16[256,384]{1,0:T(8,128)(2,1)S(1)}, bf16[256,384]{1,0:T(8,128)(2,1)S(1)}, u32[]{:S(2)}, u32[]{:S(2)}) collective-permute-start(bf16[256,384]{1,0:T(8,128)(2,1)S(1)} %collective-permute-done.refs_1_), channel_id=1, source_target_pairs={{0,1},{1,0},{2,3},{3,2},{4,5},{5,4},{6,7},{7,6},{8,9},{9,8},{10,11... | collective-permute-start | bytes 589832 | tf_op jit(solution)/shard_map/ppermute | solution.py:238
  20.1 0.0 collective-permute-done.2.refs_3_
  20.1 3.4 %collective-permute-start.6 = (bf16[256,384]{1,0:T(8,128)(2,1)S(1)}, bf16[256,384]{1,0:T(8,128)(2,1)S(1)}, u32[]{:S(2)}, u32[]{:S(2)}) collective-permute-start(bf16[256,384]{1,0:T(8,128)(2,1)S(1)} %collective-permute-done.2.refs_3_), channel_id=1, source_target_pairs={{0,1},{1,0},{2,3},{3,2},{4,5},{5,4},{6,7},{7,6},{8,9},{9,8},{10,11... | collective-permute-start | bytes 589832 | tf_op jit(solution)/shard_map/ppermute | solution.py:238
  23.5 0.0 collective-permute-done.1.refs_2_
  23.5 1.7 %collective-permute-start.5 = (bf16[256,384]{1,0:T(8,128)(2,1)S(1)}, bf16[256,384]{1,0:T(8,128)(2,1)S(1)}, u32[]{:S(2)}, u32[]{:S(2)}) collective-permute-start(bf16[256,384]{1,0:T(8,128)(2,1)S(1)} %collective-permute-done.1.refs_2_), channel_id=1, source_target_pairs={{0,1},{1,0},{2,3},{3,2},{4,5},{5,4},{6,7},{7,6},{8,9},{9,8},{10,11... | collective-permute-start | bytes 589832 | tf_op jit(solution)/shard_map/ppermute | solution.py:238
  25.2 5.4 %collective-permute-start.7 = (bf16[128,384]{1,0:T(8,128)(2,1)S(1)}, bf16[128,384]{1,0:T(8,128)(2,1)S(1)}, u32[]{:S(2)}, u32[]{:S(2)}) collective-permute-start(bf16[128,384]{1,0:T(8,128)(2,1)S(1)} %get-tuple-element.49.refs_0_), channel_id=1, source_target_pairs={{0,128},{32,160},{64,192},{96,224},{128,0},{160,32},{192,64},{224,... | collective-permute-start | bytes 294920 | tf_op jit(solution)/shard_map/ppermute | solution.py:261
  30.6 0.0 collective-permute-done.3.refs_4_
  30.6 0.0 collective-permute-done.4.refs_5_
  30.6 0.0 collective-permute-done.6.refs_7_
  30.6 0.0 collective-permute-done.5.refs_6_
  30.6 4.0 %all-to-all-done.teach_ref = bf16[8,128,384]{2,1,0:T(8,128)(2,1)S(1)} async-done(((bf16[8,128,384]{2,1,0:T(8,128)(2,1)}), bf16[8,128,384]{2,1,0:T(8,128)(2,1)S(1)}, u32[]{:S(2)}, u32[]{:S(2)}) %all-to-all-start) | async-done | bytes 786464 | tf_op jit(solution)/shard_map/all_to_all | solution.py:260
  34.6 2.7 %shard_map.38 = (f32[1024,1024]{1,0:T(8,128)S(1)}, bf16[1024,384]{1,0:T(8,128)(2,1)S(1)}, f32[1024,1024]{1,0:T(8,128)S(1)}, bf16[1024,384]{1,0:T(8,128)(2,1)S(1)}, f32[8,16,128]{2,1,0:T(8,128)S(1)}) custom-call(bf16[8,128,384]{2,1,0:T(8,128)(2,1)S(1)} %all-to-all-done.teach_ref, bf16[256,384]{1,0:T(8,128)(2,1)S(1)} %get-tuple-element.38.refs_0_, ...), custom_call_target="tpu_custom_call" | custom-call | tf_op jit(solution)/shard_map/pallas_call | solution.py:227
  37.3 1.5 %collective-permute-done.7.refs_1_ = bf16[128,384]{1,0:T(8,128)(2,1)S(1)} collective-permute-done((bf16[128,384]{1,0:T(8,128)(2,1)S(1)}, bf16[128,384]{1,0:T(8,128)(2,1)S(1)}, u32[]{:S(2)}, u32[]{:S(2)}) %collective-permute-start.7) | collective-permute-done | bytes 98336 | tf_op jit(solution)/shard_map/ppermute | solution.py:261
  38.8 0.1 collective-permute-start.8
  38.9 9.6 %all_to_all.35.col_sums_ref = f32[8,16,128]{2,1,0:T(8,128)S(1)} all-to-all(f32[8,16,128]{2,1,0:T(8,128)S(1)} %get-tuple-element.44), channel_id=1, replica_groups=mesh['z'=8,'y'=4,'x'=4,'core'=2] {'y','core'}, dimensions={0} | all-to-all | bytes 131072 | tf_op jit(solution)/shard_map/all_to_all | solution.py:287
  48.5 0.6 shard_map.39
  49.2 17.1 %all_to_all.36.row_sums_ref = bf16[32,8,128]{2,1,0:T(8,128)(2,1)S(1)} all-to-all(bf16[32,8,128]{2,1,0:T(8,128)(2,1)S(1)} %shard_map.39), channel_id=1, replica_groups=mesh['z'=8,'y'=4,'x'=4,'core'=2] {'z','x'}, dimensions={0} | all-to-all | bytes 131072 | tf_op jit(solution)/shard_map/all_to_all | solution.py:293
  66.2 0.7 shard_map.40
  66.9 0.0 collective-permute-done.8.refs_2_
  67.0 0.7 collective-permute-start.9
  67.6 9.7 %all_to_all.37.col_sums_ref = f32[8,16,128]{2,1,0:T(8,128)S(1)} all-to-all(f32[8,16,128]{2,1,0:T(8,128)S(1)} %shard_map.40), channel_id=1, replica_groups=mesh['z'=8,'y'=4,'x'=4,'core'=2] {'y','core'}, dimensions={0} | all-to-all | bytes 131072 | tf_op jit(solution)/shard_map/all_to_all | solution.py:287
  77.3 0.6 shard_map.41
  78.0 12.2 %all_to_all.38.row_sums_ref = bf16[32,8,128]{2,1,0:T(8,128)(2,1)S(1)} all-to-all(bf16[32,8,128]{2,1,0:T(8,128)(2,1)S(1)} %shard_map.41), channel_id=1, replica_groups=mesh['z'=8,'y'=4,'x'=4,'core'=2] {'z','x'}, dimensions={0} | all-to-all | bytes 131072 | tf_op jit(solution)/shard_map/all_to_all | solution.py:293
  90.2 0.7 shard_map.42
  90.8 9.4 %all_to_all.39.refs_4_.col_sums_ref = f32[8,16,128]{2,1,0:T(8,128)S(1)} all-to-all(f32[8,16,128]{2,1,0:T(8,128)S(1)} %shard_map.42), channel_id=1, replica_groups=mesh['z'=8,'y'=4,'x'=4,'core'=2] {'y','core'}, dimensions={0} | all-to-all | bytes 131072 | tf_op jit(solution)/shard_map/all_to_all | solution.py:287
  100.3 0.0 collective-permute-done.9.refs_3_
  100.3 2.8 %shard_map.43 = (f32[1024,1024]{1,0:T(8,128)S(1)}, f32[1024,1024]{1,0:T(8,128)S(1)}, bf16[1024,384]{1,0:T(8,128)(2,1)S(1)}, bf16[32,16,128]{2,1,0:T(8,128)(2,1)S(1)}) custom-call(bf16[128,384]{1,0:T(8,128)(2,1)S(1)} %get-tuple-element.49.refs_0_, bf16[128,384]{1,0:T(8,128)(2,1)S(1)} %collective-permute-done.7.refs_1_, ...), custom_call_target="tpu_custom_call" | custom-call | tf_op jit(solution)/shard_map/pallas_call | solution.py:227
  103.1 12.4 %all_to_all.40.row_sums_ref = bf16[32,16,128]{2,1,0:T(8,128)(2,1)S(1)} all-to-all(bf16[32,16,128]{2,1,0:T(8,128)(2,1)S(1)} %get-tuple-element.56), channel_id=1, replica_groups=mesh['z'=8,'y'=4,'x'=4,'core'=2] {'z','x'}, dimensions={0} | all-to-all | bytes 262144 | tf_op jit(solution)/shard_map/all_to_all | solution.py:311
  115.5 0.5 shard_map.44
  116.0 2.0 %collective-permute-start.10 = (f32[256,384]{1,0:T(8,128)S(1)}, f32[256,384]{1,0:T(8,128)S(1)}, u32[]{:S(2)}, u32[]{:S(2)}) collective-permute-start(f32[256,384]{1,0:T(8,128)S(1)} %shard_map.44), channel_id=1, source_target_pairs={{0,1},{1,0},{2,3},{3,2},{4,5},{5,4},{6,7},{7,6},{8,9},{9,8},{10,11... | collective-permute-start | bytes 1179656 | tf_op jit(solution)/shard_map/ppermute | solution.py:238
  118.0 1.1 shard_map.45
  119.1 0.1 collective-permute-start.13
  119.2 0.5 collective-permute-start.15
  119.7 0.0 collective-permute-done.10
  119.8 0.8 collective-permute-start.12
  120.6 1.3 %shard_map.46 = (f32[256,384]{1,0:T(8,128)S(1)}, f32[256,384]{1,0:T(8,128)S(1)}, f32[256,384]{1,0:T(8,128)S(1)}, f32[256,384]{1,0:T(8,128)S(1)}) custom-call(f32[8,16,128]{2,1,0:T(8,128)S(1)} %all_to_all.39.refs_4_.col_sums_ref, bf16[32,16,128]{2,1,0:T(8,128)(2,1)S(1)} %all_to_all.40.row_sums_ref, bf16[1024,384]{1,0:T(8,128)(2,1)S(1)} %get-tuple-element.57.stud_ref, ...), custom_call_target="tpu_custom_call" | custom-call | tf_op jit(solution)/shard_map/pallas_call | solution.py:227
  121.9 0.5 collective-permute-start.11
  122.4 0.0 collective-permute-done.13
  122.4 0.8 collective-permute-start.14
  123.2 0.0 collective-permute-done.15
  123.3 2.0 %collective-permute-start.16 = (bf16[256,384]{1,0:T(8,128)(2,1)S(1)}, bf16[256,384]{1,0:T(8,128)(2,1)S(1)}, u32[]{:S(2)}, u32[]{:S(2)}) collective-permute-start(bf16[256,384]{1,0:T(8,128)(2,1)S(1)} %add_convert_fusion), channel_id=1, source_target_pairs={{0,24},{8,0},{16,8},{24,16},{1,25},{9,1},{17,9},{25,17},{2,26},{10... | collective-permute-start | bytes 589832 | tf_op jit(solution)/shard_map/ppermute | solution.py:238
  125.3 2.5 %collective-permute-done.12 = bf16[256,384]{1,0:T(8,128)(2,1)S(1)} collective-permute-done((bf16[256,384]{1,0:T(8,128)(2,1)S(1)}, bf16[256,384]{1,0:T(8,128)(2,1)S(1)}, u32[]{:S(2)}, u32[]{:S(2)}) %collective-permute-start.12) | collective-permute-done | bytes 196640 | tf_op jit(solution)/shard_map/ppermute | solution.py:238
  127.8 4.6 %collective-permute-done.14 = bf16[256,384]{1,0:T(8,128)(2,1)S(1)} collective-permute-done((bf16[256,384]{1,0:T(8,128)(2,1)S(1)}, bf16[256,384]{1,0:T(8,128)(2,1)S(1)}, u32[]{:S(2)}, u32[]{:S(2)}) %collective-permute-start.14) | collective-permute-done | bytes 196640 | tf_op jit(solution)/shard_map/ppermute | solution.py:238
  132.4 0.0 collective-permute-done.16
  132.4 0.0 collective-permute-done.11
  132.5 0.8 convert_add_fusion
  (5 shorter events, 0.2 us)
Async XLA Ops:
  2.0 32.6 %all-to-all-start = ((bf16[8,128,384]{2,1,0:T(8,128)(2,1)}), bf16[8,128,384]{2,1,0:T(8,128)(2,1)S(1)}, u32[]{:S(2)}, u32[]{:S(2)}) async-start(bf16[8,128,384]{2,1,0:T(8,128)(2,1)} %get-tuple-element.37), calls=%async_computation | async-start | bytes 1572864 | tf_op jit(solution)/shard_map/all_to_all | solution.py:260
  11.0 7.0 %collective-permute-start = (bf16[256,384]{1,0:T(8,128)(2,1)}, bf16[256,384]{1,0:T(8,128)(2,1)S(1)}, u32[]{:S(2)}, u32[]{:S(2)}) collective-permute-start(bf16[256,384]{1,0:T(8,128)(2,1)} %proto_hbm.1), channel_id=1, source_target_pairs={{0,8},{8,16},{16,24},{24,0},{1,9},{9,17},{17,25},{25,1},{2,10},{10... | collective-permute-start | bytes 589832 | tf_op jit(solution)/shard_map/ppermute | solution.py:238
  12.3 7.8 %collective-permute-start.2 = (bf16[256,384]{1,0:T(8,128)(2,1)}, bf16[256,384]{1,0:T(8,128)(2,1)S(1)}, u32[]{:S(2)}, u32[]{:S(2)}) collective-permute-start(bf16[256,384]{1,0:T(8,128)(2,1)} %proto_hbm.1), channel_id=1, source_target_pairs={{0,24},{8,0},{16,8},{24,16},{1,25},{9,1},{17,9},{25,17},{2,26},{10... | collective-permute-start | bytes 589832 | tf_op jit(solution)/shard_map/ppermute | solution.py:238
  13.8 9.7 %collective-permute-start.1 = (bf16[256,384]{1,0:T(8,128)(2,1)}, bf16[256,384]{1,0:T(8,128)(2,1)S(1)}, u32[]{:S(2)}, u32[]{:S(2)}) collective-permute-start(bf16[256,384]{1,0:T(8,128)(2,1)} %proto_hbm.1), channel_id=1, source_target_pairs={{0,16},{8,24},{16,0},{24,8},{1,17},{9,25},{17,1},{25,9},{2,18},{10... | collective-permute-start | bytes 589832 | tf_op jit(solution)/shard_map/ppermute | solution.py:238
  15.4 15.2 %collective-permute-start.3 = (bf16[256,384]{1,0:T(8,128)(2,1)S(1)}, bf16[256,384]{1,0:T(8,128)(2,1)S(1)}, u32[]{:S(2)}, u32[]{:S(2)}) collective-permute-start(bf16[256,384]{1,0:T(8,128)(2,1)S(1)} %get-tuple-element.38.refs_0_), channel_id=1, source_target_pairs={{0,1},{1,0},{2,3},{3,2},{4,5},{5,4},{6,7},{7,6},{8,9},{9,8},{10,11... | collective-permute-start | bytes 589832 | tf_op jit(solution)/shard_map/ppermute | solution.py:238
  18.0 12.6 %collective-permute-start.4 = (bf16[256,384]{1,0:T(8,128)(2,1)S(1)}, bf16[256,384]{1,0:T(8,128)(2,1)S(1)}, u32[]{:S(2)}, u32[]{:S(2)}) collective-permute-start(bf16[256,384]{1,0:T(8,128)(2,1)S(1)} %collective-permute-done.refs_1_), channel_id=1, source_target_pairs={{0,1},{1,0},{2,3},{3,2},{4,5},{5,4},{6,7},{7,6},{8,9},{9,8},{10,11... | collective-permute-start | bytes 589832 | tf_op jit(solution)/shard_map/ppermute | solution.py:238
  20.1 10.5 %collective-permute-start.6 = (bf16[256,384]{1,0:T(8,128)(2,1)S(1)}, bf16[256,384]{1,0:T(8,128)(2,1)S(1)}, u32[]{:S(2)}, u32[]{:S(2)}) collective-permute-start(bf16[256,384]{1,0:T(8,128)(2,1)S(1)} %collective-permute-done.2.refs_3_), channel_id=1, source_target_pairs={{0,1},{1,0},{2,3},{3,2},{4,5},{5,4},{6,7},{7,6},{8,9},{9,8},{10,11... | collective-permute-start | bytes 589832 | tf_op jit(solution)/shard_map/ppermute | solution.py:238
  23.5 7.1 %collective-permute-start.5 = (bf16[256,384]{1,0:T(8,128)(2,1)S(1)}, bf16[256,384]{1,0:T(8,128)(2,1)S(1)}, u32[]{:S(2)}, u32[]{:S(2)}) collective-permute-start(bf16[256,384]{1,0:T(8,128)(2,1)S(1)} %collective-permute-done.1.refs_2_), channel_id=1, source_target_pairs={{0,1},{1,0},{2,3},{3,2},{4,5},{5,4},{6,7},{7,6},{8,9},{9,8},{10,11... | collective-permute-start | bytes 589832 | tf_op jit(solution)/shard_map/ppermute | solution.py:238
  25.2 13.6 %collective-permute-start.7 = (bf16[128,384]{1,0:T(8,128)(2,1)S(1)}, bf16[128,384]{1,0:T(8,128)(2,1)S(1)}, u32[]{:S(2)}, u32[]{:S(2)}) collective-permute-start(bf16[128,384]{1,0:T(8,128)(2,1)S(1)} %get-tuple-element.49.refs_0_), channel_id=1, source_target_pairs={{0,128},{32,160},{64,192},{96,224},{128,0},{160,32},{192,64},{224,... | collective-permute-start | bytes 294920 | tf_op jit(solution)/shard_map/ppermute | solution.py:261
  38.8 28.1 %collective-permute-start.8 = (bf16[256,384]{1,0:T(8,128)(2,1)S(1)}, bf16[256,384]{1,0:T(8,128)(2,1)S(1)}, u32[]{:S(2)}, u32[]{:S(2)}) collective-permute-start(bf16[256,384]{1,0:T(8,128)(2,1)S(1)} %pad_maximum_fusion.1), channel_id=1, source_target_pairs={{0,64},{32,96},{64,0},{96,32},{128,192},{160,224},{192,128},{224,1... | collective-permute-start | bytes 589832 | tf_op jit(solution)/shard_map/ppermute | solution.py:286
  67.0 33.3 %collective-permute-start.9 = (bf16[512,384]{1,0:T(8,128)(2,1)S(1)}, bf16[512,384]{1,0:T(8,128)(2,1)S(1)}, u32[]{:S(2)}, u32[]{:S(2)}) collective-permute-start(bf16[512,384]{1,0:T(8,128)(2,1)S(1)} %pad_maximum_fusion), channel_id=1, source_target_pairs={{0,32},{32,0},{64,96},{96,64},{128,160},{160,128},{192,224},{224,1... | collective-permute-start | bytes 1179656 | tf_op jit(solution)/shard_map/ppermute | solution.py:286
  116.0 3.7 %collective-permute-start.10 = (f32[256,384]{1,0:T(8,128)S(1)}, f32[256,384]{1,0:T(8,128)S(1)}, u32[]{:S(2)}, u32[]{:S(2)}) collective-permute-start(f32[256,384]{1,0:T(8,128)S(1)} %shard_map.44), channel_id=1, source_target_pairs={{0,1},{1,0},{2,3},{3,2},{4,5},{5,4},{6,7},{7,6},{8,9},{9,8},{10,11... | collective-permute-start | bytes 1179656 | tf_op jit(solution)/shard_map/ppermute | solution.py:238
  119.1 3.3 %collective-permute-start.13 = (f32[256,384]{1,0:T(8,128)S(1)}, f32[256,384]{1,0:T(8,128)S(1)}, u32[]{:S(2)}, u32[]{:S(2)}) collective-permute-start(f32[256,384]{1,0:T(8,128)S(1)} %get-tuple-element.66), channel_id=1, source_target_pairs={{0,1},{1,0},{2,3},{3,2},{4,5},{5,4},{6,7},{7,6},{8,9},{9,8},{10,11... | collective-permute-start | bytes 1179656 | tf_op jit(solution)/shard_map/ppermute | solution.py:238
  119.2 4.0 %collective-permute-start.15 = (f32[256,384]{1,0:T(8,128)S(1)}, f32[256,384]{1,0:T(8,128)S(1)}, u32[]{:S(2)}, u32[]{:S(2)}) collective-permute-start(f32[256,384]{1,0:T(8,128)S(1)} %get-tuple-element.68), channel_id=1, source_target_pairs={{0,1},{1,0},{2,3},{3,2},{4,5},{5,4},{6,7},{7,6},{8,9},{9,8},{10,11... | collective-permute-start | bytes 1179656 | tf_op jit(solution)/shard_map/ppermute | solution.py:238
  119.8 8.1 %collective-permute-start.12 = (bf16[256,384]{1,0:T(8,128)(2,1)S(1)}, bf16[256,384]{1,0:T(8,128)(2,1)S(1)}, u32[]{:S(2)}, u32[]{:S(2)}) collective-permute-start(bf16[256,384]{1,0:T(8,128)(2,1)S(1)} %add_convert_fusion.2), channel_id=1, source_target_pairs={{0,16},{8,24},{16,0},{24,8},{1,17},{9,25},{17,1},{25,9},{2,18},{10... | collective-permute-start | bytes 589832 | tf_op jit(solution)/shard_map/ppermute | solution.py:238
  121.9 10.5 %collective-permute-start.11 = (f32[256,384]{1,0:T(8,128)S(1)}, f32[256,384]{1,0:T(8,128)S(1)}, u32[]{:S(2)}, u32[]{:S(2)}) collective-permute-start(f32[256,384]{1,0:T(8,128)S(1)} %get-tuple-element.64), channel_id=1, source_target_pairs={{0,1},{1,0},{2,3},{3,2},{4,5},{5,4},{6,7},{7,6},{8,9},{9,8},{10,11... | collective-permute-start | bytes 1179656 | tf_op jit(solution)/shard_map/ppermute | solution.py:238
  122.4 10.0 %collective-permute-start.14 = (bf16[256,384]{1,0:T(8,128)(2,1)S(1)}, bf16[256,384]{1,0:T(8,128)(2,1)S(1)}, u32[]{:S(2)}, u32[]{:S(2)}) collective-permute-start(bf16[256,384]{1,0:T(8,128)(2,1)S(1)} %add_convert_fusion.1), channel_id=1, source_target_pairs={{0,8},{8,16},{16,24},{24,0},{1,9},{9,17},{17,25},{25,1},{2,10},{10... | collective-permute-start | bytes 589832 | tf_op jit(solution)/shard_map/ppermute | solution.py:238
  123.3 9.2 %collective-permute-start.16 = (bf16[256,384]{1,0:T(8,128)(2,1)S(1)}, bf16[256,384]{1,0:T(8,128)(2,1)S(1)}, u32[]{:S(2)}, u32[]{:S(2)}) collective-permute-start(bf16[256,384]{1,0:T(8,128)(2,1)S(1)} %add_convert_fusion), channel_id=1, source_target_pairs={{0,24},{8,0},{16,8},{24,16},{1,25},{9,1},{17,9},{25,17},{2,26},{10... | collective-permute-start | bytes 589832 | tf_op jit(solution)/shard_map/ppermute | solution.py:238

commit v8 on v7

--- a/solution.py
+++ b/solution.py
@@ -104,38 +104,35 @@
 
 def both_teacher_kernel(teach_ref, *refs):
     near, far, outs = refs[:NY], refs[NY : 2 * NY], refs[2 * NY :]
-    near_ref, near_unit, far_ref, far_unit, sums_ref, near_sums, far_sums = outs
+    near_ref, near_unit, far_ref, far_unit, sums_ref, near_sums, far_sums, all_ref = outs
     teacher_kernel(teach_ref, *near, near_ref, near_unit, near_sums)
     teacher_kernel(teach_ref, *far, far_ref, far_unit, far_sums)
     core = lax.axis_index("core")
+    for which, part_ref in enumerate((near_sums, far_sums)):
+        base = pl.multiple_of(own_first(core, which) * HROWS, HROWS)
+        all_ref[pl.ds(base, HROWS), :] = part_ref[...]
+    spread_sums(all_ref, sums_ref)
+
+
+def spread_sums(all_ref, sums_ref):
+    sums = all_ref[...].astype(sums_ref.dtype)
     for peer in range(TGROUP):
-        for which, part_ref in enumerate((near_sums, far_sums)):
-            base = pl.multiple_of(own_first(core, which) * HROWS, HROWS)
-            sums_ref[peer, pl.ds(base, HROWS), :] = part_ref[...]
-
-
-def col_sums(expo_refs, weights, sums_ref):
+        sums_ref[peer] = sums
+
+
+def col_kernel(row_sums_ref, first_ref, second_ref, sums_ref, all_ref):
+    weights = 1.0 / jnp.sum(row_sums_ref[...].astype(F32), axis=0)
     core = lax.axis_index("core")
-    for which, expo_ref in enumerate(expo_refs):
+    for which, expo_ref in enumerate((first_ref, second_ref)):
         base = own_first(core, which) * HROWS
-
-        def group(i, carry):
-            rows = pl.ds(pl.multiple_of(i * LANES, LANES), LANES)
+        for i in range(HROWS):
+            rows = slice(i * LANES, (i + 1) * LANES)
             total = None
             for j in range(TROWS):
                 term = expo_ref[rows, j * LANES : (j + 1) * LANES] * weights[j : j + 1, :]
                 total = term if total is None else total + term
-            sums_ref[0, pl.ds(base + i, 1), :] = to_rows(total)
-            return carry
-
-        lax.fori_loop(0, HROWS, group, 0, unroll=True)
-    for peer in range(1, TGROUP):
-        sums_ref[peer] = sums_ref[0]
-
-
-def col_kernel(row_sums_ref, first_ref, second_ref, sums_ref):
-    weights = 1.0 / jnp.sum(row_sums_ref[...].astype(F32), axis=0)
-    col_sums((first_ref, second_ref), weights, sums_ref)
+            all_ref[pl.ds(base + i, 1), :] = to_rows(total)
+    spread_sums(all_ref, sums_ref)
 
 
 def row_sums(expo_refs, weights_ref):
@@ -158,7 +155,7 @@
 
 
 def row_kernel(col_sums_ref, first_ref, second_ref, sums_ref, weights_ref):
-    weights_ref[...] = 1.0 / jnp.sum(col_sums_ref[...], axis=0)
+    weights_ref[...] = 1.0 / jnp.sum(col_sums_ref[...].astype(F32), axis=0)
     sums = row_sums((first_ref, second_ref), weights_ref).astype(BF16)
     for peer in range(PGROUP):
         sums_ref[peer] = sums
@@ -177,7 +174,7 @@
         if hop:
             offsets = offsets + hops
     stud = stud_out[...]
-    weights_ref[...] = 1.0 / jnp.sum(col_sums_ref[...], axis=0)
+    weights_ref[...] = 1.0 / jnp.sum(col_sums_ref[...].astype(F32), axis=0)
     totals = [jnp.zeros((8, LANES), F32)] * TROWS
     for i in range(PRO // PRO_BLOCK):
         proto_ref, expz_ref = protos[i // NY], expzs[i // NY]
@@ -199,7 +196,7 @@
 def grad_kernel(tasks, col_sums_ref, row_sums_ref, stud_ref, *refs):
     expos, expzs, outs, weights_ref = refs[:2], refs[2:4], refs[4:-1], refs[-1]
     core = lax.axis_index("core")
-    weights_ref[...] = 1.0 / jnp.sum(col_sums_ref[...], axis=0)
+    weights_ref[...] = 1.0 / jnp.sum(col_sums_ref[...].astype(F32), axis=0)
     totals = jnp.sum(row_sums_ref[...].astype(F32), axis=0)
     target_scale = SCALE / totals[:TROWS]
     prob_scale = SCALE / totals[TROWS:]
@@ -261,7 +258,8 @@
     got = lax.ppermute(stud, "z", [(i, i ^ 4) for i in range(NZ)])
     far = [shift(proto, "core", NC, 1) for proto in near]
 
-    col_shape = struct((TGROUP, PROWS, LANES), F32)
+    col_shape = struct((TGROUP, PROWS, LANES), BF16)
+    last_col_shape = struct((TGROUP, PROWS, LANES), F32)
     row_shape = struct((PGROUP, TROWS, LANES), BF16)
     weights = pltpu.VMEM((PROWS, LANES), F32)
 
@@ -274,7 +272,7 @@
         teach,
         *near,
         *far,
-        scratch=(half_sums, half_sums),
+        scratch=(half_sums, half_sums, weights),
     )
     pieces = [stud, got]
     for step in range(ITERS):
@@ -291,7 +289,14 @@
                 row_kernel, row_shape, cols, pinned(near_expo), pinned(far_expo), scratch=(weights,)
             )
             rows = lax.all_to_all(rows, ("z", "x"), 0, 0, tiled=True)
-            cols = call(col_kernel, col_shape, rows, pinned(near_expo), pinned(far_expo))
+            cols = call(
+                col_kernel,
+                last_col_shape if step + 2 == ITERS else col_shape,
+                rows,
+                pinned(near_expo),
+                pinned(far_expo),
+                scratch=(weights,),
+            )
     near_expz, far_expz, stud, rows = call(
         last_row_kernel,
         (

time: 134 us -> 133 us (level)
  no operation moved by 1% of the time
where the time goes in v8:
time: 133 us
  blocking collectives  70 us (53%)
  starting transfers between devices  35.2 us (26%)
  waiting for transfers between devices  13.5 us (10%)
  Pallas kernels  13.1 us (10%)
    all_to_all x3, blocking collectives, shards(): rows = lax.all_to_all(rows, ('z', 'x'), 0, 0, tiled=True)  41.7 us
    all_to_all x3, blocking collectives, shards(): cols = lax.all_to_all(cols, ('y', 'core'), 0, 0, tiled=True)  28.4 us
    ppermute x14, starting transfers between devices, shift(): return lax.ppermute(x, axis, [(i, (i + step) % size) for i in range(size)])  20.1 us
    pallas_call x10, Pallas kernels, call(): pl.pallas_call(kernel, out_shape=out_shape, in_specs=specs or [VMEM] * le...  13.1 us
    all_to_all x1, starting transfers between devices, shards(): teach = lax.all_to_all(teach, 'z', 0, 0, tiled=True)  9.03 us
    ppermute x14, waiting for transfers between devices, shift(): return lax.ppermute(x, axis, [(i, (i + step) % size) for i in range(size)])  8.03 us
    ppermute x1, starting transfers between devices, shards(): got = lax.ppermute(stud, 'z', [(i, i ^ 4) for i in range(NZ)])  5.37 us
    all_to_all x1, waiting for transfers between devices, shards(): teach = lax.all_to_all(teach, 'z', 0, 0, tiled=True)  3.99 us
  transfers between devices with their start and end apart: 18, of which 5 were waited for; matrix products, arithmetic and copies ran while one was open for 0% of the time, Pallas kernels for 6%

profile of v8, /device:TPU:1, one launch (start us, length us, event | category | flops | bytes accessed | tf_op | source)
XLA Modules:
  0.0 132.9 jit_solution(16064424119285511114)
XLA Ops:
  0.0 2.0 %shard_map.37 = (bf16[8,128,384]{2,1,0:T(8,128)(2,1)}, bf16[128,384]{1,0:T(8,128)(2,1)S(1)}, bf16[256,384]{1,0:T(8,128)(2,1)S(1)}) custom-call(bf16[256,384]{1,0:T(8,128)(2,1)} %teach_hbm.1, bf16[256,384]{1,0:T(8,128)(2,1)} %stud_hbm.1, bf16[256,384]{1,0:T(8,128)(2,1)} %proto_hbm.1), custom_call_target="tpu_custom_call" | custom-call | tf_op jit(solution)/shard_map/pallas_call | solution.py:224
  2.0 9.0 %all-to-all-start = ((bf16[8,128,384]{2,1,0:T(8,128)(2,1)}), bf16[8,128,384]{2,1,0:T(8,128)(2,1)S(1)}, u32[]{:S(2)}, u32[]{:S(2)}) async-start(bf16[8,128,384]{2,1,0:T(8,128)(2,1)} %get-tuple-element.37), calls=%async_computation | async-start | bytes 1572864 | tf_op jit(solution)/shard_map/all_to_all | solution.py:257
  11.0 1.3 collective-permute-start
  12.3 1.5 %collective-permute-start.2 = (bf16[256,384]{1,0:T(8,128)(2,1)}, bf16[256,384]{1,0:T(8,128)(2,1)S(1)}, u32[]{:S(2)}, u32[]{:S(2)}) collective-permute-start(bf16[256,384]{1,0:T(8,128)(2,1)} %proto_hbm.1), channel_id=1, source_target_pairs={{0,24},{8,0},{16,8},{24,16},{1,25},{9,1},{17,9},{25,17},{2,26},{10... | collective-permute-start | bytes 589832 | tf_op jit(solution)/shard_map/ppermute | solution.py:235
  13.8 1.6 %collective-permute-start.1 = (bf16[256,384]{1,0:T(8,128)(2,1)}, bf16[256,384]{1,0:T(8,128)(2,1)S(1)}, u32[]{:S(2)}, u32[]{:S(2)}) collective-permute-start(bf16[256,384]{1,0:T(8,128)(2,1)} %proto_hbm.1), channel_id=1, source_target_pairs={{0,16},{8,24},{16,0},{24,8},{1,17},{9,25},{17,1},{25,9},{2,18},{10... | collective-permute-start | bytes 589832 | tf_op jit(solution)/shard_map/ppermute | solution.py:235
  15.4 1.8 %collective-permute-start.3 = (bf16[256,384]{1,0:T(8,128)(2,1)S(1)}, bf16[256,384]{1,0:T(8,128)(2,1)S(1)}, u32[]{:S(2)}, u32[]{:S(2)}) collective-permute-start(bf16[256,384]{1,0:T(8,128)(2,1)S(1)} %get-tuple-element.38.refs_0_), channel_id=1, source_target_pairs={{0,1},{1,0},{2,3},{3,2},{4,5},{5,4},{6,7},{7,6},{8,9},{9,8},{10,11... | collective-permute-start | bytes 589832 | tf_op jit(solution)/shard_map/ppermute | solution.py:235
  17.2 0.8 collective-permute-done.refs_1_
  18.0 2.1 %collective-permute-start.4 = (bf16[256,384]{1,0:T(8,128)(2,1)S(1)}, bf16[256,384]{1,0:T(8,128)(2,1)S(1)}, u32[]{:S(2)}, u32[]{:S(2)}) collective-permute-start(bf16[256,384]{1,0:T(8,128)(2,1)S(1)} %collective-permute-done.refs_1_), channel_id=1, source_target_pairs={{0,1},{1,0},{2,3},{3,2},{4,5},{5,4},{6,7},{7,6},{8,9},{9,8},{10,11... | collective-permute-start | bytes 589832 | tf_op jit(solution)/shard_map/ppermute | solution.py:235
  20.1 0.0 collective-permute-done.2.refs_3_
  20.1 3.4 %collective-permute-start.6 = (bf16[256,384]{1,0:T(8,128)(2,1)S(1)}, bf16[256,384]{1,0:T(8,128)(2,1)S(1)}, u32[]{:S(2)}, u32[]{:S(2)}) collective-permute-start(bf16[256,384]{1,0:T(8,128)(2,1)S(1)} %collective-permute-done.2.refs_3_), channel_id=1, source_target_pairs={{0,1},{1,0},{2,3},{3,2},{4,5},{5,4},{6,7},{7,6},{8,9},{9,8},{10,11... | collective-permute-start | bytes 589832 | tf_op jit(solution)/shard_map/ppermute | solution.py:235
  23.5 0.0 collective-permute-done.1.refs_2_
  23.5 1.7 %collective-permute-start.5 = (bf16[256,384]{1,0:T(8,128)(2,1)S(1)}, bf16[256,384]{1,0:T(8,128)(2,1)S(1)}, u32[]{:S(2)}, u32[]{:S(2)}) collective-permute-start(bf16[256,384]{1,0:T(8,128)(2,1)S(1)} %collective-permute-done.1.refs_2_), channel_id=1, source_target_pairs={{0,1},{1,0},{2,3},{3,2},{4,5},{5,4},{6,7},{7,6},{8,9},{9,8},{10,11... | collective-permute-start | bytes 589832 | tf_op jit(solution)/shard_map/ppermute | solution.py:235
  25.2 5.4 %collective-permute-start.7 = (bf16[128,384]{1,0:T(8,128)(2,1)S(1)}, bf16[128,384]{1,0:T(8,128)(2,1)S(1)}, u32[]{:S(2)}, u32[]{:S(2)}) collective-permute-start(bf16[128,384]{1,0:T(8,128)(2,1)S(1)} %get-tuple-element.49.refs_0_), channel_id=1, source_target_pairs={{0,128},{32,160},{64,192},{96,224},{128,0},{160,32},{192,64},{224,... | collective-permute-start | bytes 294920 | tf_op jit(solution)/shard_map/ppermute | solution.py:258
  30.6 0.0 collective-permute-done.3.refs_4_
  30.6 0.0 collective-permute-done.4.refs_5_
  30.6 0.0 collective-permute-done.6.refs_7_
  30.6 0.0 collective-permute-done.5.refs_6_
  30.6 4.0 %all-to-all-done.teach_ref = bf16[8,128,384]{2,1,0:T(8,128)(2,1)S(1)} async-done(((bf16[8,128,384]{2,1,0:T(8,128)(2,1)}), bf16[8,128,384]{2,1,0:T(8,128)(2,1)S(1)}, u32[]{:S(2)}, u32[]{:S(2)}) %all-to-all-start) | async-done | bytes 786464 | tf_op jit(solution)/shard_map/all_to_all | solution.py:257
  34.6 2.8 %shard_map.38 = (f32[1024,1024]{1,0:T(8,128)S(1)}, bf16[1024,384]{1,0:T(8,128)(2,1)S(1)}, f32[1024,1024]{1,0:T(8,128)S(1)}, bf16[1024,384]{1,0:T(8,128)(2,1)S(1)}, bf16[8,16,128]{2,1,0:T(8,128)(2,1)S(1)}) custom-call(bf16[8,128,384]{2,1,0:T(8,128)(2,1)S(1)} %all-to-all-done.teach_ref, bf16[256,384]{1,0:T(8,128)(2,1)S(1)} %get-tuple-element.38.refs_0_, ...), custom_call_target="tpu_custom_call" | custom-call | tf_op jit(solution)/shard_map/pallas_call | solution.py:224
  37.3 1.5 %collective-permute-done.7.refs_1_ = bf16[128,384]{1,0:T(8,128)(2,1)S(1)} collective-permute-done((bf16[128,384]{1,0:T(8,128)(2,1)S(1)}, bf16[128,384]{1,0:T(8,128)(2,1)S(1)}, u32[]{:S(2)}, u32[]{:S(2)}) %collective-permute-start.7) | collective-permute-done | bytes 98336 | tf_op jit(solution)/shard_map/ppermute | solution.py:258
  38.8 0.1 collective-permute-start.8
  38.9 9.5 %all_to_all.35.col_sums_ref = bf16[8,16,128]{2,1,0:T(8,128)(2,1)S(1)} all-to-all(bf16[8,16,128]{2,1,0:T(8,128)(2,1)S(1)} %get-tuple-element.44), channel_id=1, replica_groups=mesh['z'=8,'y'=4,'x'=4,'core'=2] {'y','core'}, dimensions={0} | all-to-all | bytes 65536 | tf_op jit(solution)/shard_map/all_to_all | solution.py:285
  48.4 0.6 shard_map.39
  49.1 17.1 %all_to_all.36.row_sums_ref = bf16[32,8,128]{2,1,0:T(8,128)(2,1)S(1)} all-to-all(bf16[32,8,128]{2,1,0:T(8,128)(2,1)S(1)} %shard_map.39), channel_id=1, replica_groups=mesh['z'=8,'y'=4,'x'=4,'core'=2] {'z','x'}, dimensions={0} | all-to-all | bytes 131072 | tf_op jit(solution)/shard_map/all_to_all | solution.py:291
  66.1 0.7 shard_map.40
  66.8 0.0 collective-permute-done.8.refs_2_
  66.8 0.7 collective-permute-start.9
  67.5 9.5 %all_to_all.37.col_sums_ref = bf16[8,16,128]{2,1,0:T(8,128)(2,1)S(1)} all-to-all(bf16[8,16,128]{2,1,0:T(8,128)(2,1)S(1)} %shard_map.40), channel_id=1, replica_groups=mesh['z'=8,'y'=4,'x'=4,'core'=2] {'y','core'}, dimensions={0} | all-to-all | bytes 65536 | tf_op jit(solution)/shard_map/all_to_all | solution.py:285
  77.0 0.6 shard_map.41
  77.7 12.2 %all_to_all.38.row_sums_ref = bf16[32,8,128]{2,1,0:T(8,128)(2,1)S(1)} all-to-all(bf16[32,8,128]{2,1,0:T(8,128)(2,1)S(1)} %shard_map.41), channel_id=1, replica_groups=mesh['z'=8,'y'=4,'x'=4,'core'=2] {'z','x'}, dimensions={0} | all-to-all | bytes 131072 | tf_op jit(solution)/shard_map/all_to_all | solution.py:291
  89.9 0.7 shard_map.42
  90.5 9.4 %all_to_all.39.refs_4_.col_sums_ref = f32[8,16,128]{2,1,0:T(8,128)S(1)} all-to-all(f32[8,16,128]{2,1,0:T(8,128)S(1)} %shard_map.42), channel_id=1, replica_groups=mesh['z'=8,'y'=4,'x'=4,'core'=2] {'y','core'}, dimensions={0} | all-to-all | bytes 131072 | tf_op jit(solution)/shard_map/all_to_all | solution.py:285
  99.9 0.0 collective-permute-done.9.refs_3_
  99.9 2.8 %shard_map.43 = (f32[1024,1024]{1,0:T(8,128)S(1)}, f32[1024,1024]{1,0:T(8,128)S(1)}, bf16[1024,384]{1,0:T(8,128)(2,1)S(1)}, bf16[32,16,128]{2,1,0:T(8,128)(2,1)S(1)}) custom-call(bf16[128,384]{1,0:T(8,128)(2,1)S(1)} %get-tuple-element.49.refs_0_, bf16[128,384]{1,0:T(8,128)(2,1)S(1)} %collective-permute-done.7.refs_1_, ...), custom_call_target="tpu_custom_call" | custom-call | tf_op jit(solution)/shard_map/pallas_call | solution.py:224
  102.8 12.4 %all_to_all.40.row_sums_ref = bf16[32,16,128]{2,1,0:T(8,128)(2,1)S(1)} all-to-all(bf16[32,16,128]{2,1,0:T(8,128)(2,1)S(1)} %get-tuple-element.56), channel_id=1, replica_groups=mesh['z'=8,'y'=4,'x'=4,'core'=2] {'z','x'}, dimensions={0} | all-to-all | bytes 262144 | tf_op jit(solution)/shard_map/all_to_all | solution.py:316
  115.1 0.5 shard_map.44
  115.7 2.0 %collective-permute-start.10 = (f32[256,384]{1,0:T(8,128)S(1)}, f32[256,384]{1,0:T(8,128)S(1)}, u32[]{:S(2)}, u32[]{:S(2)}) collective-permute-start(f32[256,384]{1,0:T(8,128)S(1)} %shard_map.44), channel_id=1, source_target_pairs={{0,1},{1,0},{2,3},{3,2},{4,5},{5,4},{6,7},{7,6},{8,9},{9,8},{10,11... | collective-permute-start | bytes 1179656 | tf_op jit(solution)/shard_map/ppermute | solution.py:235
  117.7 1.1 shard_map.45
  118.8 0.1 collective-permute-start.13
  118.9 0.5 collective-permute-start.15
  119.4 0.0 collective-permute-done.10
  119.4 0.8 collective-permute-start.12
  120.2 1.3 %shard_map.46 = (f32[256,384]{1,0:T(8,128)S(1)}, f32[256,384]{1,0:T(8,128)S(1)}, f32[256,384]{1,0:T(8,128)S(1)}, f32[256,384]{1,0:T(8,128)S(1)}) custom-call(f32[8,16,128]{2,1,0:T(8,128)S(1)} %all_to_all.39.refs_4_.col_sums_ref, bf16[32,16,128]{2,1,0:T(8,128)(2,1)S(1)} %all_to_all.40.row_sums_ref, bf16[1024,384]{1,0:T(8,128)(2,1)S(1)} %get-tuple-element.57.stud_ref, ...), custom_call_target="tpu_custom_call" | custom-call | tf_op jit(solution)/shard_map/pallas_call | solution.py:224
  121.5 0.5 collective-permute-start.11
  122.0 0.0 collective-permute-done.13
  122.0 0.8 collective-permute-start.14
  122.9 0.0 collective-permute-done.15
  122.9 2.0 %collective-permute-start.16 = (bf16[256,384]{1,0:T(8,128)(2,1)S(1)}, bf16[256,384]{1,0:T(8,128)(2,1)S(1)}, u32[]{:S(2)}, u32[]{:S(2)}) collective-permute-start(bf16[256,384]{1,0:T(8,128)(2,1)S(1)} %add_convert_fusion), channel_id=1, source_target_pairs={{0,24},{8,0},{16,8},{24,16},{1,25},{9,1},{17,9},{25,17},{2,26},{10... | collective-permute-start | bytes 589832 | tf_op jit(solution)/shard_map/ppermute | solution.py:235
  124.9 2.5 %collective-permute-done.12 = bf16[256,384]{1,0:T(8,128)(2,1)S(1)} collective-permute-done((bf16[256,384]{1,0:T(8,128)(2,1)S(1)}, bf16[256,384]{1,0:T(8,128)(2,1)S(1)}, u32[]{:S(2)}, u32[]{:S(2)}) %collective-permute-start.12) | collective-permute-done | bytes 196640 | tf_op jit(solution)/shard_map/ppermute | solution.py:235
  127.5 4.6 %collective-permute-done.14 = bf16[256,384]{1,0:T(8,128)(2,1)S(1)} collective-permute-done((bf16[256,384]{1,0:T(8,128)(2,1)S(1)}, bf16[256,384]{1,0:T(8,128)(2,1)S(1)}, u32[]{:S(2)}, u32[]{:S(2)}) %collective-permute-start.14) | collective-permute-done | bytes 196640 | tf_op jit(solution)/shard_map/ppermute | solution.py:235
  132.1 0.0 collective-permute-done.16
  132.1 0.0 collective-permute-done.11
  132.1 0.8 convert_add_fusion
  (5 shorter events, 0.2 us)
Async XLA Ops:
  2.0 32.6 %all-to-all-start = ((bf16[8,128,384]{2,1,0:T(8,128)(2,1)}), bf16[8,128,384]{2,1,0:T(8,128)(2,1)S(1)}, u32[]{:S(2)}, u32[]{:S(2)}) async-start(bf16[8,128,384]{2,1,0:T(8,128)(2,1)} %get-tuple-element.37), calls=%async_computation | async-start | bytes 1572864 | tf_op jit(solution)/shard_map/all_to_all | solution.py:257
  11.0 7.0 %collective-permute-start = (bf16[256,384]{1,0:T(8,128)(2,1)}, bf16[256,384]{1,0:T(8,128)(2,1)S(1)}, u32[]{:S(2)}, u32[]{:S(2)}) collective-permute-start(bf16[256,384]{1,0:T(8,128)(2,1)} %proto_hbm.1), channel_id=1, source_target_pairs={{0,8},{8,16},{16,24},{24,0},{1,9},{9,17},{17,25},{25,1},{2,10},{10... | collective-permute-start | bytes 589832 | tf_op jit(solution)/shard_map/ppermute | solution.py:235
  12.3 7.8 %collective-permute-start.2 = (bf16[256,384]{1,0:T(8,128)(2,1)}, bf16[256,384]{1,0:T(8,128)(2,1)S(1)}, u32[]{:S(2)}, u32[]{:S(2)}) collective-permute-start(bf16[256,384]{1,0:T(8,128)(2,1)} %proto_hbm.1), channel_id=1, source_target_pairs={{0,24},{8,0},{16,8},{24,16},{1,25},{9,1},{17,9},{25,17},{2,26},{10... | collective-permute-start | bytes 589832 | tf_op jit(solution)/shard_map/ppermute | solution.py:235
  13.8 9.7 %collective-permute-start.1 = (bf16[256,384]{1,0:T(8,128)(2,1)}, bf16[256,384]{1,0:T(8,128)(2,1)S(1)}, u32[]{:S(2)}, u32[]{:S(2)}) collective-permute-start(bf16[256,384]{1,0:T(8,128)(2,1)} %proto_hbm.1), channel_id=1, source_target_pairs={{0,16},{8,24},{16,0},{24,8},{1,17},{9,25},{17,1},{25,9},{2,18},{10... | collective-permute-start | bytes 589832 | tf_op jit(solution)/shard_map/ppermute | solution.py:235
  15.4 15.2 %collective-permute-start.3 = (bf16[256,384]{1,0:T(8,128)(2,1)S(1)}, bf16[256,384]{1,0:T(8,128)(2,1)S(1)}, u32[]{:S(2)}, u32[]{:S(2)}) collective-permute-start(bf16[256,384]{1,0:T(8,128)(2,1)S(1)} %get-tuple-element.38.refs_0_), channel_id=1, source_target_pairs={{0,1},{1,0},{2,3},{3,2},{4,5},{5,4},{6,7},{7,6},{8,9},{9,8},{10,11... | collective-permute-start | bytes 589832 | tf_op jit(solution)/shard_map/ppermute | solution.py:235
  18.0 12.6 %collective-permute-start.4 = (bf16[256,384]{1,0:T(8,128)(2,1)S(1)}, bf16[256,384]{1,0:T(8,128)(2,1)S(1)}, u32[]{:S(2)}, u32[]{:S(2)}) collective-permute-start(bf16[256,384]{1,0:T(8,128)(2,1)S(1)} %collective-permute-done.refs_1_), channel_id=1, source_target_pairs={{0,1},{1,0},{2,3},{3,2},{4,5},{5,4},{6,7},{7,6},{8,9},{9,8},{10,11... | collective-permute-start | bytes 589832 | tf_op jit(solution)/shard_map/ppermute | solution.py:235
  20.1 10.5 %collective-permute-start.6 = (bf16[256,384]{1,0:T(8,128)(2,1)S(1)}, bf16[256,384]{1,0:T(8,128)(2,1)S(1)}, u32[]{:S(2)}, u32[]{:S(2)}) collective-permute-start(bf16[256,384]{1,0:T(8,128)(2,1)S(1)} %collective-permute-done.2.refs_3_), channel_id=1, source_target_pairs={{0,1},{1,0},{2,3},{3,2},{4,5},{5,4},{6,7},{7,6},{8,9},{9,8},{10,11... | collective-permute-start | bytes 589832 | tf_op jit(solution)/shard_map/ppermute | solution.py:235
  23.5 7.1 %collective-permute-start.5 = (bf16[256,384]{1,0:T(8,128)(2,1)S(1)}, bf16[256,384]{1,0:T(8,128)(2,1)S(1)}, u32[]{:S(2)}, u32[]{:S(2)}) collective-permute-start(bf16[256,384]{1,0:T(8,128)(2,1)S(1)} %collective-permute-done.1.refs_2_), channel_id=1, source_target_pairs={{0,1},{1,0},{2,3},{3,2},{4,5},{5,4},{6,7},{7,6},{8,9},{9,8},{10,11... | collective-permute-start | bytes 589832 | tf_op jit(solution)/shard_map/ppermute | solution.py:235
  25.2 13.6 %collective-permute-start.7 = (bf16[128,384]{1,0:T(8,128)(2,1)S(1)}, bf16[128,384]{1,0:T(8,128)(2,1)S(1)}, u32[]{:S(2)}, u32[]{:S(2)}) collective-permute-start(bf16[128,384]{1,0:T(8,128)(2,1)S(1)} %get-tuple-element.49.refs_0_), channel_id=1, source_target_pairs={{0,128},{32,160},{64,192},{96,224},{128,0},{160,32},{192,64},{224,... | collective-permute-start | bytes 294920 | tf_op jit(solution)/shard_map/ppermute | solution.py:258
  38.8 28.0 %collective-permute-start.8 = (bf16[256,384]{1,0:T(8,128)(2,1)S(1)}, bf16[256,384]{1,0:T(8,128)(2,1)S(1)}, u32[]{:S(2)}, u32[]{:S(2)}) collective-permute-start(bf16[256,384]{1,0:T(8,128)(2,1)S(1)} %pad_maximum_fusion.1), channel_id=1, source_target_pairs={{0,64},{32,96},{64,0},{96,32},{128,192},{160,224},{192,128},{224,1... | collective-permute-start | bytes 589832 | tf_op jit(solution)/shard_map/ppermute | solution.py:284
  66.8 33.1 %collective-permute-start.9 = (bf16[512,384]{1,0:T(8,128)(2,1)S(1)}, bf16[512,384]{1,0:T(8,128)(2,1)S(1)}, u32[]{:S(2)}, u32[]{:S(2)}) collective-permute-start(bf16[512,384]{1,0:T(8,128)(2,1)S(1)} %pad_maximum_fusion), channel_id=1, source_target_pairs={{0,32},{32,0},{64,96},{96,64},{128,160},{160,128},{192,224},{224,1... | collective-permute-start | bytes 1179656 | tf_op jit(solution)/shard_map/ppermute | solution.py:284
  115.7 3.7 %collective-permute-start.10 = (f32[256,384]{1,0:T(8,128)S(1)}, f32[256,384]{1,0:T(8,128)S(1)}, u32[]{:S(2)}, u32[]{:S(2)}) collective-permute-start(f32[256,384]{1,0:T(8,128)S(1)} %shard_map.44), channel_id=1, source_target_pairs={{0,1},{1,0},{2,3},{3,2},{4,5},{5,4},{6,7},{7,6},{8,9},{9,8},{10,11... | collective-permute-start | bytes 1179656 | tf_op jit(solution)/shard_map/ppermute | solution.py:235
  118.8 3.2 %collective-permute-start.13 = (f32[256,384]{1,0:T(8,128)S(1)}, f32[256,384]{1,0:T(8,128)S(1)}, u32[]{:S(2)}, u32[]{:S(2)}) collective-permute-start(f32[256,384]{1,0:T(8,128)S(1)} %get-tuple-element.66), channel_id=1, source_target_pairs={{0,1},{1,0},{2,3},{3,2},{4,5},{5,4},{6,7},{7,6},{8,9},{9,8},{10,11... | collective-permute-start | bytes 1179656 | tf_op jit(solution)/shard_map/ppermute | solution.py:235
  118.9 4.0 %collective-permute-start.15 = (f32[256,384]{1,0:T(8,128)S(1)}, f32[256,384]{1,0:T(8,128)S(1)}, u32[]{:S(2)}, u32[]{:S(2)}) collective-permute-start(f32[256,384]{1,0:T(8,128)S(1)} %get-tuple-element.68), channel_id=1, source_target_pairs={{0,1},{1,0},{2,3},{3,2},{4,5},{5,4},{6,7},{7,6},{8,9},{9,8},{10,11... | collective-permute-start | bytes 1179656 | tf_op jit(solution)/shard_map/ppermute | solution.py:235
  119.4 8.1 %collective-permute-start.12 = (bf16[256,384]{1,0:T(8,128)(2,1)S(1)}, bf16[256,384]{1,0:T(8,128)(2,1)S(1)}, u32[]{:S(2)}, u32[]{:S(2)}) collective-permute-start(bf16[256,384]{1,0:T(8,128)(2,1)S(1)} %add_convert_fusion.2), channel_id=1, source_target_pairs={{0,16},{8,24},{16,0},{24,8},{1,17},{9,25},{17,1},{25,9},{2,18},{10... | collective-permute-start | bytes 589832 | tf_op jit(solution)/shard_map/ppermute | solution.py:235
  121.5 10.6 %collective-permute-start.11 = (f32[256,384]{1,0:T(8,128)S(1)}, f32[256,384]{1,0:T(8,128)S(1)}, u32[]{:S(2)}, u32[]{:S(2)}) collective-permute-start(f32[256,384]{1,0:T(8,128)S(1)} %get-tuple-element.64), channel_id=1, source_target_pairs={{0,1},{1,0},{2,3},{3,2},{4,5},{5,4},{6,7},{7,6},{8,9},{9,8},{10,11... | collective-permute-start | bytes 1179656 | tf_op jit(solution)/shard_map/ppermute | solution.py:235
  122.0 10.1 %collective-permute-start.14 = (bf16[256,384]{1,0:T(8,128)(2,1)S(1)}, bf16[256,384]{1,0:T(8,128)(2,1)S(1)}, u32[]{:S(2)}, u32[]{:S(2)}) collective-permute-start(bf16[256,384]{1,0:T(8,128)(2,1)S(1)} %add_convert_fusion.1), channel_id=1, source_target_pairs={{0,8},{8,16},{16,24},{24,0},{1,9},{9,17},{17,25},{25,1},{2,10},{10... | collective-permute-start | bytes 589832 | tf_op jit(solution)/shard_map/ppermute | solution.py:235
  122.9 9.2 %collective-permute-start.16 = (bf16[256,384]{1,0:T(8,128)(2,1)S(1)}, bf16[256,384]{1,0:T(8,128)(2,1)S(1)}, u32[]{:S(2)}, u32[]{:S(2)}) collective-permute-start(bf16[256,384]{1,0:T(8,128)(2,1)S(1)} %add_convert_fusion), channel_id=1, source_target_pairs={{0,24},{8,0},{16,8},{24,16},{1,25},{9,1},{17,9},{25,17},{2,26},{10... | collective-permute-start | bytes 589832 | tf_op jit(solution)/shard_map/ppermute | solution.py:235

commit v9 on v8

--- a/solution.py
+++ b/solution.py
@@ -333,8 +333,8 @@
     def merge(near, far):
         return (near + swap(far)).astype(BF16)
 
-    (far2,) = grad((1, 2))
-    near2, far1, far3 = grad((0, 2), (1, 1), (1, 3), after=far2)
+    far2, near2 = grad((1, 2), (0, 2))
+    far1, far3 = grad((1, 1), (1, 3), after=far2)
     parts = [merge(near2, far2)]
     near1, near3, near0, far0 = grad((0, 1), (0, 3), (0, 0), (1, 0), after=parts)
     parts += [merge(near1, far1), merge(near3, far3)]

time: 133 us -> 133 us (level)
  no operation moved by 1% of the time
where the time goes in v9:
time: 133 us
  blocking collectives  70 us (53%)
  starting transfers between devices  35.7 us (27%)
  Pallas kernels  13.1 us (10%)
  waiting for transfers between devices  12.9 us (10%)
    all_to_all x3, blocking collectives, shards(): rows = lax.all_to_all(rows, ('z', 'x'), 0, 0, tiled=True)  41.7 us
    all_to_all x3, blocking collectives, shards(): cols = lax.all_to_all(cols, ('y', 'core'), 0, 0, tiled=True)  28.4 us
    ppermute x14, starting transfers between devices, shift(): return lax.ppermute(x, axis, [(i, (i + step) % size) for i in range(size)])  20.5 us
    pallas_call x10, Pallas kernels, call(): pl.pallas_call(kernel, out_shape=out_shape, in_specs=specs or [VMEM] * le...  13.1 us
    all_to_all x1, starting transfers between devices, shards(): teach = lax.all_to_all(teach, 'z', 0, 0, tiled=True)  9.03 us
    ppermute x14, waiting for transfers between devices, shift(): return lax.ppermute(x, axis, [(i, (i + step) % size) for i in range(size)])  7.47 us
    ppermute x1, starting transfers between devices, shards(): got = lax.ppermute(stud, 'z', [(i, i ^ 4) for i in range(NZ)])  5.37 us
    all_to_all x1, waiting for transfers between devices, shards(): teach = lax.all_to_all(teach, 'z', 0, 0, tiled=True)  3.99 us
  transfers between devices with their start and end apart: 18, of which 5 were waited for; matrix products, arithmetic and copies ran while one was open for 0% of the time, Pallas kernels for 6%

profile of v9, /device:TPU:1, one launch (start us, length us, event | category | flops | bytes accessed | tf_op | source)
XLA Modules:
  0.0 132.9 jit_solution(3660419767888045279)
XLA Ops:
  0.0 2.0 %shard_map.37 = (bf16[8,128,384]{2,1,0:T(8,128)(2,1)}, bf16[128,384]{1,0:T(8,128)(2,1)S(1)}, bf16[256,384]{1,0:T(8,128)(2,1)S(1)}) custom-call(bf16[256,384]{1,0:T(8,128)(2,1)} %teach_hbm.1, bf16[256,384]{1,0:T(8,128)(2,1)} %stud_hbm.1, bf16[256,384]{1,0:T(8,128)(2,1)} %proto_hbm.1), custom_call_target="tpu_custom_call" | custom-call | tf_op jit(solution)/shard_map/pallas_call | solution.py:224
  2.0 9.0 %all-to-all-start = ((bf16[8,128,384]{2,1,0:T(8,128)(2,1)}), bf16[8,128,384]{2,1,0:T(8,128)(2,1)S(1)}, u32[]{:S(2)}, u32[]{:S(2)}) async-start(bf16[8,128,384]{2,1,0:T(8,128)(2,1)} %get-tuple-element.38), calls=%async_computation | async-start | bytes 1572864 | tf_op jit(solution)/shard_map/all_to_all | solution.py:257
  11.0 1.3 collective-permute-start
  12.3 1.5 %collective-permute-start.2 = (bf16[256,384]{1,0:T(8,128)(2,1)}, bf16[256,384]{1,0:T(8,128)(2,1)S(1)}, u32[]{:S(2)}, u32[]{:S(2)}) collective-permute-start(bf16[256,384]{1,0:T(8,128)(2,1)} %proto_hbm.1), channel_id=1, source_target_pairs={{0,24},{8,0},{16,8},{24,16},{1,25},{9,1},{17,9},{25,17},{2,26},{10... | collective-permute-start | bytes 589832 | tf_op jit(solution)/shard_map/ppermute | solution.py:235
  13.8 1.6 %collective-permute-start.1 = (bf16[256,384]{1,0:T(8,128)(2,1)}, bf16[256,384]{1,0:T(8,128)(2,1)S(1)}, u32[]{:S(2)}, u32[]{:S(2)}) collective-permute-start(bf16[256,384]{1,0:T(8,128)(2,1)} %proto_hbm.1), channel_id=1, source_target_pairs={{0,16},{8,24},{16,0},{24,8},{1,17},{9,25},{17,1},{25,9},{2,18},{10... | collective-permute-start | bytes 589832 | tf_op jit(solution)/shard_map/ppermute | solution.py:235
  15.4 1.8 %collective-permute-start.3 = (bf16[256,384]{1,0:T(8,128)(2,1)S(1)}, bf16[256,384]{1,0:T(8,128)(2,1)S(1)}, u32[]{:S(2)}, u32[]{:S(2)}) collective-permute-start(bf16[256,384]{1,0:T(8,128)(2,1)S(1)} %get-tuple-element.39.refs_0_), channel_id=1, source_target_pairs={{0,1},{1,0},{2,3},{3,2},{4,5},{5,4},{6,7},{7,6},{8,9},{9,8},{10,11... | collective-permute-start | bytes 589832 | tf_op jit(solution)/shard_map/ppermute | solution.py:235
  17.2 0.8 collective-permute-done.refs_1_
  18.0 2.1 %collective-permute-start.4 = (bf16[256,384]{1,0:T(8,128)(2,1)S(1)}, bf16[256,384]{1,0:T(8,128)(2,1)S(1)}, u32[]{:S(2)}, u32[]{:S(2)}) collective-permute-start(bf16[256,384]{1,0:T(8,128)(2,1)S(1)} %collective-permute-done.refs_1_), channel_id=1, source_target_pairs={{0,1},{1,0},{2,3},{3,2},{4,5},{5,4},{6,7},{7,6},{8,9},{9,8},{10,11... | collective-permute-start | bytes 589832 | tf_op jit(solution)/shard_map/ppermute | solution.py:235
  20.1 0.0 collective-permute-done.2.refs_3_
  20.1 3.4 %collective-permute-start.6 = (bf16[256,384]{1,0:T(8,128)(2,1)S(1)}, bf16[256,384]{1,0:T(8,128)(2,1)S(1)}, u32[]{:S(2)}, u32[]{:S(2)}) collective-permute-start(bf16[256,384]{1,0:T(8,128)(2,1)S(1)} %collective-permute-done.2.refs_3_), channel_id=1, source_target_pairs={{0,1},{1,0},{2,3},{3,2},{4,5},{5,4},{6,7},{7,6},{8,9},{9,8},{10,11... | collective-permute-start | bytes 589832 | tf_op jit(solution)/shard_map/ppermute | solution.py:235
  23.5 0.0 collective-permute-done.1.refs_2_
  23.5 1.7 %collective-permute-start.5 = (bf16[256,384]{1,0:T(8,128)(2,1)S(1)}, bf16[256,384]{1,0:T(8,128)(2,1)S(1)}, u32[]{:S(2)}, u32[]{:S(2)}) collective-permute-start(bf16[256,384]{1,0:T(8,128)(2,1)S(1)} %collective-permute-done.1.refs_2_), channel_id=1, source_target_pairs={{0,1},{1,0},{2,3},{3,2},{4,5},{5,4},{6,7},{7,6},{8,9},{9,8},{10,11... | collective-permute-start | bytes 589832 | tf_op jit(solution)/shard_map/ppermute | solution.py:235
  25.2 5.4 %collective-permute-start.7 = (bf16[128,384]{1,0:T(8,128)(2,1)S(1)}, bf16[128,384]{1,0:T(8,128)(2,1)S(1)}, u32[]{:S(2)}, u32[]{:S(2)}) collective-permute-start(bf16[128,384]{1,0:T(8,128)(2,1)S(1)} %get-tuple-element.50.refs_0_), channel_id=1, source_target_pairs={{0,128},{32,160},{64,192},{96,224},{128,0},{160,32},{192,64},{224,... | collective-permute-start | bytes 294920 | tf_op jit(solution)/shard_map/ppermute | solution.py:258
  30.6 0.0 collective-permute-done.3.refs_4_
  30.6 0.0 collective-permute-done.4.refs_5_
  30.6 0.0 collective-permute-done.6.refs_7_
  30.6 0.0 collective-permute-done.5.refs_6_
  30.6 4.0 %all-to-all-done.teach_ref = bf16[8,128,384]{2,1,0:T(8,128)(2,1)S(1)} async-done(((bf16[8,128,384]{2,1,0:T(8,128)(2,1)}), bf16[8,128,384]{2,1,0:T(8,128)(2,1)S(1)}, u32[]{:S(2)}, u32[]{:S(2)}) %all-to-all-start) | async-done | bytes 786464 | tf_op jit(solution)/shard_map/all_to_all | solution.py:257
  34.6 2.8 %shard_map.38 = (f32[1024,1024]{1,0:T(8,128)S(1)}, bf16[1024,384]{1,0:T(8,128)(2,1)S(1)}, f32[1024,1024]{1,0:T(8,128)S(1)}, bf16[1024,384]{1,0:T(8,128)(2,1)S(1)}, bf16[8,16,128]{2,1,0:T(8,128)(2,1)S(1)}) custom-call(bf16[8,128,384]{2,1,0:T(8,128)(2,1)S(1)} %all-to-all-done.teach_ref, bf16[256,384]{1,0:T(8,128)(2,1)S(1)} %get-tuple-element.39.refs_0_, ...), custom_call_target="tpu_custom_call" | custom-call | tf_op jit(solution)/shard_map/pallas_call | solution.py:224
  37.3 1.5 %collective-permute-done.7.refs_1_ = bf16[128,384]{1,0:T(8,128)(2,1)S(1)} collective-permute-done((bf16[128,384]{1,0:T(8,128)(2,1)S(1)}, bf16[128,384]{1,0:T(8,128)(2,1)S(1)}, u32[]{:S(2)}, u32[]{:S(2)}) %collective-permute-start.7) | collective-permute-done | bytes 98336 | tf_op jit(solution)/shard_map/ppermute | solution.py:258
  38.8 0.1 collective-permute-start.8
  38.9 9.5 %all_to_all.35.col_sums_ref = bf16[8,16,128]{2,1,0:T(8,128)(2,1)S(1)} all-to-all(bf16[8,16,128]{2,1,0:T(8,128)(2,1)S(1)} %get-tuple-element.45), channel_id=1, replica_groups=mesh['z'=8,'y'=4,'x'=4,'core'=2] {'y','core'}, dimensions={0} | all-to-all | bytes 65536 | tf_op jit(solution)/shard_map/all_to_all | solution.py:285
  48.4 0.6 shard_map.39
  49.0 17.1 %all_to_all.36.row_sums_ref = bf16[32,8,128]{2,1,0:T(8,128)(2,1)S(1)} all-to-all(bf16[32,8,128]{2,1,0:T(8,128)(2,1)S(1)} %shard_map.39), channel_id=1, replica_groups=mesh['z'=8,'y'=4,'x'=4,'core'=2] {'z','x'}, dimensions={0} | all-to-all | bytes 131072 | tf_op jit(solution)/shard_map/all_to_all | solution.py:291
  66.1 0.7 shard_map.40
  66.8 0.0 collective-permute-done.8.refs_2_
  66.8 0.7 collective-permute-start.9
  67.5 9.5 %all_to_all.37.col_sums_ref = bf16[8,16,128]{2,1,0:T(8,128)(2,1)S(1)} all-to-all(bf16[8,16,128]{2,1,0:T(8,128)(2,1)S(1)} %shard_map.40), channel_id=1, replica_groups=mesh['z'=8,'y'=4,'x'=4,'core'=2] {'y','core'}, dimensions={0} | all-to-all | bytes 65536 | tf_op jit(solution)/shard_map/all_to_all | solution.py:285
  77.0 0.6 shard_map.41
  77.7 12.2 %all_to_all.38.row_sums_ref = bf16[32,8,128]{2,1,0:T(8,128)(2,1)S(1)} all-to-all(bf16[32,8,128]{2,1,0:T(8,128)(2,1)S(1)} %shard_map.41), channel_id=1, replica_groups=mesh['z'=8,'y'=4,'x'=4,'core'=2] {'z','x'}, dimensions={0} | all-to-all | bytes 131072 | tf_op jit(solution)/shard_map/all_to_all | solution.py:291
  89.9 0.7 shard_map.42
  90.5 9.4 %all_to_all.39.refs_4_.col_sums_ref = f32[8,16,128]{2,1,0:T(8,128)S(1)} all-to-all(f32[8,16,128]{2,1,0:T(8,128)S(1)} %shard_map.42), channel_id=1, replica_groups=mesh['z'=8,'y'=4,'x'=4,'core'=2] {'y','core'}, dimensions={0} | all-to-all | bytes 131072 | tf_op jit(solution)/shard_map/all_to_all | solution.py:285
  99.9 0.0 collective-permute-done.9.refs_3_
  99.9 2.8 %shard_map.43 = (f32[1024,1024]{1,0:T(8,128)S(1)}, f32[1024,1024]{1,0:T(8,128)S(1)}, bf16[1024,384]{1,0:T(8,128)(2,1)S(1)}, bf16[32,16,128]{2,1,0:T(8,128)(2,1)S(1)}) custom-call(bf16[128,384]{1,0:T(8,128)(2,1)S(1)} %get-tuple-element.50.refs_0_, bf16[128,384]{1,0:T(8,128)(2,1)S(1)} %collective-permute-done.7.refs_1_, ...), custom_call_target="tpu_custom_call" | custom-call | tf_op jit(solution)/shard_map/pallas_call | solution.py:224
  102.8 12.4 %all_to_all.40.row_sums_ref = bf16[32,16,128]{2,1,0:T(8,128)(2,1)S(1)} all-to-all(bf16[32,16,128]{2,1,0:T(8,128)(2,1)S(1)} %get-tuple-element.57), channel_id=1, replica_groups=mesh['z'=8,'y'=4,'x'=4,'core'=2] {'z','x'}, dimensions={0} | all-to-all | bytes 262144 | tf_op jit(solution)/shard_map/all_to_all | solution.py:316
  115.1 0.8 shard_map.44
  115.9 2.0 %collective-permute-start.10 = (f32[256,384]{1,0:T(8,128)S(1)}, f32[256,384]{1,0:T(8,128)S(1)}, u32[]{:S(2)}, u32[]{:S(2)}) collective-permute-start(f32[256,384]{1,0:T(8,128)S(1)} %get-tuple-element.62), channel_id=1, source_target_pairs={{0,1},{1,0},{2,3},{3,2},{4,5},{5,4},{6,7},{7,6},{8,9},{9,8},{10,11... | collective-permute-start | bytes 1179656 | tf_op jit(solution)/shard_map/ppermute | solution.py:235
  118.0 0.8 shard_map.46
  118.8 0.1 collective-permute-start.13
  118.9 0.5 collective-permute-start.15
  119.4 0.0 collective-permute-done.10
  119.4 0.8 collective-permute-start.12
  120.2 1.3 %shard_map.45 = (f32[256,384]{1,0:T(8,128)S(1)}, f32[256,384]{1,0:T(8,128)S(1)}, f32[256,384]{1,0:T(8,128)S(1)}, f32[256,384]{1,0:T(8,128)S(1)}) custom-call(f32[8,16,128]{2,1,0:T(8,128)S(1)} %all_to_all.39.refs_4_.col_sums_ref, bf16[32,16,128]{2,1,0:T(8,128)(2,1)S(1)} %all_to_all.40.row_sums_ref, bf16[1024,384]{1,0:T(8,128)(2,1)S(1)} %get-tuple-element.58.stud_ref, ...), custom_call_target="tpu_custom_call" | custom-call | tf_op jit(solution)/shard_map/pallas_call | solution.py:224
  121.6 0.0 collective-permute-done.13
  121.6 0.8 collective-permute-start.14
  122.5 0.9 collective-permute-start.11
  123.3 0.0 collective-permute-done.15
  123.4 2.0 %collective-permute-start.16 = (bf16[256,384]{1,0:T(8,128)(2,1)S(1)}, bf16[256,384]{1,0:T(8,128)(2,1)S(1)}, u32[]{:S(2)}, u32[]{:S(2)}) collective-permute-start(bf16[256,384]{1,0:T(8,128)(2,1)S(1)} %add_convert_fusion), channel_id=1, source_target_pairs={{0,24},{8,0},{16,8},{24,16},{1,25},{9,1},{17,9},{25,17},{2,26},{10... | collective-permute-start | bytes 589832 | tf_op jit(solution)/shard_map/ppermute | solution.py:235
  125.4 1.8 %collective-permute-done.12 = bf16[256,384]{1,0:T(8,128)(2,1)S(1)} collective-permute-done((bf16[256,384]{1,0:T(8,128)(2,1)S(1)}, bf16[256,384]{1,0:T(8,128)(2,1)S(1)}, u32[]{:S(2)}, u32[]{:S(2)}) %collective-permute-start.12) | collective-permute-done | bytes 196640 | tf_op jit(solution)/shard_map/ppermute | solution.py:235
  127.2 4.9 %collective-permute-done.14 = bf16[256,384]{1,0:T(8,128)(2,1)S(1)} collective-permute-done((bf16[256,384]{1,0:T(8,128)(2,1)S(1)}, bf16[256,384]{1,0:T(8,128)(2,1)S(1)}, u32[]{:S(2)}, u32[]{:S(2)}) %collective-permute-start.14) | collective-permute-done | bytes 196640 | tf_op jit(solution)/shard_map/ppermute | solution.py:235
  132.0 0.0 collective-permute-done.16
  132.0 0.0 collective-permute-done.11
  132.0 0.8 convert_add_fusion
  (5 shorter events, 0.2 us)
Async XLA Ops:
  2.0 32.6 %all-to-all-start = ((bf16[8,128,384]{2,1,0:T(8,128)(2,1)}), bf16[8,128,384]{2,1,0:T(8,128)(2,1)S(1)}, u32[]{:S(2)}, u32[]{:S(2)}) async-start(bf16[8,128,384]{2,1,0:T(8,128)(2,1)} %get-tuple-element.38), calls=%async_computation | async-start | bytes 1572864 | tf_op jit(solution)/shard_map/all_to_all | solution.py:257
  11.0 7.0 %collective-permute-start = (bf16[256,384]{1,0:T(8,128)(2,1)}, bf16[256,384]{1,0:T(8,128)(2,1)S(1)}, u32[]{:S(2)}, u32[]{:S(2)}) collective-permute-start(bf16[256,384]{1,0:T(8,128)(2,1)} %proto_hbm.1), channel_id=1, source_target_pairs={{0,8},{8,16},{16,24},{24,0},{1,9},{9,17},{17,25},{25,1},{2,10},{10... | collective-permute-start | bytes 589832 | tf_op jit(solution)/shard_map/ppermute | solution.py:235
  12.3 7.8 %collective-permute-start.2 = (bf16[256,384]{1,0:T(8,128)(2,1)}, bf16[256,384]{1,0:T(8,128)(2,1)S(1)}, u32[]{:S(2)}, u32[]{:S(2)}) collective-permute-start(bf16[256,384]{1,0:T(8,128)(2,1)} %proto_hbm.1), channel_id=1, source_target_pairs={{0,24},{8,0},{16,8},{24,16},{1,25},{9,1},{17,9},{25,17},{2,26},{10... | collective-permute-start | bytes 589832 | tf_op jit(solution)/shard_map/ppermute | solution.py:235
  13.8 9.7 %collective-permute-start.1 = (bf16[256,384]{1,0:T(8,128)(2,1)}, bf16[256,384]{1,0:T(8,128)(2,1)S(1)}, u32[]{:S(2)}, u32[]{:S(2)}) collective-permute-start(bf16[256,384]{1,0:T(8,128)(2,1)} %proto_hbm.1), channel_id=1, source_target_pairs={{0,16},{8,24},{16,0},{24,8},{1,17},{9,25},{17,1},{25,9},{2,18},{10... | collective-permute-start | bytes 589832 | tf_op jit(solution)/shard_map/ppermute | solution.py:235
  15.4 15.2 %collective-permute-start.3 = (bf16[256,384]{1,0:T(8,128)(2,1)S(1)}, bf16[256,384]{1,0:T(8,128)(2,1)S(1)}, u32[]{:S(2)}, u32[]{:S(2)}) collective-permute-start(bf16[256,384]{1,0:T(8,128)(2,1)S(1)} %get-tuple-element.39.refs_0_), channel_id=1, source_target_pairs={{0,1},{1,0},{2,3},{3,2},{4,5},{5,4},{6,7},{7,6},{8,9},{9,8},{10,11... | collective-permute-start | bytes 589832 | tf_op jit(solution)/shard_map/ppermute | solution.py:235
  18.0 12.6 %collective-permute-start.4 = (bf16[256,384]{1,0:T(8,128)(2,1)S(1)}, bf16[256,384]{1,0:T(8,128)(2,1)S(1)}, u32[]{:S(2)}, u32[]{:S(2)}) collective-permute-start(bf16[256,384]{1,0:T(8,128)(2,1)S(1)} %collective-permute-done.refs_1_), channel_id=1, source_target_pairs={{0,1},{1,0},{2,3},{3,2},{4,5},{5,4},{6,7},{7,6},{8,9},{9,8},{10,11... | collective-permute-start | bytes 589832 | tf_op jit(solution)/shard_map/ppermute | solution.py:235
  20.1 10.5 %collective-permute-start.6 = (bf16[256,384]{1,0:T(8,128)(2,1)S(1)}, bf16[256,384]{1,0:T(8,128)(2,1)S(1)}, u32[]{:S(2)}, u32[]{:S(2)}) collective-permute-start(bf16[256,384]{1,0:T(8,128)(2,1)S(1)} %collective-permute-done.2.refs_3_), channel_id=1, source_target_pairs={{0,1},{1,0},{2,3},{3,2},{4,5},{5,4},{6,7},{7,6},{8,9},{9,8},{10,11... | collective-permute-start | bytes 589832 | tf_op jit(solution)/shard_map/ppermute | solution.py:235
  23.5 7.1 %collective-permute-start.5 = (bf16[256,384]{1,0:T(8,128)(2,1)S(1)}, bf16[256,384]{1,0:T(8,128)(2,1)S(1)}, u32[]{:S(2)}, u32[]{:S(2)}) collective-permute-start(bf16[256,384]{1,0:T(8,128)(2,1)S(1)} %collective-permute-done.1.refs_2_), channel_id=1, source_target_pairs={{0,1},{1,0},{2,3},{3,2},{4,5},{5,4},{6,7},{7,6},{8,9},{9,8},{10,11... | collective-permute-start | bytes 589832 | tf_op jit(solution)/shard_map/ppermute | solution.py:235
  25.2 13.6 %collective-permute-start.7 = (bf16[128,384]{1,0:T(8,128)(2,1)S(1)}, bf16[128,384]{1,0:T(8,128)(2,1)S(1)}, u32[]{:S(2)}, u32[]{:S(2)}) collective-permute-start(bf16[128,384]{1,0:T(8,128)(2,1)S(1)} %get-tuple-element.50.refs_0_), channel_id=1, source_target_pairs={{0,128},{32,160},{64,192},{96,224},{128,0},{160,32},{192,64},{224,... | collective-permute-start | bytes 294920 | tf_op jit(solution)/shard_map/ppermute | solution.py:258
  38.8 28.0 %collective-permute-start.8 = (bf16[256,384]{1,0:T(8,128)(2,1)S(1)}, bf16[256,384]{1,0:T(8,128)(2,1)S(1)}, u32[]{:S(2)}, u32[]{:S(2)}) collective-permute-start(bf16[256,384]{1,0:T(8,128)(2,1)S(1)} %pad_maximum_fusion.1), channel_id=1, source_target_pairs={{0,64},{32,96},{64,0},{96,32},{128,192},{160,224},{192,128},{224,1... | collective-permute-start | bytes 589832 | tf_op jit(solution)/shard_map/ppermute | solution.py:284
  66.8 33.1 %collective-permute-start.9 = (bf16[512,384]{1,0:T(8,128)(2,1)S(1)}, bf16[512,384]{1,0:T(8,128)(2,1)S(1)}, u32[]{:S(2)}, u32[]{:S(2)}) collective-permute-start(bf16[512,384]{1,0:T(8,128)(2,1)S(1)} %pad_maximum_fusion), channel_id=1, source_target_pairs={{0,32},{32,0},{64,96},{96,64},{128,160},{160,128},{192,224},{224,1... | collective-permute-start | bytes 1179656 | tf_op jit(solution)/shard_map/ppermute | solution.py:284
  115.9 3.4 %collective-permute-start.10 = (f32[256,384]{1,0:T(8,128)S(1)}, f32[256,384]{1,0:T(8,128)S(1)}, u32[]{:S(2)}, u32[]{:S(2)}) collective-permute-start(f32[256,384]{1,0:T(8,128)S(1)} %get-tuple-element.62), channel_id=1, source_target_pairs={{0,1},{1,0},{2,3},{3,2},{4,5},{5,4},{6,7},{7,6},{8,9},{9,8},{10,11... | collective-permute-start | bytes 1179656 | tf_op jit(solution)/shard_map/ppermute | solution.py:235
  118.8 2.8 %collective-permute-start.13 = (f32[256,384]{1,0:T(8,128)S(1)}, f32[256,384]{1,0:T(8,128)S(1)}, u32[]{:S(2)}, u32[]{:S(2)}) collective-permute-start(f32[256,384]{1,0:T(8,128)S(1)} %get-tuple-element.68), channel_id=1, source_target_pairs={{0,1},{1,0},{2,3},{3,2},{4,5},{5,4},{6,7},{7,6},{8,9},{9,8},{10,11... | collective-permute-start | bytes 1179656 | tf_op jit(solution)/shard_map/ppermute | solution.py:235
  118.9 4.5 %collective-permute-start.15 = (f32[256,384]{1,0:T(8,128)S(1)}, f32[256,384]{1,0:T(8,128)S(1)}, u32[]{:S(2)}, u32[]{:S(2)}) collective-permute-start(f32[256,384]{1,0:T(8,128)S(1)} %get-tuple-element.70), channel_id=1, source_target_pairs={{0,1},{1,0},{2,3},{3,2},{4,5},{5,4},{6,7},{7,6},{8,9},{9,8},{10,11... | collective-permute-start | bytes 1179656 | tf_op jit(solution)/shard_map/ppermute | solution.py:235
  119.4 7.8 %collective-permute-start.12 = (bf16[256,384]{1,0:T(8,128)(2,1)S(1)}, bf16[256,384]{1,0:T(8,128)(2,1)S(1)}, u32[]{:S(2)}, u32[]{:S(2)}) collective-permute-start(bf16[256,384]{1,0:T(8,128)(2,1)S(1)} %add_convert_fusion.2), channel_id=1, source_target_pairs={{0,16},{8,24},{16,0},{24,8},{1,17},{9,25},{17,1},{25,9},{2,18},{10... | collective-permute-start | bytes 589832 | tf_op jit(solution)/shard_map/ppermute | solution.py:235
  121.6 10.4 %collective-permute-start.14 = (bf16[256,384]{1,0:T(8,128)(2,1)S(1)}, bf16[256,384]{1,0:T(8,128)(2,1)S(1)}, u32[]{:S(2)}, u32[]{:S(2)}) collective-permute-start(bf16[256,384]{1,0:T(8,128)(2,1)S(1)} %add_convert_fusion.1), channel_id=1, source_target_pairs={{0,8},{8,16},{16,24},{24,0},{1,9},{9,17},{17,25},{25,1},{2,10},{10... | collective-permute-start | bytes 589832 | tf_op jit(solution)/shard_map/ppermute | solution.py:235
  122.5 9.6 %collective-permute-start.11 = (f32[256,384]{1,0:T(8,128)S(1)}, f32[256,384]{1,0:T(8,128)S(1)}, u32[]{:S(2)}, u32[]{:S(2)}) collective-permute-start(f32[256,384]{1,0:T(8,128)S(1)} %get-tuple-element.65), channel_id=1, source_target_pairs={{0,1},{1,0},{2,3},{3,2},{4,5},{5,4},{6,7},{7,6},{8,9},{9,8},{10,11... | collective-permute-start | bytes 1179656 | tf_op jit(solution)/shard_map/ppermute | solution.py:235
  123.4 8.7 %collective-permute-start.16 = (bf16[256,384]{1,0:T(8,128)(2,1)S(1)}, bf16[256,384]{1,0:T(8,128)(2,1)S(1)}, u32[]{:S(2)}, u32[]{:S(2)}) collective-permute-start(bf16[256,384]{1,0:T(8,128)(2,1)S(1)} %add_convert_fusion), channel_id=1, source_target_pairs={{0,24},{8,0},{16,8},{24,16},{1,25},{9,1},{17,9},{25,17},{2,26},{10... | collective-permute-start | bytes 589832 | tf_op jit(solution)/shard_map/ppermute | solution.py:235
